TPU v7x, 128 devices: a whole 4x4x4 slice. The times are simulated.
128 devices in a mesh: seq: 32 (over x, y, core), head: 4 (over z).
Axes of the slice: x: 4, y: 4, z: 4, core: 2. Of those that a mesh axis runs over, the one named last changes fastest.
Arguments:
- tokens: bfloat16 [16384, 1152], P('seq'), may hold values from -6 to 6
- cotangent: bfloat16 [16384, 1152], P('seq'), may hold values from -6 to 6
- doc_starts: int32 [7], replicated, may hold values from 0 to 16256, as said below
- query_weight: bfloat16 [1152, 1024], P(None, 'head'), may hold values from -0.1875 to 0.1875
- key_weight: bfloat16 [1152, 256], replicated, may hold values from -0.1875 to 0.1875
- value_weight: bfloat16 [1152, 256], replicated, may hold values from -0.1875 to 0.1875
- out_weight: bfloat16 [1024, 1152], P('head'), may hold values from -0.1875 to 0.1875
- gate_weight: bfloat16 [1152, 6912], P(None, 'head'), may hold values from -0.1875 to 0.1875
- up_weight: bfloat16 [1152, 6912], P(None, 'head'), may hold values from -0.1875 to 0.1875
- down_weight: bfloat16 [6912, 1152], P('head'), may hold values from -0.078125 to 0.078125
- input_gain: float32 [1152], replicated, may hold values from 0.5 to 1.5
- attn_gain: float32 [1152], replicated, may hold values from 0.5 to 1.5
- prenorm_gain: float32 [1152], replicated, may hold values from 0.5 to 1.5
- post_gain: float32 [1152], replicated, may hold values from 0.5 to 1.5
- query_gain: float32 [256], replicated, may hold values from 0.5 to 1.5
- key_gain: float32 [256], replicated, may hold values from 0.5 to 1.5
Outputs:
- mixed: bfloat16 [16384, 1152], P('seq')
- tokens_grad: float32 [16384, 1152], P('seq')
- query_weight_grad: float32 [1152, 1024], P(None, 'head')
- key_weight_grad: float32 [1152, 256], replicated
- value_weight_grad: float32 [1152, 256], replicated
- out_weight_grad: float32 [1024, 1152], P('head')
- gate_weight_grad: float32 [1152, 6912], P(None, 'head')
- up_weight_grad: float32 [1152, 6912], P(None, 'head')
- down_weight_grad: float32 [6912, 1152], P('head')
- input_gain_grad: float32 [1152], replicated
- attn_gain_grad: float32 [1152], replicated
- prenorm_gain_grad: float32 [1152], replicated
- post_gain_grad: float32 [1152], replicated
- query_gain_grad: float32 [256], replicated
- key_gain_grad: float32 [256], replicated
Inputs may be any that keep to these rules, and one draw needn't show every extreme that they name: doc_starts[0] is 0 and the starts rise strictly. Each of the first 3 and the last 3 sequences has at most 128 tokens, and the last sequence has exactly 128, so sequence number 3 begins among the first 512 tokens and ends among the last 512.
All inputs are finite; a program needn't handle non-finite values.
Results may differ from a plain program's by a relative error of at most 0.025.
Values may be sent and summed in bfloat16 or wider, within the bound.
A program may use at most 256 MiB of HBM per device.

v0:
```python
import math

import jax
import jax.numpy as jnp
from jax import lax
from jax.sharding import PartitionSpec as P

HD = 256


EPS = 1e-06
THETA = 1000000.0
NEG = -1e30


def rms_norm(values, scaling):
    return values * lax.rsqrt(jnp.mean(values * values, axis=-1, keepdims=True) + EPS) * scaling


def doc_layout(doc_starts, token_index):
    before = doc_starts[None, :] <= token_index[:, None]
    segment = jnp.sum(before.astype(jnp.int32), axis=1)
    doc_begin = jnp.max(jnp.where(before, doc_starts[None, :], 0), axis=1)
    return (segment, token_index - doc_begin)


def rope_tables(position, head_width):
    half_width = head_width // 2
    inverse = jnp.exp(
        -math.log(THETA) * 2.0 * jnp.arange(half_width, dtype=jnp.float32) / head_width
    )
    angles = position.astype(jnp.float32)[:, None] * inverse[None, :]
    angles = jnp.concatenate([angles, angles], axis=1)
    return (jnp.cos(angles), jnp.sin(angles))


def rotate(values, cos_table, sine_table):
    half_width = values.shape[-1] // 2
    turned = jnp.concatenate([-values[..., half_width:], values[..., :half_width]], axis=-1)
    return values * cos_table + turned * sine_table


def dot_last(left_side, right_side):
    return lax.dot_general(
        left_side, right_side, (((1,), (1,)), ((), ())), preferred_element_type=jnp.float32
    )


def dot_first(left_side, right_side):
    return lax.dot_general(
        left_side, right_side, (((0,), (0,)), ((), ())), preferred_element_type=jnp.float32
    )


def residual_norm(residual, branch, scaling):
    return residual + rms_norm(branch, scaling)


def gated_act(gate_vals, up_vals):
    return jax.nn.gelu(gate_vals, approximate=True) * up_vals


def per_device(
    tokens,
    cotangent,
    doc_starts,
    query_weight,
    key_weight,
    value_weight,
    out_weight,
    gate_weight,
    up_weight,
    down_weight,
    input_gain,
    attn_gain,
    prenorm_gain,
    post_gain,
    query_gain,
    key_gain,
):
    row_count = tokens.shape[0]
    head_count = query_weight.shape[1] // HD
    key_count = row_count * lax.axis_size("seq")
    first_row = lax.axis_index("seq") * row_count
    own_index = first_row + jnp.arange(row_count, dtype=jnp.int32)
    all_index = jnp.arange(key_count, dtype=jnp.int32)
    own_segment, own_position = doc_layout(doc_starts, own_index)
    all_segment = doc_layout(doc_starts, all_index)[0]
    cos_table, sine_table = rope_tables(own_position, HD)
    query_scale = HD ** (-0.5)
    inputs = tokens.astype(jnp.float32)
    span_rows = math.gcd(key_count, 512)
    span_total = (first_row + row_count - 1) // span_rows + 1
    normed, input_back = jax.vjp(rms_norm, inputs, input_gain)
    normed_low = normed.astype(jnp.bfloat16)
    query_raw = jnp.dot(normed_low, query_weight, preferred_element_type=jnp.float32)
    key_raw = jnp.dot(normed_low, key_weight, preferred_element_type=jnp.float32)
    value_low = jnp.dot(normed_low, value_weight, preferred_element_type=jnp.float32).astype(
        jnp.bfloat16
    )

    def query_piece(source, scaling):
        heads_normed = rms_norm(source.reshape(row_count, head_count, HD), scaling)
        return rotate(heads_normed, cos_table[:, None, :], sine_table[:, None, :]) * query_scale

    def key_piece(source, scaling):
        return rotate(rms_norm(source, scaling), cos_table, sine_table)

    query_rows, query_back = jax.vjp(query_piece, query_raw, query_gain)
    query_low = query_rows.astype(jnp.bfloat16)
    key_rows, key_back = jax.vjp(key_piece, key_raw, key_gain)
    key_low = key_rows.astype(jnp.bfloat16)
    key_all, value_all = (
        lax.all_gather(key_low, "seq", axis=0, tiled=True),
        lax.all_gather(value_low, "seq", axis=0, tiled=True),
    )

    def span_scores(span_number):
        start = (span_number * span_rows).astype(jnp.int32)
        key_block = lax.dynamic_slice_in_dim(key_all, start, span_rows, 0)
        value_block = lax.dynamic_slice_in_dim(value_all, start, span_rows, 0)
        block_segment = lax.dynamic_slice_in_dim(all_segment, start, span_rows, 0)
        block_index = start + jnp.arange(span_rows, dtype=jnp.int32)
        block_mask = (block_index[None, :] <= own_index[:, None]) & (
            block_segment[None, :] == own_segment[:, None]
        )
        raw_scores = jnp.einsum(
            "qhd,kd->hqk", query_low, key_block, preferred_element_type=jnp.float32
        )
        return (start, raw_scores, block_mask[None], key_block, value_block)

    def total_step(span_number, carry):
        running_max, running_total = carry
        start, raw_scores, block_mask, key_block, value_block = span_scores(span_number)
        masked = jnp.where(block_mask, raw_scores, NEG)
        new_max = jnp.maximum(running_max, jnp.max(masked, axis=-1, keepdims=True))
        block_exp = jnp.where(block_mask, jnp.exp(masked - new_max), 0.0)
        new_total = running_total * jnp.exp(running_max - new_max) + jnp.sum(
            block_exp, axis=-1, keepdims=True
        )
        return (new_max, new_total)

    stat_shape = (head_count, row_count, 1)
    row_max, row_total = lax.fori_loop(
        0,
        span_total,
        total_step,
        (jnp.full(stat_shape, NEG, jnp.float32), jnp.zeros(stat_shape, jnp.float32)),
    )
    log_total = row_max + jnp.log(row_total)

    def soft_block(raw_scores, block_mask):
        return jnp.where(
            block_mask, jnp.exp(jnp.where(block_mask, raw_scores, NEG) - log_total), 0.0
        )

    def mix_step(span_number, mixed_sum):
        start, raw_scores, block_mask, key_block, value_block = span_scores(span_number)
        probs_low = soft_block(raw_scores, block_mask).astype(jnp.bfloat16)
        return mixed_sum + jnp.einsum(
            "hqk,kd->qhd", probs_low, value_block, preferred_element_type=jnp.float32
        )

    mixed_heads = lax.fori_loop(
        0, span_total, mix_step, jnp.zeros((row_count, head_count, HD), jnp.float32)
    )
    attn_mix = mixed_heads.reshape(row_count, head_count * HD).astype(jnp.bfloat16)
    attn_out = lax.psum(jnp.dot(attn_mix, out_weight, preferred_element_type=jnp.float32), "head")
    hidden_state, attn_back = jax.vjp(residual_norm, inputs, attn_out, attn_gain)
    ffn_in, prenorm_back = jax.vjp(rms_norm, hidden_state, prenorm_gain)
    ffn_low = ffn_in.astype(jnp.bfloat16)
    gate_rows = jnp.dot(ffn_low, gate_weight, preferred_element_type=jnp.float32)
    up_rows = jnp.dot(ffn_low, up_weight, preferred_element_type=jnp.float32)
    act_rows, act_back = jax.vjp(gated_act, gate_rows, up_rows)
    act_low = act_rows.astype(jnp.bfloat16)
    ffn_out = lax.psum(
        jnp.dot(act_low, down_weight, preferred_element_type=jnp.float32).astype(jnp.bfloat16),
        "head",
    ).astype(jnp.float32)
    mixed, post_back = jax.vjp(residual_norm, hidden_state, ffn_out, post_gain)
    upstream = cotangent.astype(jnp.float32)
    hidden_grad, ffn_out_grad, post_gain_grad = post_back(upstream)
    ffn_out_low = ffn_out_grad.astype(jnp.bfloat16)
    down_weight_grad = dot_first(act_low, ffn_out_low)
    act_grad = dot_last(ffn_out_low, down_weight)
    gate_grad, up_grad = act_back(act_grad)
    gate_low = gate_grad.astype(jnp.bfloat16)
    up_low = up_grad.astype(jnp.bfloat16)
    gate_weight_grad = dot_first(ffn_low, gate_low)
    up_weight_grad = dot_first(ffn_low, up_low)
    ffn_in_grad = lax.psum(
        (dot_last(gate_low, gate_weight) + dot_last(up_low, up_weight)).astype(jnp.bfloat16), "head"
    ).astype(jnp.float32)
    hidden_more, prenorm_gain_grad = prenorm_back(ffn_in_grad)
    hidden_grad = hidden_grad + hidden_more
    input_grad, attn_out_grad, attn_gain_grad = attn_back(hidden_grad)
    attn_out_low = attn_out_grad.astype(jnp.bfloat16)
    out_weight_grad = dot_first(attn_mix, attn_out_low)
    mix_grad = (
        dot_last(attn_out_low, out_weight).astype(jnp.bfloat16).reshape(row_count, head_count, HD)
    )

    def delta_step(span_number, delta_rows):
        start, raw_scores, block_mask, key_block, value_block = span_scores(span_number)
        soft_again = soft_block(raw_scores, block_mask)
        prob_grad = jnp.einsum(
            "qhd,kd->hqk", mix_grad, value_block, preferred_element_type=jnp.float32
        )
        return delta_rows + jnp.sum(soft_again * prob_grad, axis=-1, keepdims=True)

    delta_rows = lax.fori_loop(0, span_total, delta_step, jnp.zeros(stat_shape, jnp.float32))

    def grad_step(span_number, carry):
        query_grad, key_all_grad, value_all_grad = carry
        start, raw_scores, block_mask, key_block, value_block = span_scores(span_number)
        soft_again = soft_block(raw_scores, block_mask)
        probs_low = soft_again.astype(jnp.bfloat16)
        prob_grad = jnp.einsum(
            "qhd,kd->hqk", mix_grad, value_block, preferred_element_type=jnp.float32
        )
        value_part = jnp.einsum(
            "hqk,qhd->kd", probs_low, mix_grad, preferred_element_type=jnp.float32
        )
        score_low = (soft_again * (prob_grad - delta_rows)).astype(jnp.bfloat16)
        query_grad = query_grad + jnp.einsum(
            "hqk,kd->qhd", score_low, key_block, preferred_element_type=jnp.float32
        )
        key_part = jnp.einsum(
            "hqk,qhd->kd", score_low, query_low, preferred_element_type=jnp.float32
        )
        key_all_grad = lax.dynamic_update_slice_in_dim(
            key_all_grad,
            lax.dynamic_slice_in_dim(key_all_grad, start, span_rows, 0) + key_part,
            start,
            0,
        )
        value_all_grad = lax.dynamic_update_slice_in_dim(
            value_all_grad,
            lax.dynamic_slice_in_dim(value_all_grad, start, span_rows, 0) + value_part,
            start,
            0,
        )
        return (query_grad, key_all_grad, value_all_grad)

    query_grad, key_all_grad, value_all_grad = lax.fori_loop(
        0,
        span_total,
        grad_step,
        (
            jnp.zeros((row_count, head_count, HD), jnp.float32),
            jnp.zeros((key_count, HD), jnp.float32),
            jnp.zeros((key_count, HD), jnp.float32),
        ),
    )
    key_grad, value_grad = (
        lax.psum_scatter(
            key_all_grad.astype(jnp.bfloat16), "seq", scatter_dimension=0, tiled=True
        ).astype(jnp.float32),
        lax.psum_scatter(
            value_all_grad.astype(jnp.bfloat16), "seq", scatter_dimension=0, tiled=True
        ).astype(jnp.float32),
    )
    query_raw_grad, query_gain_part = query_back(query_grad)
    query_raw_low = query_raw_grad.astype(jnp.bfloat16)
    query_weight_grad = dot_first(normed_low, query_raw_low)
    normed_part = dot_last(query_raw_low, query_weight)
    key_grad, value_grad, normed_part, query_gain_grad = (
        lax.psum(key_grad.astype(jnp.bfloat16), "head").astype(jnp.float32),
        lax.psum(value_grad.astype(jnp.bfloat16), "head").astype(jnp.float32),
        lax.psum(normed_part.astype(jnp.bfloat16), "head").astype(jnp.float32),
        lax.psum(query_gain_part.astype(jnp.bfloat16), "head").astype(jnp.float32),
    )
    key_raw_grad, key_gain_grad = key_back(key_grad)
    key_raw_low = key_raw_grad.astype(jnp.bfloat16)
    value_grad_low = value_grad.astype(jnp.bfloat16)
    key_weight_grad = dot_first(normed_low, key_raw_low)
    value_weight_grad = dot_first(normed_low, value_grad_low)
    normed_grad = (
        normed_part + dot_last(key_raw_low, key_weight) + dot_last(value_grad_low, value_weight)
    )
    input_more, input_gain_grad = input_back(normed_grad)
    tokens_grad = input_grad + input_more
    (
        query_weight_grad,
        key_weight_grad,
        value_weight_grad,
        out_weight_grad,
        gate_weight_grad,
        up_weight_grad,
        down_weight_grad,
        input_gain_grad,
        attn_gain_grad,
        prenorm_gain_grad,
        post_gain_grad,
        query_gain_grad,
        key_gain_grad,
    ) = (
        lax.psum(query_weight_grad.astype(jnp.bfloat16), "seq").astype(jnp.float32),
        lax.psum(key_weight_grad.astype(jnp.bfloat16), "seq").astype(jnp.float32),
        lax.psum(value_weight_grad.astype(jnp.bfloat16), "seq").astype(jnp.float32),
        lax.psum(out_weight_grad.astype(jnp.bfloat16), "seq").astype(jnp.float32),
        lax.psum(gate_weight_grad.astype(jnp.bfloat16), "seq").astype(jnp.float32),
        lax.psum(up_weight_grad.astype(jnp.bfloat16), "seq").astype(jnp.float32),
        lax.psum(down_weight_grad.astype(jnp.bfloat16), "seq").astype(jnp.float32),
        lax.psum(input_gain_grad.astype(jnp.bfloat16), "seq").astype(jnp.float32),
        lax.psum(attn_gain_grad.astype(jnp.bfloat16), "seq").astype(jnp.float32),
        lax.psum(prenorm_gain_grad.astype(jnp.bfloat16), "seq").astype(jnp.float32),
        lax.psum(post_gain_grad.astype(jnp.bfloat16), "seq").astype(jnp.float32),
        lax.psum(query_gain_grad.astype(jnp.bfloat16), "seq").astype(jnp.float32),
        lax.psum(key_gain_grad.astype(jnp.bfloat16), "seq").astype(jnp.float32),
    )
    return (
        mixed.astype(jnp.bfloat16),
        tokens_grad,
        query_weight_grad,
        key_weight_grad,
        value_weight_grad,
        out_weight_grad,
        gate_weight_grad,
        up_weight_grad,
        down_weight_grad,
        input_gain_grad,
        attn_gain_grad,
        prenorm_gain_grad,
        post_gain_grad,
        query_gain_grad,
        key_gain_grad,
    )


def solution(mesh):
    placed = (
        P("seq", None),
        P("seq", None),
        P(),
        P(None, "head"),
        P(),
        P(),
        P("head", None),
        P(None, "head"),
        P(None, "head"),
        P("head", None),
        P(),
        P(),
        P(),
        P(),
        P(),
        P(),
    )
    return jax.shard_map(
        per_device,
        mesh=mesh,
        in_specs=placed,
        out_specs=(
            P("seq", None),
            P("seq", None),
            P(None, "head"),
            P(),
            P(),
            P("head", None),
            P(None, "head"),
            P(None, "head"),
            P("head", None),
            P(),
            P(),
            P(),
            P(),
            P(),
            P(),
        ),
        check_vma=False,
    )
```

profile of v0, /device:TPU:1, one launch (start us, length us, event | category | flops | bytes accessed | tf_op | source)
XLA Modules:
  0.0 1353.8 jit_solution(11438478312424838866)
XLA Ops:
  9.5 2.3 multiply_reduce_fusion.6
  15.8 4.6 fusion.127
  23.0 60.6 %all-gather.5.cloned.1.call-done = bf16[16384,256]{0,1:T(8,128)(2,1)} async-done(((bf16[512,256]{0,1:T(8,128)(2,1)}), bf16[16384,256]{0,1:T(8,128)(2,1)}) %all-gather.5.cloned.1.call-update) | async-done | bytes 8388624 | tf_op jit(solution)/shard_map/all_gather | solution.py:114
  83.6 11.9 copy.53
  95.5 3.8 while.50
  99.3 39.8 %all-gather.3.cloned.1.call-done = bf16[16384,256]{1,0:T(8,128)(2,1)} async-done(((bf16[512,256]{1,0:T(8,128)(2,1)}), bf16[16384,256]{1,0:T(8,128)(2,1)}) %all-gather.3.cloned.1.call-update) | async-done | bytes 8388624 | tf_op jit(solution)/shard_map/all_gather | solution.py:115
  139.2 4.0 while.51
  139.3 1.9 fusion.219
  143.2 2.0 fusion.125
  145.5 137.4 %all-reduce.13.cloned.1.call-done = f32[512,1152]{1,0:T(8,128)} async-done(((f32[512,1152]{1,0:T(8,128)}), f32[512,1152]{1,0:T(8,128)}) %all-reduce.13.cloned.1.call-update) | async-done | bytes 2359312 | tf_op jit(solution)/shard_map/psum | solution.py:168
  282.9 2.0 multiply_reduce_fusion.3
  285.5 2.0 multiply_reduce_fusion.2
  289.3 2.5 fusion.154
  291.9 5.1 multiply_convert_fusion.1
  298.2 3.6 convolution_convert_fusion.4
  302.1 45.1 %all-reduce.15.cloned.1.call-done = bf16[512,1152]{1,0:T(8,128)(2,1)} async-done(((bf16[512,1152]{1,0:T(8,128)(2,1)}), bf16[512,1152]{1,0:T(8,128)(2,1)}) %all-reduce.15.cloned.1.call-update) | async-done | bytes 1179664 | tf_op jit(solution)/shard_map/psum | solution.py:176
  349.0 3.2 fusion.90
  352.3 8.5 multiply_convert_fusion
  360.9 2.7 fusion.155
  364.3 3.7 fusion.77
  368.0 47.6 %all-reduce.17.cloned.1.call-done = bf16[512,1152]{1,0:T(8,128)(2,1)} async-done(((bf16[512,1152]{1,0:T(8,128)(2,1)}), bf16[512,1152]{1,0:T(8,128)(2,1)}) %all-reduce.17.cloned.1.call-update) | async-done | bytes 1179664 | tf_op jit(solution)/shard_map/psum | solution.py:191
  415.7 3.5 fusion.89
  419.3 4.7 multiply_reduce_fusion
  426.4 7.7 while.52
  434.1 6.0 broadcast.600
  440.1 7.8 broadcast.600.clone
  448.8 22.7 %while.53 = (s32[]{:T(128)}, f32[512,1,256]{0,2,1:T(8,128)}, f32[16384,256]{0,1:T(8,128)}, f32[16384,256]{1,0:T(8,128)}, s32[]{:T(128)}, /*index=5*/bf16[16384,2...) while((s32[]{:T(128)}, f32[512,1,256]{0,2,1:T(8,128)}, ...), condition=%wide.region_25.26_spmd.clone, body=%wide.region_24.25_spmd.clone.sunk | while | flops 674104320 | bytes 18108720 | solution.py:245
  455.9 2.2 fusion.239
  467.3 2.2 fusion.239
  471.5 8.9 convert_element_type.223
  480.5 8.9 convert_element_type.226
  492.4 2.2 fusion.120
  497.1 523.0 %reduce-scatter.3.cloned.1.call-done = bf16[512,256]{0,1:T(8,128)(2,1)} async-done(((bf16[16384,256]{0,1:T(8,128)(2,1)}), bf16[512,256]{0,1:T(8,128)(2,1)}) %reduce-scatter.3.cloned.1.call-update) | async-done | bytes 262160 | tf_op jit(solution)/shard_map/reduce_scatter | solution.py:256
  1020.1 96.2 %reduce-scatter.5.cloned.1.call-done = bf16[512,256]{1,0:T(8,128)(2,1)} async-done(((bf16[16384,256]{1,0:T(8,128)(2,1)}), bf16[512,256]{1,0:T(8,128)(2,1)}) %reduce-scatter.5.cloned.1.call-update) | async-done | bytes 262160 | tf_op jit(solution)/shard_map/reduce_scatter | solution.py:259
  1116.6 5.8 convolution_convert_fusion
  1122.4 4.4 convolution_convert_fusion.1
  1126.9 4.6 convolution_convert_fusion.2
  1134.4 39.1 %all-reduce.21.cloned.1.call-done = (bf16[512,256]{0,1:T(8,128)(2,1)}, bf16[512,1152]{1,0:T(8,128)(2,1)}, bf16[512,256]{1,0:T(8,128)(2,1)}) async-done(((bf16[512,256]{0,1:T(8,128)(2,1)}, bf16[512,1152]{1,0:T(8,128)(2,1)}, bf16[512,256]{1,0:T(8,128)(2,1)}), (bf16[512,256]{0,1:T(8,128)(2,1)}, bf16[512,1152]{1,0:T(8,128)(2,1)}, bf16[512,256]{1,0:T(8,128)(2,1)})) %all-reduce.21.cloned.1.call-update) | async-done | bytes 1703952 | tf_op jit(solution)/shard_map/psum | solution.py:268
  1173.5 2.8 convert_multiply_fusion.12
  1176.5 3.1 multiply_reduce_fusion.4
  1179.6 2.2 fusion.102
  1184.8 6.7 psum.157
  1192.1 4.1 fusion.85
  1196.3 125.0 %all-reduce.4 = (bf16[1152]{0:T(1024)(128)(2,1)S(1)}, bf16[1152]{0:T(1024)(128)(2,1)S(1)}, bf16[1152]{0:T(1024)(128)(2,1)S(1)}, bf16[1152]{0:T(1024)(128)(2,1)S(...) all-reduce(bf16[1152]{0:T(1024)(128)(2,1)S(1)} %get-tuple-element.4, ...), channel_id=1, replica_groups=mesh['seq'=32,'head'=4] {'seq'}, use_global_device_ids=true, to_apply=%region_42.43 | all-reduce | flops 5120 | bytes 20480 | tf_op jit(solution)/shard_map/psum | solution.py:305
  1324.8 4.0 fusion.93
  1328.8 6.0 convert_element_type.236
  1334.9 4.0 convert_element_type.238
  1338.8 3.8 convert_element_type.240
  (330 shorter events, 70.0 us)
Async XLA Ops:
  7.2 13.3 copy-start
  7.2 5.1 copy-start.77
  7.2 76.4 %all-gather.5.cloned.1.call-start = ((), (), s32[]{:S(2)}) async-start(), calls=%async_computation.3 | async-start | bytes 8650752 | tf_op jit(solution)/shard_map/all_gather | solution.py:114
  9.4 11.0 copy-start.66
  13.9 6.5 copy-start.16
  13.9 6.5 copy-start.53
  15.8 4.6 copy-start.22
  20.4 118.7 %all-gather.3.cloned.1.call-start = ((), (), s32[]{:S(2)}) async-start(), calls=%async_computation.2 | async-start | bytes 8650752 | tf_op jit(solution)/shard_map/all_gather | solution.py:115
  21.8 261.1 %all-reduce.13.cloned.1.call-start = ((), (), s32[]{:S(2)}) async-start(), calls=%async_computation.4 | async-start | bytes 4718592 | tf_op jit(solution)/shard_map/psum | solution.py:168
  145.2 140.3 %copy-start.50 = (f32[1152]{0:T(1024)S(1)}, f32[1152]{0:T(1024)}, u32[]{:S(2)}) copy-start(f32[1152]{0:T(1024)} %param.35) | copy-start | bytes 13828
  145.2 202.1 %all-reduce.15.cloned.1.call-start = ((), (), s32[]{:S(2)}) async-start(), calls=%async_computation.5 | async-start | bytes 2359296 | tf_op jit(solution)/shard_map/psum | solution.py:176
  291.9 5.1 copy-start.100
  291.9 6.3 copy-start.93
  301.8 113.9 %all-reduce.17.cloned.1.call-start = ((), (), s32[]{:S(2)}) async-start(), calls=%async_computation.6 | async-start | bytes 2359296 | tf_op jit(solution)/shard_map/psum | solution.py:191
  347.3 5.0 copy-start.13
  347.3 5.0 copy-start.24
  347.3 5.0 copy-start.61
  349.0 11.8 copy-start.70
  352.3 8.6 copy-start.91
  352.3 8.6 copy-start.95
  368.0 652.1 %reduce-scatter.3.cloned.1.call-start = ((), (), s32[]{:S(2)}) async-start(), calls=%async_computation.7 | async-start | bytes 8650752 | tf_op jit(solution)/shard_map/reduce_scatter | solution.py:256
  419.3 4.7 copy-start.76
  440.1 8.6 copy-start.90
  480.4 635.8 %reduce-scatter.5.cloned.1.call-start = ((), (), s32[]{:S(2)}) async-start(), calls=%async_computation.8 | async-start | bytes 8650752 | tf_op jit(solution)/shard_map/reduce_scatter | solution.py:259
  489.5 684.0 %all-reduce.21.cloned.1.call-start = ((), (), s32[]{:S(2)}) async-start(), calls=%async_computation.10 | async-start | bytes 3407872 | tf_op jit(solution)/shard_map/psum | solution.py:268
  494.6 621.9 %copy-start.21 = (bf16[512,1728]{0,1:T(8,128)(2,1)S(1)}, bf16[512,1728]{0,1:T(8,128)(2,1)}, u32[]{:S(2)}) copy-start(bf16[512,1728]{0,1:T(8,128)(2,1)} %copy-done.20) | copy-start | bytes 5308420
  1116.3 212.5 %all-reduce.19.cloned.1.call-start = ((), (), s32[]{:S(2)}) async-start(), calls=%async_computation.9 | async-start | bytes 28606464 | tf_op jit(solution)/shard_map/psum | solution.py:298
  1116.5 5.8 copy-start.35
  1116.5 5.8 copy-start.97
  1122.4 4.5 copy-start.15
  1122.4 4.5 copy-start.25
  1122.4 4.5 copy-start.63
  1126.9 4.7 copy-start.10
  1126.9 4.7 copy-start.38
  1126.9 4.7 copy-start.65
  1126.9 4.6 copy-start.67
  1131.6 42.0 %copy-start.23 = (f32[512,128]{0,1:T(8,128)S(1)}, f32[512,128]{0,1:T(8,128)}, u32[]{:S(2)}) copy-start(f32[512,128]{0,1:T(8,128)} %copy-done.22) | copy-start | bytes 786436
  1133.1 43.4 %copy-start.17 = (f32[512,256]{0,1:T(8,128)S(1)}, f32[512,256]{0,1:T(8,128)}, u32[]{:S(2)}) copy-start(f32[512,256]{0,1:T(8,128)} %copy-done.16) | copy-start | bytes 1572868
  1133.1 43.4 %copy-start.54 = (f32[512]{0:T(512)S(1)}, f32[512]{0:T(512)}, u32[]{:S(2)}) copy-start(f32[512]{0:T(512)} %copy-done.53) | copy-start | bytes 6148
  1133.1 43.4 %copy-start.80 = (f32[256]{0:T(256)S(1)}, f32[256]{0:T(256)}, u32[]{:S(2)}) copy-start(f32[256]{0:T(256)} %param.39) | copy-start | bytes 3076
  1134.4 45.1 %copy-start.85 = (f32[512]{0:T(512)S(1)}, f32[512]{0:T(512)}, u32[]{:S(2)}) copy-start(f32[512]{0:T(512)} %copy-done.84) | copy-start | bytes 6148
  1173.5 6.0 copy-start.33
  1184.8 6.8 copy-start.36
  1184.8 6.8 copy-start.40
  1192.1 132.6 %copy-start.74 = (f32[512]{0:T(512)S(1)}, f32[512]{0:T(512)}, u32[]{:S(2)}) copy-start(f32[512]{0:T(512)} %copy-done.73) | copy-start | bytes 6148
  1192.1 132.6 %copy-start.8 = (f32[512,1152]{1,0:T(8,128)S(1)}, f32[512,1152]{1,0:T(8,128)}, u32[]{:S(2)}) copy-start(f32[512,1152]{1,0:T(8,128)} %copy-done.7) | copy-start | bytes 7077892
  1328.8 6.0 copy-start.31
  1338.8 4.9 copy-start.43
  (64 other events, 171.4 us)
Sparse Core Ops, SparseCore 0:
  20.5 63.0 all-gather.4
  86.4 52.6 all-gather.2
  145.3 137.5 all-reduce.12
  301.9 45.3 all-reduce.14
  368.1 47.5 all-reduce.16
  480.6 539.5 reduce-scatter.2
  1024.3 91.9 reduce-scatter.4
  1119.4 54.0 all-reduce.20
  1184.9 141.7 all-reduce.18
where the time goes:
time: 1370 us; the launch traced here: 1350 us
  waiting for transfers between devices  989 us (72%)
  blocking collectives  132 us (10%)
  matrix products  86.6 us (6%)
  other arithmetic  83.9 us (6%)
  local copies, waits for them, and re-layouts  45.5 us (3%)
  between operations  15.2 us (1%)
    reduce_scatter x1, waiting for transfers between devices, per_device(): lax.psum_scatter(key_all_grad.astype(jnp.bfloat16), 'seq', scatter_dimens...  523 us
    psum x1, waiting for transfers between devices, per_device(): lax.psum(jnp.dot(attn_mix, out_weight, preferred_element_type=jnp.float32...  137 us
    psum x1, blocking collectives, per_device(): lax.psum(input_gain_grad.astype(jnp.bfloat16), 'seq').astype(jnp.float32)  125 us
    reduce_scatter x1, waiting for transfers between devices, per_device(): lax.psum_scatter(value_all_grad.astype(jnp.bfloat16), 'seq', scatter_dime...  96.2 us
    all_gather x1, waiting for transfers between devices, per_device(): lax.all_gather(key_low, 'seq', axis=0, tiled=True)  60.6 us
    psum x1, waiting for transfers between devices, per_device(): lax.psum((dot_last(gate_low, gate_weight) + dot_last(up_low, up_weight))....  47.6 us
    psum x1, waiting for transfers between devices, per_device(): lax.psum(jnp.dot(act_low, down_weight, preferred_element_type=jnp.float32...  45.1 us
    all_gather x1, waiting for transfers between devices, per_device(): lax.all_gather(value_low, 'seq', axis=0, tiled=True)  39.8 us
  transfers between devices with their start and end apart: 9, of which 8 were waited for; matrix products, arithmetic and copies ran while one was open for 5% of the time, Pallas kernels for 0%

commit v1 on v0

v1 whole, which is shorter than its diff:
```python
import functools
import math

import jax
import jax.numpy as jnp
from jax import lax
from jax.experimental import pallas as pl
from jax.experimental.pallas import tpu as pltpu
from jax.sharding import PartitionSpec as P

HD = 256


EPS = 1e-06
THETA = 1000000.0
NEG = -1e30


def rms_norm(values, scaling):
    return values * lax.rsqrt(jnp.mean(values * values, axis=-1, keepdims=True) + EPS) * scaling


def doc_layout(doc_starts, token_index):
    before = doc_starts[None, :] <= token_index[:, None]
    segment = jnp.sum(before.astype(jnp.int32), axis=1)
    doc_begin = jnp.max(jnp.where(before, doc_starts[None, :], 0), axis=1)
    return (segment, token_index - doc_begin)


def rope_tables(position, head_width):
    half_width = head_width // 2
    inverse = jnp.exp(
        -math.log(THETA) * 2.0 * jnp.arange(half_width, dtype=jnp.float32) / head_width
    )
    angles = position.astype(jnp.float32)[:, None] * inverse[None, :]
    angles = jnp.concatenate([angles, angles], axis=1)
    return (jnp.cos(angles), jnp.sin(angles))


def rotate(values, cos_table, sine_table):
    half_width = values.shape[-1] // 2
    turned = jnp.concatenate([-values[..., half_width:], values[..., :half_width]], axis=-1)
    return values * cos_table + turned * sine_table


def dot_last(left_side, right_side):
    return lax.dot_general(
        left_side, right_side, (((1,), (1,)), ((), ())), preferred_element_type=jnp.float32
    )


def dot_first(left_side, right_side):
    return lax.dot_general(
        left_side, right_side, (((0,), (0,)), ((), ())), preferred_element_type=jnp.float32
    )


def residual_norm(residual, branch, scaling):
    return residual + rms_norm(branch, scaling)


def gated_act(gate_vals, up_vals):
    return jax.nn.gelu(gate_vals, approximate=True) * up_vals


MESH_ID = pl.DeviceIdType.MESH
HALF = 256
BLK = 512
X_SIZE, Y_SIZE = 4, 4
STEPS = (0, 1, 3, 2)


def place():
    s = lax.axis_index("seq")
    return s // 8, (s // 2) % 4, s % 2, lax.axis_index("head")


def at(x, y, c, z):
    return ((x % 4) * 8 + (y % 4) * 2 + c, z % 4)


def greet(peers):
    barrier = pltpu.get_barrier_semaphore()
    for peer in peers:
        pl.semaphore_signal(barrier, inc=1, device_id=peer, device_id_type=MESH_ID)
    pl.semaphore_wait(barrier, len(peers))


def remote(src, dst, send_sem, recv_sem, peer):
    return pltpu.make_async_remote_copy(
        src_ref=src,
        dst_ref=dst,
        send_sem=send_sem,
        recv_sem=recv_sem,
        device_id=peer,
        device_id_type=MESH_ID,
    )


def plane_peers(x, y, c, z):
    along_x = [at(x + j, y, c, z) for j in (1, 3, 2)]
    along_y = [at(x, y + j, c, z) for j in (1, 3, 2)]
    mirror = [at(3 - x, y + j, 1 - c, z) for j in range(4)]
    sibling = at(x, y, 1 - c, z)
    along_z = [at(x, y, c, z + j) for j in (1, 3, 2)]
    return along_x, along_y, mirror, sibling, along_z


def half_token(x, y_slot, c, upper):
    d = 8 * x + 2 * y_slot + c
    return HALF * (63 - 2 * d) if upper else HALF * 2 * d


def tile_first(i, x, c):
    d = 8 * x + 2 * (i // 2) + c
    return jnp.where(i % 2 == 1, HALF * (63 - 2 * d), HALF * 2 * d)


def begin_of(token, starts_ref):
    begin = jnp.zeros_like(token)
    for n in range(starts_ref.shape[0]):
        start = starts_ref[n]
        begin = jnp.where(start <= token, start, begin)
    return begin


def attn_forward(
    starts_ref, q_ref, k_ref, v_ref,
    mix_ref, lse_ref, qg_ref, kg_ref, vg_ref,
    acc, lacc, osend, lsend, orecv, lrecv,
    q_ssem, q_rsem, kv_ssem, kv_rsem, fw_ssem, o_ssem, o_rsem, l_ssem, l_rsem, z_ssem, z_rsem,
):
    x, y, c, z = place()
    along_x, along_y, mirror, sibling, along_z = plane_peers(x, y, c, z)
    greet(along_x + along_y + mirror + [sibling] + along_z)

    own_low = y * 2
    own_high = (3 - y) * 2 + 1
    own_slot = x * 2 + c
    q_low, q_high = q_ref.at[pl.ds(0, HALF)], q_ref.at[pl.ds(HALF, HALF)]
    sends = []
    kv_peers = [sibling] + along_x
    for n, peer in enumerate(kv_peers):
        for m, (src, dst) in enumerate(((k_ref, kg_ref), (v_ref, vg_ref))):
            sends.append(remote(src, dst.at[own_slot], kv_ssem.at[n, m], kv_rsem.at[own_slot, m], peer))
    for n, peer in enumerate(along_y):
        sends.append(remote(q_low, qg_ref.at[own_low], q_ssem.at[n], q_rsem.at[own_low], peer))
    for n, peer in enumerate(mirror):
        sends.append(remote(q_high, qg_ref.at[own_high], q_ssem.at[3 + n], q_rsem.at[own_high], peer))
    for copy in sends:
        copy.start()
    qg_ref[own_low] = q_ref[0:HALF, :]
    kg_ref[own_slot] = k_ref[...]
    vg_ref[own_slot] = v_ref[...]
    acc[...] = jnp.zeros_like(acc)
    lacc[...] = jnp.zeros_like(lacc)

    def q_arrival(slot):
        remote(q_low, qg_ref.at[slot], q_ssem.at[0], q_rsem.at[slot], sibling).wait_recv()

    def kv_arrival(slot):
        for m, (src, dst) in enumerate(((k_ref, kg_ref), (v_ref, vg_ref))):
            remote(src, dst.at[slot], kv_ssem.at[0, m], kv_rsem.at[slot, m], sibling).wait_recv()

    for j in (1, 3, 2):
        q_arrival(((y + j) % 4) * 2)
    for j in range(4):
        q_arrival(j * 2 + 1)

    def chunk(i, first_q, pair, first_k, masked):
        queries = qg_ref[i]
        if masked:
            token = first_q + lax.broadcasted_iota(jnp.int32, (HALF, 1), 0)
            begin = begin_of(token, starts_ref)
        total = None
        sums = None
        for cc in range(2):
            keys, values = kg_ref[pair * 2 + cc], vg_ref[pair * 2 + cc]
            scores = lax.dot_general(
                queries, keys, (((1,), (1,)), ((), ())), preferred_element_type=jnp.float32
            )
            exps = jnp.exp(scores)
            if masked:
                key_index = first_k + cc * BLK + lax.broadcasted_iota(jnp.int32, (1, BLK), 1)
                exps = jnp.where((key_index <= token) & (key_index >= begin), exps, 0.0)
            part = jnp.dot(exps.astype(jnp.bfloat16), values, preferred_element_type=jnp.float32)
            total = part if total is None else total + part
            for n in range(BLK // 128):
                piece = exps[:, n * 128 : (n + 1) * 128]
                sums = piece if sums is None else sums + piece
        acc[i] = acc[i] + total
        lacc[i] = lacc[i] + sums

    forwards = []
    for step, j in enumerate(STEPS):
        pair = (x + j) % 4
        if step > 0:
            kv_arrival(pair * 2 + c)
            for m, ref in enumerate((kg_ref, vg_ref)):
                slot = pair * 2 + c
                copy = remote(ref.at[slot], ref.at[slot], fw_ssem.at[step - 1, m], kv_rsem.at[slot, m], sibling)
                copy.start()
                forwards.append(copy)
        kv_arrival(pair * 2 + 1 - c)
        first_k = 4096 * pair + 1024 * y

        def visit(i, carry):
            first_q = tile_first(i, x, c)
            some = first_k <= first_q + (HALF - 1)
            full = (first_k + 1023 <= first_q) & (first_k > 0) & (first_q < 31 * BLK)

            @pl.when(full)
            def _():
                chunk(i, first_q, pair, first_k, False)

            @pl.when(some & jnp.logical_not(full))
            def _():
                chunk(i, first_q, pair, first_k, True)

            return carry

        lax.fori_loop(0, 8, visit, 0)

    out_copies = []
    for slot_y in range(4):
        for upper in range(2):
            i = slot_y * 2 + upper
            osend[i] = acc[i].astype(jnp.bfloat16)
            row = jnp.sum(jnp.transpose(lacc[i]), axis=0, keepdims=True)
            lsend[i] = jnp.broadcast_to(row, (8, HALF))
    for j in (1, 3, 2):
        i = ((y + j) % 4) * 2
        peer = at(x, y + j, c, z)
        out_copies.append(remote(osend.at[i], orecv.at[y], o_ssem.at[j - 1], o_rsem.at[y], peer))
        out_copies.append(remote(lsend.at[i], lrecv.at[y], l_ssem.at[j - 1], l_rsem.at[y], peer))
    for j in range(4):
        i = j * 2 + 1
        peer = at(3 - x, 3 - j, 1 - c, z)
        out_copies.append(remote(osend.at[i], orecv.at[4 + y], o_ssem.at[3 + j], o_rsem.at[4 + y], peer))
        out_copies.append(remote(lsend.at[i], lrecv.at[4 + y], l_ssem.at[3 + j], l_rsem.at[4 + y], peer))
    for copy in out_copies:
        copy.start()
    orecv[y] = osend[own_low]
    lrecv[y] = lsend[own_low]

    def o_arrival(slot):
        remote(osend.at[0], orecv.at[slot], o_ssem.at[0], o_rsem.at[slot], sibling).wait_recv()
        remote(lsend.at[0], lrecv.at[slot], l_ssem.at[0], l_rsem.at[slot], sibling).wait_recv()

    for j in (1, 3, 2):
        o_arrival((y + j) % 4)
    for j in range(4):
        o_arrival(4 + j)
    mine = mix_ref.at[:, pl.ds(pl.multiple_of(z * HD, HD), HD)]
    for upper in range(2):
        numer = sum(orecv[4 * upper + n].astype(jnp.float32) for n in range(4))
        denom = sum(lrecv[4 * upper + n] for n in range(4))[0:1, :]
        lse_ref[:, upper * HALF : (upper + 1) * HALF] = jnp.broadcast_to(jnp.log(denom), (8, HALF))
        inverse = jnp.transpose(jnp.broadcast_to(1.0 / denom, (128, HALF)))
        scaled = numer * jnp.concatenate([inverse, inverse], axis=1)
        mix_ref[pl.ds(upper * HALF, HALF), pl.ds(pl.multiple_of(z * HD, HD), HD)] = scaled.astype(jnp.bfloat16)
    z_copies = []
    for j in (1, 3, 2):
        z_copies.append(remote(mine, mine, z_ssem.at[j - 1], z_rsem.at[z], at(x, y, c, z + j)))
    for copy in z_copies:
        copy.start()
    for j in (1, 3, 2):
        other = (z + j) % 4
        theirs = mix_ref.at[:, pl.ds(pl.multiple_of(other * HD, HD), HD)]
        remote(mine, theirs, z_ssem.at[0], z_rsem.at[other], sibling).wait_recv()
    for copy in sends + forwards + out_copies + z_copies:
        copy.wait_send()


def forward_attention(doc_starts, query, key, value):
    vmem = pl.BlockSpec(memory_space=pltpu.VMEM)
    dma = pltpu.SemaphoreType.DMA
    return pl.pallas_call(
        attn_forward,
        name="attn_forward",
        out_shape=[
            jax.ShapeDtypeStruct((BLK, 4 * HD), jnp.bfloat16),
            jax.ShapeDtypeStruct((8, BLK), jnp.float32),
            jax.ShapeDtypeStruct((8, HALF, HD), jnp.bfloat16),
            jax.ShapeDtypeStruct((8, BLK, HD), jnp.bfloat16),
            jax.ShapeDtypeStruct((8, BLK, HD), jnp.bfloat16),
        ],
        in_specs=[pl.BlockSpec(memory_space=pltpu.SMEM)] + [vmem] * 3,
        out_specs=[vmem] * 5,
        scratch_shapes=[
            pltpu.VMEM((8, HALF, HD), jnp.float32),
            pltpu.VMEM((8, HALF, 128), jnp.float32),
            pltpu.VMEM((8, HALF, HD), jnp.bfloat16),
            pltpu.VMEM((8, 8, HALF), jnp.float32),
            pltpu.VMEM((8, HALF, HD), jnp.bfloat16),
            pltpu.VMEM((8, 8, HALF), jnp.float32),
            dma((7,)), dma((8,)), dma((4, 2)), dma((8, 2)), dma((3, 2)),
            dma((7,)), dma((8,)), dma((7,)), dma((8,)), dma((3,)), dma((4,)),
        ],
        compiler_params=pltpu.CompilerParams(
            collective_id=1, has_side_effects=True, vmem_limit_bytes=40 << 20
        ),
        cost_estimate=pl.CostEstimate(flops=6 * 10**9, bytes_accessed=20 * 2**20, transcendentals=5 * 10**6),
    )(doc_starts, query, key, value)


def attn_backward(
    starts_ref, do_ref, stat_ref, q_in, k_in, v_in,
    dq_ref, dkv_ref,
    dog, statg, dqacc, dkacc, dvacc, ktbuf, sibsend, sibrecv, ringsend, ringrecv,
    dqsend, dqrecv, zpart, zsend, zrecv,
    do_ssem, do_rsem, st_ssem, st_rsem, sib_ssem, sib_rsem, ring_ssem, ring_rsem,
    dq_ssem, dq_rsem, z_ssem, z_rsem, g_ssem, g_rsem,
):
    x, y, c, z = place()
    along_x, along_y, mirror, sibling, along_z = plane_peers(x, y, c, z)
    greet(along_x + along_y + mirror + [sibling] + along_z)
    own_low = y * 2
    own_high = (3 - y) * 2 + 1
    sends = []
    for part, (own, peers, base) in enumerate(((own_low, along_y, 0), (own_high, mirror, 3))):
        do_half = do_ref.at[pl.ds(part * HALF, HALF)]
        st_half = stat_ref.at[part]
        for n, peer in enumerate(peers):
            sends.append(remote(do_half, dog.at[own], do_ssem.at[base + n], do_rsem.at[own], peer))
            sends.append(remote(st_half, statg.at[own], st_ssem.at[base + n], st_rsem.at[own], peer))
    for copy in sends:
        copy.start()
    dog[own_low] = do_ref[0:HALF, :]
    statg[own_low] = stat_ref[0]
    dqacc[...] = jnp.zeros_like(dqacc)

    def arrival(slot):
        remote(do_ref.at[pl.ds(0, HALF)], dog.at[slot], do_ssem.at[0], do_rsem.at[slot], sibling).wait_recv()
        remote(stat_ref.at[0], statg.at[slot], st_ssem.at[0], st_rsem.at[slot], sibling).wait_recv()

    for j in (1, 3, 2):
        arrival(((y + j) % 4) * 2)
    for j in range(4):
        arrival(j * 2 + 1)

    def tile(i, first_q, slot, first_k, masked):
        queries, out_grads = q_in[i], dog[i]
        lse, delta = statg[i, 0:1, :], statg[i, 1:2, :]
        if masked:
            token = first_q + lax.broadcasted_iota(jnp.int32, (1, HALF), 1)
            begin = begin_of(token, starts_ref)
        dq_part = None
        for n in range(2):
            rows = pl.ds(n * 256, 256)
            keys, values = k_in[slot, rows], v_in[slot, rows]
            nt = (((1,), (1,)), ((), ()))
            scores = lax.dot_general(keys, queries, nt, preferred_element_type=jnp.float32)
            prob_grad = lax.dot_general(values, out_grads, nt, preferred_element_type=jnp.float32)
            soft = jnp.exp(scores - lse)
            if masked:
                key_index = first_k + n * 256 + lax.broadcasted_iota(jnp.int32, (256, 1), 0)
                soft = jnp.where((key_index <= token) & (key_index >= begin), soft, 0.0)
            score_grad = (soft * (prob_grad - delta)).astype(jnp.bfloat16)
            dvacc[rows, :] += jnp.dot(soft.astype(jnp.bfloat16), out_grads, preferred_element_type=jnp.float32)
            dkacc[rows, :] += jnp.dot(score_grad, queries, preferred_element_type=jnp.float32)
            part = jnp.dot(ktbuf[:, n * 256 : (n + 1) * 256], score_grad, preferred_element_type=jnp.float32)
            dq_part = part if dq_part is None else dq_part + part
        dqacc[i] = dqacc[i] + dq_part

    copies = []
    for step, j in enumerate((2, 1, 3, 0)):
        pair = (x + j) % 4
        for turn in range(2):
            cc = 1 - c if turn == 0 else c
            slot = pair * 2 + cc
            first_k = 4096 * pair + 1024 * y + BLK * cc
            dkacc[...] = jnp.zeros_like(dkacc)
            dvacc[...] = jnp.zeros_like(dvacc)
            ktbuf[...] = jnp.transpose(k_in[slot])

            def visit(i, carry):
                first_q = tile_first(i, x, c)
                some = first_k <= first_q + (HALF - 1)
                full = (first_k + BLK - 1 <= first_q) & (first_k > 0) & (first_q < 31 * BLK)

                @pl.when(full)
                def _():
                    tile(i, first_q, slot, first_k, False)

                @pl.when(some & jnp.logical_not(full))
                def _():
                    tile(i, first_q, slot, first_k, True)

                return carry

            lax.fori_loop(0, 8, visit, 0)
            if turn == 0:
                sibsend[step, 0] = dkacc[...].astype(jnp.bfloat16)
                sibsend[step, 1] = dvacc[...].astype(jnp.bfloat16)
                copy = remote(sibsend.at[step], sibrecv.at[step], sib_ssem.at[step], sib_rsem.at[step], sibling)
                copy.start()
                copies.append(copy)
            else:
                remote(sibsend.at[step], sibrecv.at[step], sib_ssem.at[step], sib_rsem.at[step], sibling).wait_recv()
                dk = dkacc[...] + sibrecv[step, 0].astype(jnp.float32)
                dv = dvacc[...] + sibrecv[step, 1].astype(jnp.float32)
                if step < 3:
                    ringsend[step, 0] = dk.astype(jnp.bfloat16)
                    ringsend[step, 1] = dv.astype(jnp.bfloat16)
                    for m in range(2):
                        copy = remote(
                            ringsend.at[step, m], ringrecv.at[step, m], ring_ssem.at[step, m], ring_rsem.at[step, m],
                            at(x + j, y, c, z),
                        )
                        copy.start()
                        copies.append(copy)
                else:
                    dkacc[...] = dk
                    dvacc[...] = dv

    for i in range(8):
        dqsend[i] = jnp.transpose(dqacc[i]).astype(jnp.bfloat16)
    for j in (1, 3, 2):
        i = ((y + j) % 4) * 2
        copies.append(remote(dqsend.at[i], dqrecv.at[y], dq_ssem.at[j - 1], dq_rsem.at[y], at(x, y + j, c, z)))
        copies[-1].start()
    for j in range(4):
        i = j * 2 + 1
        copies.append(
            remote(dqsend.at[i], dqrecv.at[4 + y], dq_ssem.at[3 + j], dq_rsem.at[4 + y], at(3 - x, 3 - j, 1 - c, z))
        )
        copies[-1].start()
    dqrecv[y] = dqsend[own_low]

    for step in range(3):
        for m in range(2):
            remote(
                ringsend.at[step, m], ringrecv.at[step, m], ring_ssem.at[step, m], ring_rsem.at[step, m], sibling
            ).wait_recv()
    for n in range(4):
        rows = pl.ds(n * 128, 128)
        for m, ref in enumerate((dkacc, dvacc)):
            whole = ref[rows, :] + sum(ringrecv[step, m, rows, :].astype(jnp.float32) for step in range(3))
            zpart[n, m * 128 : (m + 1) * 128, :] = whole.astype(jnp.bfloat16)
    for j in (1, 3, 2):
        other = (z + j) % 4
        copies.append(remote(zpart.at[other], zrecv.at[z], z_ssem.at[j - 1], z_rsem.at[z], at(x, y, c, other)))
        copies[-1].start()
    zrecv[z] = zpart[z]

    def dq_arrival(slot):
        remote(dqsend.at[0], dqrecv.at[slot], dq_ssem.at[0], dq_rsem.at[slot], sibling).wait_recv()

    for j in (1, 3, 2):
        dq_arrival((y + j) % 4)
    for j in range(4):
        dq_arrival(4 + j)
    for upper in range(2):
        dq_ref[pl.ds(upper * HALF, HALF), :] = sum(dqrecv[4 * upper + n].astype(jnp.float32) for n in range(4))

    for j in (1, 3, 2):
        other = (z + j) % 4
        remote(zpart.at[0], zrecv.at[other], z_ssem.at[0], z_rsem.at[other], sibling).wait_recv()
    dkv_ref[z] = sum(zrecv[n].astype(jnp.float32) for n in range(4)).astype(jnp.bfloat16)
    for j in (1, 3, 2):
        copies.append(remote(dkv_ref.at[z], dkv_ref.at[z], g_ssem.at[j - 1], g_rsem.at[z], at(x, y, c, z + j)))
        copies[-1].start()
    for j in (1, 3, 2):
        other = (z + j) % 4
        remote(zpart.at[0], dkv_ref.at[other], g_ssem.at[0], g_rsem.at[other], sibling).wait_recv()
    for copy in sends + copies:
        copy.wait_send()


def backward_attention(doc_starts, out_grad, stats, q_all, k_all, v_all):
    vmem = pl.BlockSpec(memory_space=pltpu.VMEM)
    dma = pltpu.SemaphoreType.DMA
    low, full = jnp.bfloat16, jnp.float32
    return pl.pallas_call(
        attn_backward,
        name="attn_backward",
        out_shape=[
            jax.ShapeDtypeStruct((BLK, HD), full),
            jax.ShapeDtypeStruct((4, 256, HD), low),
        ],
        in_specs=[pl.BlockSpec(memory_space=pltpu.SMEM)] + [vmem] * 5,
        out_specs=[vmem] * 2,
        scratch_shapes=[
            pltpu.VMEM((8, HALF, HD), low),
            pltpu.VMEM((8, 8, HALF), full),
            pltpu.VMEM((8, HD, HALF), full),
            pltpu.VMEM((BLK, HD), full),
            pltpu.VMEM((BLK, HD), full),
            pltpu.VMEM((HD, BLK), low),
            pltpu.VMEM((4, 2, BLK, HD), low),
            pltpu.VMEM((4, 2, BLK, HD), low),
            pltpu.VMEM((3, 2, BLK, HD), low),
            pltpu.VMEM((3, 2, BLK, HD), low),
            pltpu.VMEM((8, HALF, HD), low),
            pltpu.VMEM((8, HALF, HD), low),
            pltpu.VMEM((4, 256, HD), low),
            pltpu.VMEM((8, 128), low),
            pltpu.VMEM((4, 256, HD), low),
            dma((7,)), dma((8,)), dma((7,)), dma((8,)), dma((4,)), dma((4,)), dma((3, 2)), dma((3, 2)),
            dma((7,)), dma((8,)), dma((3,)), dma((4,)), dma((3,)), dma((4,)),
        ],
        compiler_params=pltpu.CompilerParams(
            collective_id=2, has_side_effects=True, vmem_limit_bytes=48 << 20
        ),
        cost_estimate=pl.CostEstimate(flops=60 * 10**9, bytes_accessed=20 * 2**20, transcendentals=5 * 10**6),
    )(doc_starts, out_grad, stats, q_all, k_all, v_all)


def head_sum_kernel(part_ref, out_ref, recv, s_ssem, s_rsem, g_ssem, g_rsem):
    x, y, c, z = place()
    peers = [at(x, y, c, z + j) for j in (1, 3, 2)]
    greet(peers)
    rows = part_ref.shape[0] // 4

    def block(ref, n):
        return ref.at[pl.ds(pl.multiple_of(n * rows, rows), rows)]

    copies = []
    for n, j in enumerate((1, 3, 2)):
        copies.append(remote(block(part_ref, (z + j) % 4), recv.at[z], s_ssem.at[n], s_rsem.at[z], peers[n]))
        copies[-1].start()
    for j in (1, 3, 2):
        other = (z + j) % 4
        remote(block(part_ref, 0), recv.at[other], s_ssem.at[0], s_rsem.at[other], peers[0]).wait_recv()
    own = pl.ds(pl.multiple_of(z * rows, rows), rows)
    total = part_ref[own, :].astype(jnp.float32)
    for j in (1, 3, 2):
        total = total + recv[(z + j) % 4].astype(jnp.float32)
    out_ref[own, :] = total.astype(out_ref.dtype)
    for n, j in enumerate((1, 3, 2)):
        copies.append(remote(block(out_ref, z), block(out_ref, z), g_ssem.at[n], g_rsem.at[z], peers[n]))
        copies[-1].start()
    for j in (1, 3, 2):
        other = (z + j) % 4
        remote(block(part_ref, 0), block(out_ref, other), g_ssem.at[0], g_rsem.at[other], peers[0]).wait_recv()
    for copy in copies:
        copy.wait_send()


def head_sum(part, number):
    vmem = pl.BlockSpec(memory_space=pltpu.VMEM)
    dma = pltpu.SemaphoreType.DMA
    rows, columns = part.shape
    return pl.pallas_call(
        head_sum_kernel,
        name=f"head_sum_{number}",
        out_shape=jax.ShapeDtypeStruct(part.shape, part.dtype),
        in_specs=[vmem],
        out_specs=vmem,
        scratch_shapes=[
            pltpu.VMEM((4, rows // 4, columns), part.dtype),
            dma((3,)), dma((4,)), dma((3,)), dma((4,)),
        ],
        compiler_params=pltpu.CompilerParams(
            collective_id=3 + number, has_side_effects=True, vmem_limit_bytes=32 << 20
        ),
        cost_estimate=pl.CostEstimate(flops=10**7, bytes_accessed=10 * 2**20, transcendentals=0),
    )(part)


def head_gather_kernel(part_ref, out_ref, g_ssem, g_rsem):
    x, y, c, z = place()
    peers = [at(x, y, c, z + j) for j in (1, 3, 2)]
    greet(peers)
    width = part_ref.shape[1]

    def block(n):
        return out_ref.at[:, pl.ds(pl.multiple_of(n * width, width), width)]

    copies = []
    for n, j in enumerate((1, 3, 2)):
        copies.append(remote(part_ref, block(z), g_ssem.at[n], g_rsem.at[z], peers[n]))
        copies[-1].start()
    out_ref[:, pl.ds(pl.multiple_of(z * width, width), width)] = part_ref[...]
    for j in (1, 3, 2):
        other = (z + j) % 4
        remote(part_ref, block(other), g_ssem.at[0], g_rsem.at[other], peers[0]).wait_recv()
    for copy in copies:
        copy.wait_send()


def head_gather(part):
    vmem = pl.BlockSpec(memory_space=pltpu.VMEM)
    dma = pltpu.SemaphoreType.DMA
    rows, columns = part.shape
    return pl.pallas_call(
        head_gather_kernel,
        name="head_gather",
        out_shape=jax.ShapeDtypeStruct((rows, 4 * columns), part.dtype),
        in_specs=[vmem],
        out_specs=vmem,
        scratch_shapes=[dma((3,)), dma((4,))],
        compiler_params=pltpu.CompilerParams(
            collective_id=8, has_side_effects=True, vmem_limit_bytes=32 << 20
        ),
        cost_estimate=pl.CostEstimate(flops=10**7, bytes_accessed=10 * 2**20, transcendentals=0),
    )(part)


def per_device(
    tokens,
    cotangent,
    doc_starts,
    query_weight,
    key_weight,
    value_weight,
    out_weight,
    gate_weight,
    up_weight,
    down_weight,
    input_gain,
    attn_gain,
    prenorm_gain,
    post_gain,
    query_gain,
    key_gain,
):
    row_count = tokens.shape[0]
    first_row = lax.axis_index("seq") * row_count
    own_index = first_row + jnp.arange(row_count, dtype=jnp.int32)
    own_position = doc_layout(doc_starts, own_index)[1]
    cos_table, sine_table = rope_tables(own_position, HD)
    query_scale = HD ** (-0.5)
    inputs = tokens.astype(jnp.float32)
    query_weight_all = lax.all_gather(query_weight, "head", axis=1, tiled=True)
    out_weight_all = lax.all_gather(out_weight, "head", axis=0, tiled=True)
    normed, input_back = jax.vjp(rms_norm, inputs, input_gain)
    normed_low = normed.astype(jnp.bfloat16)
    query_raw = jnp.dot(normed_low, query_weight, preferred_element_type=jnp.float32)
    key_raw = jnp.dot(normed_low, key_weight, preferred_element_type=jnp.float32)
    value_low = jnp.dot(normed_low, value_weight, preferred_element_type=jnp.float32).astype(
        jnp.bfloat16
    )

    def query_piece(source, scaling):
        return rotate(rms_norm(source, scaling), cos_table, sine_table) * query_scale

    def key_piece(source, scaling):
        return rotate(rms_norm(source, scaling), cos_table, sine_table)

    query_rows, query_back = jax.vjp(query_piece, query_raw, query_gain)
    query_low = query_rows.astype(jnp.bfloat16)
    key_rows, key_back = jax.vjp(key_piece, key_raw, key_gain)
    key_low = key_rows.astype(jnp.bfloat16)
    mix_all, lse_rows, q_all, k_all, v_all = forward_attention(
        doc_starts, query_low, key_low, value_low
    )
    attn_mix = lax.dynamic_slice_in_dim(mix_all, lax.axis_index("head") * HD, HD, 1)
    attn_out = jnp.dot(mix_all, out_weight_all, preferred_element_type=jnp.float32)
    hidden_state, attn_back = jax.vjp(residual_norm, inputs, attn_out, attn_gain)
    ffn_in, prenorm_back = jax.vjp(rms_norm, hidden_state, prenorm_gain)
    ffn_low = ffn_in.astype(jnp.bfloat16)
    gate_rows = jnp.dot(ffn_low, gate_weight, preferred_element_type=jnp.float32)
    up_rows = jnp.dot(ffn_low, up_weight, preferred_element_type=jnp.float32)
    act_rows, act_back = jax.vjp(gated_act, gate_rows, up_rows)
    act_low = act_rows.astype(jnp.bfloat16)
    ffn_out = head_sum(
        jnp.dot(act_low, down_weight, preferred_element_type=jnp.float32).astype(jnp.bfloat16), 0
    ).astype(jnp.float32)
    mixed, post_back = jax.vjp(residual_norm, hidden_state, ffn_out, post_gain)
    upstream = cotangent.astype(jnp.float32)
    hidden_grad, ffn_out_grad, post_gain_grad = post_back(upstream)
    ffn_out_low = ffn_out_grad.astype(jnp.bfloat16)
    down_weight_grad = dot_first(act_low, ffn_out_low).astype(jnp.bfloat16)
    act_grad = dot_last(ffn_out_low, down_weight)
    gate_grad, up_grad = act_back(act_grad)
    gate_low = gate_grad.astype(jnp.bfloat16)
    up_low = up_grad.astype(jnp.bfloat16)
    gate_weight_grad = dot_first(ffn_low, gate_low).astype(jnp.bfloat16)
    up_weight_grad = dot_first(ffn_low, up_low).astype(jnp.bfloat16)
    ffn_in_grad = head_sum(
        (dot_last(gate_low, gate_weight) + dot_last(up_low, up_weight)).astype(jnp.bfloat16), 1
    ).astype(jnp.float32)
    hidden_more, prenorm_gain_grad = prenorm_back(ffn_in_grad)
    hidden_grad = hidden_grad + hidden_more
    input_grad, attn_out_grad, attn_gain_grad = attn_back(hidden_grad)
    attn_out_low = attn_out_grad.astype(jnp.bfloat16)
    out_weight_grad = dot_first(attn_mix, attn_out_low)
    mix_grad = dot_last(attn_out_low, out_weight).astype(jnp.bfloat16)
    delta = jnp.sum(mix_grad.astype(jnp.float32) * attn_mix.astype(jnp.float32), axis=1)
    stats = jnp.stack([lse_rows[0], delta] + [jnp.zeros_like(delta)] * 6)
    stats = jnp.transpose(stats.reshape(8, 2, HALF), (1, 0, 2))
    down_weight_grad, gate_weight_grad, up_weight_grad, mix_grad = lax.optimization_barrier(
        (down_weight_grad, gate_weight_grad, up_weight_grad, mix_grad)
    )
    down_weight_grad, gate_weight_grad, up_weight_grad = lax.psum(
        (down_weight_grad, gate_weight_grad, up_weight_grad), "seq"
    )
    query_grad, key_value_grad = backward_attention(
        doc_starts, mix_grad, stats, q_all, k_all, v_all
    )
    key_value_grad = key_value_grad.reshape(4, 2, 128, HD)
    key_grad = key_value_grad[:, 0].reshape(row_count, HD).astype(jnp.float32)
    value_grad_low = key_value_grad[:, 1].reshape(row_count, HD)
    query_raw_grad, query_gain_part = query_back(query_grad)
    query_raw_low = query_raw_grad.astype(jnp.bfloat16)
    query_weight_grad = dot_first(normed_low, query_raw_low)
    query_raw_all = head_gather(query_raw_low)
    key_raw_grad, key_gain_grad = key_back(key_grad)
    key_raw_low = key_raw_grad.astype(jnp.bfloat16)
    key_weight_grad = dot_first(normed_low, key_raw_low)
    value_weight_grad = dot_first(normed_low, value_grad_low)
    normed_grad = (
        dot_last(query_raw_all, query_weight_all)
        + dot_last(key_raw_low, key_weight)
        + dot_last(value_grad_low, value_weight)
    )
    input_more, input_gain_grad = input_back(normed_grad)
    tokens_grad = input_grad + input_more
    query_gain_part = lax.psum(query_gain_part, "head")
    late = (
        query_weight_grad,
        key_weight_grad,
        value_weight_grad,
        out_weight_grad,
        input_gain_grad,
        attn_gain_grad,
        prenorm_gain_grad,
        post_gain_grad,
        query_gain_part,
        key_gain_grad,
    )
    late = tuple(piece.astype(jnp.bfloat16) for piece in late)
    late, down_weight_grad, gate_weight_grad, up_weight_grad = lax.optimization_barrier(
        (late, down_weight_grad, gate_weight_grad, up_weight_grad)
    )
    (
        query_weight_grad,
        key_weight_grad,
        value_weight_grad,
        out_weight_grad,
        input_gain_grad,
        attn_gain_grad,
        prenorm_gain_grad,
        post_gain_grad,
        query_gain_grad,
        key_gain_grad,
    ) = (piece.astype(jnp.float32) for piece in lax.psum(late, "seq"))
    gate_weight_grad = gate_weight_grad.astype(jnp.float32)
    up_weight_grad = up_weight_grad.astype(jnp.float32)
    down_weight_grad = down_weight_grad.astype(jnp.float32)
    return (
        mixed.astype(jnp.bfloat16),
        tokens_grad,
        query_weight_grad,
        key_weight_grad,
        value_weight_grad,
        out_weight_grad,
        gate_weight_grad,
        up_weight_grad,
        down_weight_grad,
        input_gain_grad,
        attn_gain_grad,
        prenorm_gain_grad,
        post_gain_grad,
        query_gain_grad,
        key_gain_grad,
    )


def solution(mesh):
    placed = (
        P("seq", None),
        P("seq", None),
        P(),
        P(None, "head"),
        P(),
        P(),
        P("head", None),
        P(None, "head"),
        P(None, "head"),
        P("head", None),
        P(),
        P(),
        P(),
        P(),
        P(),
        P(),
    )
    return jax.shard_map(
        per_device,
        mesh=mesh,
        in_specs=placed,
        out_specs=(
            P("seq", None),
            P("seq", None),
            P(None, "head"),
            P(),
            P(),
            P("head", None),
            P(None, "head"),
            P(None, "head"),
            P("head", None),
            P(),
            P(),
            P(),
            P(),
            P(),
            P(),
        ),
        check_vma=False,
    )
```

time: 1370 us -> 572 us (0.42)
  waiting for transfers between devices: 989 us -> 31.7 us
  Pallas kernels: 0 us -> 265 us
  other arithmetic: 83.9 us -> 47.6 us
  local copies, waits for them, and re-layouts: 45.5 us -> 12.5 us
  matrix products: 86.6 us -> 58.5 us
    reduce_scatter x2 -> x0, waiting for transfers between devices: 619 us -> none  [the longest x1 523 us: per_device(): lax.psum_scatter(key_all_grad.astype(jnp.bfloat16), 'seq', scatter_dimens...]
    pallas_call x0 -> x5, Pallas kernels: none -> 265 us  [the longest x1 98.7 us: forward_attention(): pl.pallas_call(attn_forward, name='attn_forward', out_shape=[jax.ShapeDty...]
    psum x5 -> x2, waiting for transfers between devices: 269 us -> 30.3 us  [the longest x1 30.3 us: per_device(): lax.psum((down_weight_grad, gate_weight_grad, up_weight_grad), 'seq')]
    all_gather x2, waiting for transfers between devices: 100 us -> 0.01 us  [the longest x1 0.01 us: per_device(): out_weight_all = lax.all_gather(out_weight, 'head', axis=0, tiled=True)]
    dot_general x19 -> x1, matrix products: 29 us -> 3.33 us  [per_device(): jnp.dot(mix_all, out_weight_all, preferred_element_type=jnp.float32)]
    convert_element_type x16 -> x14, other arithmetic: 44.1 us -> 25.3 us  [the longest x10 10.1 us: per_device(): piece.astype(jnp.float32)]
    another operation x6 -> x4, local copies, waits for them, and re-layouts: 14.7 us -> 0.16 us  [per_device(): stats = jnp.stack([lse_rows[0], delta] + [jnp.zeros_like(delta)] * 6)]
  transfers between devices with their start and end apart: 9 -> 4, of which waited for: 8 -> 1; matrix products, arithmetic and copies ran while one was open for 5% -> 18% of each run, Pallas kernels for 0% -> 47%
where the time goes in v1:
time: 572 us; the launch traced here: 561 us
  Pallas kernels  265 us (46%)
  blocking collectives  130 us (23%)
  matrix products  58.5 us (10%)
  other arithmetic  47.6 us (8%)
  waiting for transfers between devices  31.7 us (6%)
  between operations  14.8 us (3%)
  local copies, waits for them, and re-layouts  12.5 us (2%)
    psum x1, blocking collectives, per_device(): lax.psum(late, 'seq')  122 us
    pallas_call x1, Pallas kernels, forward_attention(): pl.pallas_call(attn_forward, name='attn_forward', out_shape=[jax.ShapeDty...  98.7 us
    pallas_call x1, Pallas kernels, backward_attention(): pl.pallas_call(attn_backward, name='attn_backward', out_shape=[jax.ShapeD...  96.4 us
    pallas_call x2, Pallas kernels, head_sum(): pl.pallas_call(head_sum_kernel, name=f'head_sum_{number}', out_shape=jax....  55.6 us
    psum x1, waiting for transfers between devices, per_device(): lax.psum((down_weight_grad, gate_weight_grad, up_weight_grad), 'seq')  30.3 us
    dot_general x7, matrix products, dot_first(): lax.dot_general(left_side, right_side, (((0,), (0,)), ((), ())), preferre...  21.8 us
    dot_general x7, matrix products, dot_last(): lax.dot_general(left_side, right_side, (((1,), (1,)), ((), ())), preferre...  19.7 us
    pallas_call x1, Pallas kernels, head_gather(): pl.pallas_call(head_gather_kernel, name='head_gather', out_shape=jax.Shap...  14.2 us
  transfers between devices with their start and end apart: 4, of which 1 were waited for; matrix products, arithmetic and copies ran while one was open for 18% of the time, Pallas kernels for 47%

profile of v1, /device:TPU:1, one launch (start us, length us, event | category | flops | bytes accessed | tf_op | source)
XLA Modules:
  0.0 560.8 jit_solution(5488380791691309439)
XLA Ops:
  9.6 1.6 fusion.26
  11.2 1.5 multiply_reduce_fusion.10
  12.7 1.5 multiply_reduce_fusion.9
  14.1 1.2 copy.40
  15.4 1.4 copy.39
  19.7 3.3 fusion.44
  22.9 98.7 %attn_forward.1 = (bf16[512,1024]{1,0:T(8,128)(2,1)S(1)}, f32[8,512]{1,0:T(8,128)S(1)}, bf16[8,256,256]{2,1,0:T(8,128)(2,1)S(1)}, bf16[8,512,256]{2,1,0:T(8,128)(2,1)S(1)}, bf16[8,512,256]{2,1,0:T(8,128)(2,1)S(1)}) custom-call(s32[7]{0:T(128)S(1)} %copy-done.1, bf16[512,256]{1,0:T(8,128)(2,1)S(1)} %get-tuple-element.108.q_ref, ...), custom_call_target="tpu_custom_call" | custom-call | flops 6000000000 | bytes 20971520 | tf_op jit(solution)/shard_map/attn_forward/pallas_call | solution.py:278
  121.7 1.3 copy-done.2
  123.0 1.4 copy-done.4
  125.5 3.3 multiply_reduce_fusion.3
  129.8 1.2 copy-done.37
  131.0 2.5 fusion.70
  133.5 5.1 multiply_convert_fusion.1
  138.6 2.6 convolution_convert_fusion.3.part_ref
  141.2 28.7 %head_sum_0.1 = bf16[512,1152]{1,0:T(8,128)(2,1)S(1)} custom-call(bf16[512,1152]{1,0:T(8,128)(2,1)S(1)} %convolution_convert_fusion.3.part_ref), custom_call_target="tpu_custom_call" | custom-call | flops 10000000 | bytes 10485760 | tf_op jit(solution)/shard_map/head_sum_0/pallas_call | solution.py:545
  171.3 7.6 %multiply_convert_fusion = (bf16[512,1728]{0,1:T(8,128)(2,1)S(1)}, bf16[512,1728]{0,1:T(8,128)(2,1)S(1)}) fusion(f32[512,1728]{0,1:T(8,128)} %copy-done.38, f32[512,1728]{0,1:T(8,128)} %get-tuple-element.116, bf16[1728,1152]{1,0:T(8,128)(2,1)S(1)} %copy-done.36, bf16[512,1152]{1,0:T(8,128)(2,1)S(1)} %copy-done.17, bf16[512,1152]{1,0:T(8,128)(2,1)S(1)} %head_sum_0.1, ...), kind=kOutput, calls=%fused_computation.21 | convolution fusion | flops 2064384000 | bytes 16966144 | tf_op jit(solution)/shard_map/dot_general | solution.py:47
  178.8 2.6 fusion.71
  181.5 2.6 fusion.7.part_ref
  184.1 26.9 %head_sum_1.1 = bf16[512,1152]{1,0:T(8,128)(2,1)S(1)} custom-call(bf16[512,1152]{1,0:T(8,128)(2,1)S(1)} %fusion.7.part_ref), custom_call_target="tpu_custom_call" | custom-call | flops 10000000 | bytes 10485760 | tf_op jit(solution)/shard_map/head_sum_1/pallas_call | solution.py:545
  211.8 2.9 multiply_reduce_fusion
  216.8 4.4 convolution_convert_fusion.1
  221.2 4.4 convolution_convert_fusion
  225.6 4.6 convolution_convert_fusion.2
  230.4 1.6 copy-done.3
  232.0 1.2 copy-done.6
  233.2 96.4 %attn_backward.1 = (f32[512,256]{1,0:T(8,128)S(1)}, bf16[4,256,256]{2,1,0:T(8,128)(2,1)S(1)}) custom-call(s32[7]{0:T(128)S(1)} %copy-done.1, bf16[512,256]{1,0:T(8,128)(2,1)S(1)} %get-tuple-element.40.do_ref, f32[2,8,256]{2,1,0:T(8,128)S(1)} %maximum_bitcast_fusion.stat_ref, bf16[8,256,256]{2,1,0:T(8,128)(2,1)S(1)} %copy-done.6, ...), custom_call_target="tpu_custom_call" | custom-call | flops 60000002048 | bytes 20971520 | tf_op jit(solution)/shard_map/attn_backward/pallas_call | solution.py:475
  329.6 1.8 convert_multiply_fusion.12
  331.5 1.4 multiply_reduce_fusion.4
  332.9 2.4 fusion.31
  335.4 1.4 multiply_reduce_fusion.5
  337.0 14.2 %head_gather.1 = bf16[512,1024]{1,0:T(8,128)(2,1)S(1)} custom-call(bf16[512,256]{1,0:T(8,128)(2,1)S(1)} %fusion.30.part_ref), custom_call_target="tpu_custom_call" | custom-call | flops 10000000 | bytes 10485760 | tf_op jit(solution)/shard_map/head_gather/pallas_call | solution.py:587
  351.2 8.1 %psum.98 = bf16[256]{0:T(256)(128)(2,1)S(1)} all-reduce(f32[256]{0:T(256)S(1)} %get-tuple-element.73), channel_id=1, replica_groups=mesh['seq'=32,'head'=4] {'head'}, use_global_device_ids=true, to_apply=%region_19.20 | all-reduce | flops 256 | bytes 1536 | tf_op jit(solution)/shard_map/psum | solution.py:711
  359.3 2.7 convolution_convert_fusion.4
  362.0 2.7 convolution_convert_fusion.7
  364.8 1.5 convolution_convert_fusion.6
  366.2 1.5 convolution_convert_fusion.5
  367.7 3.3 fusion.72
  372.4 2.4 fusion.15
  374.8 30.3 %all-reduce.12.cloned.1.call-done = (bf16[1728,1152]{1,0:T(8,128)(2,1)}, bf16[1152,1728]{0,1:T(8,128)(2,1)}, bf16[1152,1728]{0,1:T(8,128)(2,1)}) async-done(((bf16[1728,1152]{1,0:T(8,128)(2,1)}, bf16[1152,1728]{0,1:T(8,128)(2,1)}, bf16[1152,1728]{0,1:T(8,128)(2,1)}), (bf16[1728,1152]{1,0:T(8,128)(2,1)}, bf16[1152,1728]{0,1:T(8,128)(2,1)}, bf16[1152,1728]{0,1:T(8,128)(2,1)})) %all-reduce.12.cloned.1.call-update) | async-done | bytes 11943952 | tf_op jit(solution)/shard_map/psum | solution.py:687
  405.1 4.2 fusion.23
  409.3 4.0 convert_element_type.199
  413.3 4.2 convert_element_type.200
  417.4 3.8 convert_element_type.201
  421.2 122.4 %all-reduce.4 = (bf16[1152]{0:T(1024)(128)(2,1)S(1)}, bf16[1152]{0:T(1024)(128)(2,1)S(1)}, bf16[1152]{0:T(1024)(128)(2,1)S(1)}, bf16[1152]{0:T(1024)(128)(2,1)S(...) all-reduce(bf16[1152]{0:T(1024)(128)(2,1)S(1)} %get-tuple-element.5, ...), channel_id=1, replica_groups=mesh['seq'=32,'head'=4] {'seq'}, use_global_device_ids=true, to_apply=%region_28.29 | all-reduce | flops 5120 | bytes 20480 | tf_op jit(solution)/shard_map/psum | solution.py:739
  547.2 2.3 convert_element_type.195
  549.4 2.2 convert_element_type.196
  551.6 1.1 convert_element_type.197
  552.7 1.1 convert_element_type.198
  (129 shorter events, 16.8 us)
Async XLA Ops:
  7.2 11.7 %copy-start = (bf16[1152,256]{1,0:T(8,128)(2,1)S(1)}, bf16[1152,256]{1,0:T(8,128)(2,1)}, u32[]{:S(2)}) copy-start(bf16[1152,256]{1,0:T(8,128)(2,1)} %param.21) | copy-start | bytes 1769476
  7.2 3.9 copy-start.27
  7.2 3.9 copy-start.9
  7.2 3.9 copy-start.33
  7.2 118.2 %all-gather.3.cloned.1.call-start = ((), (), s32[]{:S(2)}) async-start(), calls=%async_computation | async-start | bytes 2949120 | tf_op jit(solution)/shard_map/all_gather | solution.py:627
  8.0 4.7 copy-start.28
  8.0 359.7 %all-gather.5.cloned.1.call-start = ((), (), s32[]{:S(2)}) async-start(), calls=%async_computation.1 | async-start | bytes 2949120 | tf_op jit(solution)/shard_map/all_gather | solution.py:626
  8.7 396.4 %all-reduce.12.cloned.1.call-start = ((), (), s32[]{:S(2)}) async-start(), calls=%async_computation.3 | async-start | bytes 23887872 | tf_op jit(solution)/shard_map/psum | solution.py:687
  12.7 4.2 copy-start.34
  12.7 4.2 copy-start.35
  15.4 3.5 copy-start.13
  16.8 2.7 copy-start.15
  17.1 1.8 copy-start.19
  17.1 1.8 copy-start.20
  19.5 3.4 copy-start.1
  121.7 1.3 copy-start.2
  123.0 1.4 copy-start.4
  124.3 1.0 copy-start.5
  125.5 3.3 copy-start.31
  128.8 0.7 copy-start.30
  128.8 2.1 copy-start.37
  131.0 2.5 copy-start.12
  133.5 5.1 copy-start.38
  133.5 5.1 copy-start.36
  141.2 29.1 %copy-start.17 = (bf16[512,1152]{1,0:T(8,128)(2,1)S(1)}, bf16[512,1152]{1,0:T(8,128)(2,1)}, u32[]{:S(2)}) copy-start(bf16[512,1152]{1,0:T(8,128)(2,1)} %param.17) | copy-start | bytes 3538948
  141.2 29.1 %copy-start.32 = (f32[1152]{0:T(1024)S(1)}, f32[1152]{0:T(1024)}, u32[]{:S(2)}) copy-start(f32[1152]{0:T(1024)} %param.29) | copy-start | bytes 13828
  214.6 1.4 copy-start.7
  214.7 1.5 copy-start.26
  216.2 5.0 copy-start.18
  230.3 316.8 %all-reduce.10.cloned.1.call-start = ((), (), s32[]{:S(2)}) async-start(), calls=%async_computation.2 | async-start | bytes 4718592 | tf_op jit(solution)/shard_map/psum | solution.py:739
  230.4 1.6 copy-start.3
  232.0 1.2 copy-start.6
  329.6 1.9 copy-start.14
  332.9 2.5 copy-start.16
  359.3 5.4 copy-start.10
  367.7 3.3 copy-start.29
  371.0 1.4 copy-start.11
  374.8 30.3 %copy-start.8 = (f32[512,1152]{1,0:T(8,128)S(1)}, f32[512,1152]{1,0:T(8,128)}, u32[]{:S(2)}) copy-start(f32[512,1152]{1,0:T(8,128)} %copy-done.7) | copy-start | bytes 7077892
  405.1 4.2 copy-start.23
  409.3 4.0 copy-start.22
  413.3 4.2 copy-start.21
  547.2 4.4 copy-start.25
  547.2 5.5 copy-start.24
Sparse Core Ops, SparseCore 0:
  9.7 36.4 all-gather.2
  47.9 35.9 all-gather.4
  230.4 174.5 all-reduce.11
  409.4 107.3 all-reduce.9

commit v2 on v0

v2 whole, which is shorter than its diff:
```python
import functools
import math

import jax
import jax.numpy as jnp
from jax import lax
from jax.experimental import pallas as pl
from jax.experimental.pallas import tpu as pltpu
from jax.sharding import PartitionSpec as P

HD = 256


EPS = 1e-06
THETA = 1000000.0
NEG = -1e30


def rms_norm(values, scaling):
    return values * lax.rsqrt(jnp.mean(values * values, axis=-1, keepdims=True) + EPS) * scaling


def doc_layout(doc_starts, token_index):
    before = doc_starts[None, :] <= token_index[:, None]
    segment = jnp.sum(before.astype(jnp.int32), axis=1)
    doc_begin = jnp.max(jnp.where(before, doc_starts[None, :], 0), axis=1)
    return (segment, token_index - doc_begin)


def rope_tables(position, head_width):
    half_width = head_width // 2
    inverse = jnp.exp(
        -math.log(THETA) * 2.0 * jnp.arange(half_width, dtype=jnp.float32) / head_width
    )
    angles = position.astype(jnp.float32)[:, None] * inverse[None, :]
    angles = jnp.concatenate([angles, angles], axis=1)
    return (jnp.cos(angles), jnp.sin(angles))


def rotate(values, cos_table, sine_table):
    half_width = values.shape[-1] // 2
    turned = jnp.concatenate([-values[..., half_width:], values[..., :half_width]], axis=-1)
    return values * cos_table + turned * sine_table


def dot_last(left_side, right_side):
    return lax.dot_general(
        left_side, right_side, (((1,), (1,)), ((), ())), preferred_element_type=jnp.float32
    )


def dot_first(left_side, right_side):
    return lax.dot_general(
        left_side, right_side, (((0,), (0,)), ((), ())), preferred_element_type=jnp.float32
    )


def residual_norm(residual, branch, scaling):
    return residual + rms_norm(branch, scaling)


def gated_act(gate_vals, up_vals):
    return jax.nn.gelu(gate_vals, approximate=True) * up_vals


MESH_ID = pl.DeviceIdType.MESH
HALF = 256
BLK = 512
LOW = jnp.bfloat16
FULL = jnp.float32
NT = (((1,), (1,)), ((), ()))


def place():
    s = lax.axis_index("seq")
    return s // 8, (s // 2) % 4, s % 2, lax.axis_index("head")


def at(x, y, c, z):
    return ((x % 4) * 8 + (y % 4) * 2 + c, z % 4)


def greet(peers):
    barrier = pltpu.get_barrier_semaphore()
    for peer in peers:
        pl.semaphore_signal(barrier, inc=1, device_id=peer, device_id_type=MESH_ID)
    pl.semaphore_wait(barrier, len(peers))


def remote(src, dst, send_sem, recv_sem, peer):
    return pltpu.make_async_remote_copy(
        src_ref=src,
        dst_ref=dst,
        send_sem=send_sem,
        recv_sem=recv_sem,
        device_id=peer,
        device_id_type=MESH_ID,
    )


def rows_at(ref, start, size):
    return ref.at[pl.ds(pl.multiple_of(start, 16), size)]


class RingGather:
    def __init__(self, view, me, plus, minus, sems, ring, source=None):
        send, recv = sems

        def near(rel, half):
            return view((me + rel) % 4, half)

        own = source or (lambda half: near(0, half))
        plan = (
            (own(0), near(0, 0), plus),
            (own(1), near(0, 1), plus),
            (near(3, 0), near(3, 0), plus),
            (own(0), near(0, 0), minus),
            (own(1), near(0, 1), minus),
            (near(1, 1), near(1, 1), minus),
        )
        self.copies = [
            remote(src, dst, send.at[ring, k], recv.at[ring, k], peer) for k, (src, dst, peer) in enumerate(plan)
        ]

    def own(self, half):
        self.copies[half].start()
        self.copies[3 + half].start()

    def forward(self):
        self.copies[0].wait_recv()
        self.copies[2].start()
        self.copies[4].wait_recv()
        self.copies[5].start()

    def near(self):
        self.copies[1].wait_recv()
        self.copies[3].wait_recv()

    def far(self):
        self.copies[2].wait_recv()
        self.copies[5].wait_recv()

    def drain(self):
        for copy in self.copies:
            copy.wait_send()


class RingReduce:
    def __init__(self, view, passing, got, plus, minus, sems, ring):
        send, recv = sems
        self.view, self.passing, self.got = view, passing, got
        plan = (
            (view(2, 0), passing(0), minus),
            (view(2, 1), passing(1), plus),
            (view(3, 1), got(0, 1), minus),
            (view(1, 0), got(1, 0), plus),
            (passing(0), got(0, 0), minus),
            (passing(1), got(1, 1), plus),
        )
        self.copies = [
            remote(src, dst, send.at[ring, k], recv.at[ring, k], peer) for k, (src, dst, peer) in enumerate(plan)
        ]

    def start(self, *numbers):
        for k in numbers or (0, 1, 2, 3):
            self.copies[k].start()

    def relay(self):
        for half, rel in ((0, 3), (1, 1)):
            self.copies[half].wait_recv()
            land, term = self.passing(half), self.view(rel, half)
            land[...] = (land[...].astype(FULL) + term[...].astype(FULL)).astype(LOW)
            self.copies[4 + half].start()

    def finish(self):
        for k in (2, 3, 4, 5):
            self.copies[k].wait_recv()

    def arrived(self, half):
        return self.got(0, half)[...].astype(FULL) + self.got(1, half)[...].astype(FULL)

    def drain(self):
        for copy in self.copies:
            copy.wait_send()


def tile_first(i, x, c):
    column = jnp.where(i % 2 == 1, 3 - x, x)
    return BLK * (8 * column + 2 * (i // 2) + c) + HALF * (i % 2)


def begin_of(token, starts_ref):
    begin = jnp.zeros_like(token)
    for n in range(starts_ref.shape[0]):
        start = starts_ref[n]
        begin = jnp.where(start <= token, start, begin)
    return begin


def attn_forward(
    starts_ref, q_ref, k_ref, v_ref,
    mix_ref, lse_ref, qg_ref, kg_ref, vg_ref,
    acc, lacc, osend, opass, ogot, lsend, lrecv, hsend, lhsend,
    rs, rr, sib_s, sib_r, l_s, l_r, sw_s, sw_r,
):
    x, y, c, z = place()
    xp, xm, yp, ym = at(x + 1, y, c, z), at(x + 3, y, c, z), at(x, y + 1, c, z), at(x, y + 3, c, z)
    zp, zm, y2 = at(x, y, c, z + 1), at(x, y, c, z + 3), at(x, y + 2, c, z)
    sibling, partner = at(x, y, 1 - c, z), at(3 - x, y, c, z)
    greet([partner, sibling, xp, xm, yp, ym, y2, zp, zm])
    copies = []

    def go(copy):
        copy.start()
        copies.append(copy)

    q_low, q_high = q_ref.at[pl.ds(0, HALF)], q_ref.at[pl.ds(HALF, HALF)]
    swap = remote(q_high, qg_ref.at[2 * y + 1], sw_s.at[0], sw_r.at[0], partner)
    go(swap)

    def kv_view(index, half):
        return (kg_ref, vg_ref)[half].at[2 * index + c]

    kv = RingGather(kv_view, x, xp, xm, (rs, rr), 0, lambda half: (k_ref, v_ref)[half])
    kv.own(0)
    kv.own(1)
    qs = RingGather(
        lambda index, half: qg_ref.at[2 * index + half], y, yp, ym, (rs, rr), 1,
        lambda half: q_low if half == 0 else qg_ref.at[2 * y + 1],
    )
    qs.own(0)

    def pass_on(index, half, source=None):
        block = kv_view(index, half)
        return remote(block if source is None else source, block, sib_s.at[index, half], sib_r.at[index, half], sibling)

    for half, source in enumerate((k_ref, v_ref)):
        go(pass_on(x, half, source))
    qg_ref[2 * y] = q_ref[0:HALF, :]
    kg_ref[2 * x + c] = k_ref[...]
    vg_ref[2 * x + c] = v_ref[...]
    acc[...] = jnp.zeros_like(acc)
    lacc[...] = jnp.zeros_like(lacc)
    swap.wait_recv()
    qs.own(1)
    kv.forward()
    qs.forward()
    kv.near()
    for rel in (1, 3):
        for half in range(2):
            go(pass_on((x + rel) % 4, half))
    qs.near()
    qs.far()

    def chunk(i, first_q, pair, first_k, masked):
        queries = qg_ref[i]
        if masked:
            token = first_q + lax.broadcasted_iota(jnp.int32, (HALF, 1), 0)
            begin = begin_of(token, starts_ref)
        total = None
        sums = None
        for cc in range(2):
            keys, values = kg_ref[pair * 2 + cc], vg_ref[pair * 2 + cc]
            scores = lax.dot_general(queries, keys, NT, preferred_element_type=FULL)
            exps = jnp.exp(scores)
            if masked:
                key_index = first_k + cc * BLK + lax.broadcasted_iota(jnp.int32, (1, BLK), 1)
                exps = jnp.where((key_index <= token) & (key_index >= begin), exps, 0.0)
            part = jnp.dot(exps.astype(LOW), values, preferred_element_type=FULL)
            total = part if total is None else total + part
            for n in range(BLK // 128):
                piece = exps[:, n * 128 : (n + 1) * 128]
                sums = piece if sums is None else sums + piece
        acc[i] = acc[i] + total
        lacc[i] = lacc[i] + sums

    for rel in (0, 1, 3, 2):
        pair = (x + rel) % 4
        if rel == 2:
            kv.far()
            for half in range(2):
                go(pass_on(pair, half))
        for half in range(2):
            pass_on(pair, half).wait_recv()
        first_k = 4096 * pair + 1024 * y

        def visit(i, carry):
            first_q = tile_first(i, x, c)
            some = first_k <= first_q + (HALF - 1)
            full = (first_k + 1023 <= first_q) & (first_k > 0) & (first_q < 31 * BLK)

            @pl.when(full)
            def _():
                chunk(i, first_q, pair, first_k, False)

            @pl.when(some & jnp.logical_not(full))
            def _():
                chunk(i, first_q, pair, first_k, True)

            return carry

        lax.fori_loop(0, 8, visit, 0)

    def cast(i, carry):
        osend[i] = acc[i].astype(LOW)
        row = jnp.sum(jnp.transpose(lacc[i]), axis=0, keepdims=True)
        lsend[i] = jnp.broadcast_to(row, (8, HALF))
        return carry

    lax.fori_loop(0, 8, cast, 0)
    numer = RingReduce(
        lambda rel, half: osend.at[2 * ((y + rel) % 4) + half],
        lambda half: opass.at[half],
        lambda side, half: ogot.at[side, half],
        yp, ym, (rs, rr), 2,
    )
    numer.start()

    def sums_to(rel, peer):
        index = (y + rel) % 4
        return remote(lsend.at[pl.ds(2 * index, 2)], lrecv.at[y], l_s.at[rel - 1], l_r.at[y], peer)

    for rel, peer in ((1, yp), (3, ym), (2, y2)):
        go(sums_to(rel, peer))
    lrecv[y] = lsend[pl.ds(2 * y, 2)]
    numer.relay()
    for rel in (1, 3, 2):
        remote(lsend.at[pl.ds(0, 2)], lrecv.at[(y + rel) % 4], l_s.at[0], l_r.at[(y + rel) % 4], sibling).wait_recv()
    numer.finish()

    def mix_view(index, half):
        return mix_ref.at[pl.ds(half * HALF, HALF), pl.ds(pl.multiple_of(index * HD, HD), HD)]

    mixes = RingGather(mix_view, z, zp, zm, (rs, rr), 3)
    returns = (
        remote(hsend, mix_view(z, 1), sw_s.at[1], sw_r.at[1], partner),
        remote(lhsend, lse_ref.at[1], sw_s.at[2], sw_r.at[2], partner),
    )
    for half in (1, 0):
        denom = sum(lrecv[n, half] for n in range(4))
        total = osend[2 * y + half].astype(FULL) + numer.arrived(half)
        inverse = jnp.transpose(jnp.broadcast_to(1.0 / denom[0:1, :], (128, HALF)))
        scaled = (total * jnp.concatenate([inverse, inverse], axis=1)).astype(LOW)
        if half == 1:
            hsend[...] = scaled
            lhsend[...] = jnp.log(denom)
            for copy in returns:
                go(copy)
        else:
            mix_view(z, 0)[...] = scaled
            lse_ref[0] = jnp.log(denom)
    mixes.own(0)
    for copy in returns:
        copy.wait_recv()
    mixes.own(1)
    mixes.forward()
    mixes.near()
    mixes.far()
    for ring in (kv, qs, numer, mixes):
        ring.drain()
    for copy in copies:
        copy.wait_send()


VMEM = pl.BlockSpec(memory_space=pltpu.VMEM)
SMEM = pl.BlockSpec(memory_space=pltpu.SMEM)
ANY = pl.BlockSpec(memory_space=pl.ANY)


def dma(*shape):
    return pltpu.SemaphoreType.DMA(shape)


def shape(dtype, *dims):
    return jax.ShapeDtypeStruct(dims, dtype)


def vmem(dtype, *dims):
    return pltpu.VMEM(dims, dtype)


def params(number, mebibytes):
    return pltpu.CompilerParams(collective_id=number, has_side_effects=True, vmem_limit_bytes=mebibytes << 20)


def cost(gflops):
    return pl.CostEstimate(flops=gflops * 10**9, bytes_accessed=20 * 2**20, transcendentals=0)


def forward_attention(doc_starts, query, key, value):
    return pl.pallas_call(
        attn_forward,
        name="attn_forward",
        out_shape=[
            shape(LOW, BLK, 4 * HD),
            shape(FULL, 2, 8, HALF),
            shape(LOW, 8, HALF, HD),
            shape(LOW, 8, BLK, HD),
            shape(LOW, 8, BLK, HD),
        ],
        in_specs=[SMEM] + [VMEM] * 3,
        out_specs=[VMEM] * 5,
        scratch_shapes=[
            vmem(FULL, 8, HALF, HD),
            vmem(FULL, 8, HALF, 128),
            vmem(LOW, 8, HALF, HD),
            vmem(LOW, 2, HALF, HD),
            vmem(LOW, 2, 2, HALF, HD),
            vmem(FULL, 8, 8, HALF),
            vmem(FULL, 4, 2, 8, HALF),
            vmem(LOW, HALF, HD),
            vmem(FULL, 8, HALF),
            dma(4, 6), dma(4, 6), dma(4, 2), dma(4, 2), dma(3), dma(4), dma(3), dma(3),
        ],
        compiler_params=params(1, 40),
        cost_estimate=cost(6),
    )(doc_starts, query, key, value)


ROWS = 2560
SIDE = ROWS // 2
PIECE = SIDE // 4
WINDOW = PIECE // 4
CUTS = (0, 448, 896, 1280, 1728, 2144, 2560)


def ffn_grads_kernel(
    part_ref, ffn_ref, out_grad_ref, gate_ref, up_ref, act_ref,
    sum_ref, piece_a_ref, piece_b_ref, rest_ref,
    left, right, sib_send, sib_recv, mine, pass_ab, got_ab, z_pass, z_got,
    in_sem, sib_s, sib_r, rs, rr,
):
    x, y, c, z = place()
    xp, xm, yp, ym = at(x + 1, y, c, z), at(x + 3, y, c, z), at(x, y + 1, c, z), at(x, y + 3, c, z)
    zp, zm, sibling = at(x, y, c, z + 1), at(x, y, c, z + 3), at(x, y, 1 - c, z)
    hidden = gate_ref.shape[0]
    loads = [pltpu.make_async_copy(out_grad_ref, right.at[1], in_sem.at[0])]
    loads.append(pltpu.make_async_copy(ffn_ref, right.at[0], in_sem.at[1]))
    for n, ref in enumerate((gate_ref, up_ref, act_ref)):
        loads.append(pltpu.make_async_copy(ref, left.at[pl.ds(n * hidden, hidden)], in_sem.at[2 + n]))
    for load in loads:
        load.start()
    greet([xp, xm, yp, ym, zp, zm, sibling])
    rows = part_ref.shape[0] // 4

    zs = RingReduce(
        lambda rel, half: rows_at(part_ref, ((z + rel) % 4) * rows + half * (rows // 2), rows // 2),
        lambda half: z_pass.at[half],
        lambda side, half: z_got.at[side, half],
        zp, zm, (rs, rr), 0,
    )
    zg = RingGather(
        lambda index, half: rows_at(sum_ref, index * rows + half * (rows // 2), rows // 2),
        z, zp, zm, (rs, rr), 1,
    )
    zs.start()
    for load in loads:
        load.wait()

    def product(core, n, target, added):
        first, size = CUTS[n], CUTS[n + 1] - CUTS[n]
        lhs = left[pl.ds(pl.multiple_of(ROWS * core + first, 16), size), :]
        which = jnp.where(n >= 2, core, 0)
        width = right.shape[2] // 3
        for k in range(3):
            columns = pl.ds(k * width, width)
            tile = jnp.dot(lhs, right[which, :, columns], preferred_element_type=FULL)
            if added is not None:
                tile = tile + added[pl.ds(first, size), columns].astype(FULL)
            target[pl.ds(first, size), columns] = tile.astype(LOW)

    def to_sibling(n):
        span = pl.ds(CUTS[n], CUTS[n + 1] - CUTS[n])
        return remote(sib_send.at[span], sib_recv.at[span], sib_s.at[n], sib_r.at[n], sibling)

    count = len(CUTS) - 1
    for n in range(count):
        product(1 - c, n, sib_send, None)
        to_sibling(n).start()
        if n == count // 2 - 1:
            zs.relay()
    zs.finish()
    for half in range(2):
        own = pl.ds(pl.multiple_of(z * rows + half * (rows // 2), 16), rows // 2)
        sum_ref[own, :] = (part_ref[own, :].astype(FULL) + zs.arrived(half)).astype(LOW)
        zg.own(half)

    def side_ring(h, me, plus, minus):
        return RingReduce(
            lambda rel, half: rows_at(mine, SIDE * h + PIECE * ((me + rel) % 4) + half * (PIECE // 2), PIECE // 2),
            lambda half: pass_ab.at[h, half],
            lambda side, half: got_ab.at[h, side, half],
            plus, minus, (rs, rr), 2 + h,
        )

    rings = (side_ring(0, x, xp, xm), side_ring(1, y, yp, ym))
    for n in range(count):
        to_sibling(n).wait_recv()
        product(c, n, mine, sib_recv)
        if n == count // 2 - 1:
            rings[0].start()
            zg.forward()
    rings[1].start()
    rest = jnp.dot(left[2 * ROWS :, :], right[1], preferred_element_type=FULL)
    rest_ref[...] = rest.astype(LOW)
    for ring in rings:
        ring.relay()
    zg.near()
    zg.far()
    for h, (ring, me, out) in enumerate(((rings[0], x, piece_a_ref), (rings[1], y, piece_b_ref))):
        ring.finish()
        for half in range(2):
            size = PIECE // 2
            own = mine[pl.ds(pl.multiple_of(SIDE * h + PIECE * me + half * size, 16), size), :]
            out[pl.ds(half * size, size), :] = (own.astype(FULL) + ring.arrived(half)).astype(LOW)
    for ring in (zs, zg) + rings:
        ring.drain()
    for n in range(count):
        to_sibling(n).wait_send()


def ffn_grads(part, ffn_low, ffn_out_low, gate_t, up_t, act_t):
    rows, width = part.shape
    hidden = gate_t.shape[0]
    return pl.pallas_call(
        ffn_grads_kernel,
        name="ffn_grads",
        out_shape=[
            shape(LOW, rows, width),
            shape(LOW, PIECE, width),
            shape(LOW, PIECE, width),
            shape(LOW, 3 * hidden - 2 * ROWS, width),
        ],
        in_specs=[VMEM] + [ANY] * 5,
        out_specs=[VMEM] * 4,
        scratch_shapes=[
            vmem(LOW, 3 * hidden, rows),
            vmem(LOW, 2, rows, width),
            vmem(LOW, ROWS, width),
            vmem(LOW, ROWS, width),
            vmem(LOW, ROWS, width),
            vmem(LOW, 2, 2, PIECE // 2, width),
            vmem(LOW, 2, 2, 2, PIECE // 2, width),
            vmem(LOW, 2, rows // 8, width),
            vmem(LOW, 2, 2, rows // 8, width),
            dma(5), dma(6), dma(6), dma(4, 6), dma(4, 6),
        ],
        compiler_params=params(4, 56),
        cost_estimate=cost(6),
    )(part, ffn_low, ffn_out_low, gate_t, up_t, act_t)


def attn_backward(
    starts_ref, do_ref, stat_ref, q_in, k_in, v_in, piece_a_ref, piece_b_ref, raw_ref, cos_ref, sin_ref, gain_ref,
    draw_ref, dgain_ref, dkv_ref, big_ref,
    dog, statg, dqacc, dkacc, dvacc, ktbuf, sibsend, sibrecv, kvsrc, kvpass, kvgot,
    dqsend, dqpass, dqgot, dqback, dqhigh, zpart, zpass, zgot, gaing, winpass, wingot, full_a, full_b,
    rs, rr, st_s, st_r, sw_s, sw_r, sib_s, sib_r, gn_s, gn_r, sf_s, sf_r, own_sem,
):
    x, y, c, z = place()
    xp, xm, yp, ym = at(x + 1, y, c, z), at(x + 3, y, c, z), at(x, y + 1, c, z), at(x, y + 3, c, z)
    zp, zm, y2, z2 = at(x, y, c, z + 1), at(x, y, c, z + 3), at(x, y + 2, c, z), at(x, y, c, z + 2)
    sibling, partner = at(x, y, 1 - c, z), at(3 - x, y, c, z)
    greet([partner, sibling, xp, xm, yp, ym, y2, zp, zm, z2])
    copies = []

    def go(copy):
        copy.start()
        copies.append(copy)

    sems = (rs, rr)
    do_low, do_high = do_ref.at[pl.ds(0, HALF)], do_ref.at[pl.ds(HALF, HALF)]
    swaps = (
        remote(do_high, dog.at[2 * y + 1], sw_s.at[0], sw_r.at[0], partner),
        remote(stat_ref.at[1], statg.at[2 * y + 1], sw_s.at[1], sw_r.at[1], partner),
    )
    for copy in swaps:
        go(copy)
    dos = RingGather(
        lambda index, half: dog.at[2 * index + half], y, yp, ym, sems, 0,
        lambda half: do_low if half == 0 else dog.at[2 * y + 1],
    )
    dos.own(0)

    def stats_to(upper, rel, peer):
        slot = 2 * y + upper
        source = statg.at[slot] if upper else stat_ref.at[0]
        return remote(source, statg.at[slot], st_s.at[upper, rel - 1], st_r.at[slot], peer)

    y_peers = ((1, yp), (3, ym), (2, y2))
    for rel, peer in y_peers:
        go(stats_to(0, rel, peer))

    cut = (48, WINDOW - 48)

    def window(ref, index, half):
        return rows_at(ref, WINDOW * index + 48 * half, cut[half])

    sides = ((piece_a_ref, full_a, y, yp, ym), (piece_b_ref, full_b, x, xp, xm))
    reduces, gathers = [], []
    for h, (piece, full, me, plus, minus) in enumerate(sides):
        reduces.append(
            RingReduce(
                lambda rel, half, piece=piece, me=me: window(piece, (me + rel) % 4, half),
                lambda half, h=h: winpass.at[h, pl.ds(48 * half, cut[half])],
                lambda side, half, h=h: wingot.at[h, side, pl.ds(48 * half, cut[half])],
                plus, minus, sems, 1 + h,
            )
        )
        gathers.append(
            RingGather(lambda index, half, full=full: window(full, index, half), me, plus, minus, sems, 3 + h)
        )
        reduces[h].start()

    def big_view(core, h, index, half):
        return rows_at(big_ref, ROWS * core + SIDE * h + PIECE * index + half * (PIECE // 2), PIECE // 2)

    owners = ((x, xp, xm), (y, yp, ym))
    pieces = [
        RingGather(
            lambda index, half, h=h: big_view(c, h, index, half), me, plus, minus, sems, 5 + h,
            lambda half, h=h: sides[h][1].at[pl.ds(half * (PIECE // 2), PIECE // 2)],
        )
        for h, (me, plus, minus) in enumerate(owners)
    ]

    def piece_to_sibling(h, index, half, source=None):
        block = big_view(c, h, index, half)
        return remote(block if source is None else source, block, sf_s.at[h, index, half], sf_r.at[h, index, half], sibling)

    def keep(h, half):
        source = sides[h][1].at[pl.ds(half * (PIECE // 2), PIECE // 2)]
        return pltpu.make_async_copy(source, big_view(c, h, owners[h][0], half), own_sem.at[h, half])

    dog[2 * y] = do_ref[0:HALF, :]
    statg[2 * y] = stat_ref[0]
    dqacc[...] = jnp.zeros_like(dqacc)
    for copy in swaps:
        copy.wait_recv()
    dos.own(1)
    for rel, peer in y_peers:
        go(stats_to(1, rel, peer))
    dos.forward()
    dos.near()
    dos.far()
    for upper in range(2):
        for rel, peer in y_peers:
            slot = 2 * ((y + rel) % 4) + upper
            remote(stat_ref.at[0], statg.at[slot], st_s.at[0, 0], st_r.at[slot], sibling).wait_recv()

    def windows_relayed():
        for ring in reduces:
            ring.relay()

    def windows_summed():
        for ring, gather, (piece, full, me, _, _) in zip(reduces, gathers, sides):
            ring.finish()
            for half in range(2):
                total = window(piece, me, half)[...].astype(FULL) + ring.arrived(half)
                window(full, me, half)[...] = total.astype(LOW)
                gather.own(half)

    def windows_forwarded():
        for gather in gathers:
            gather.forward()

    def pieces_sent():
        for h, gather in enumerate(gathers):
            gather.near()
            gather.far()
            for half in range(2):
                pieces[h].own(half)
                source = sides[h][1].at[pl.ds(half * (PIECE // 2), PIECE // 2)]
                go(piece_to_sibling(h, owners[h][0], half, source))
                keep(h, half).start()

    def pieces_forwarded():
        for ring in pieces:
            ring.forward()

    def pieces_near():
        for h, ring in enumerate(pieces):
            ring.near()
            for rel in (1, 3):
                for half in range(2):
                    go(piece_to_sibling(h, (owners[h][0] + rel) % 4, half))

    def pieces_far():
        for h, ring in enumerate(pieces):
            ring.far()
            for half in range(2):
                go(piece_to_sibling(h, (owners[h][0] + 2) % 4, half))

    def tile(i, first_q, slot, first_k, masked):
        queries, out_grads = q_in[i], dog[i]
        lse, delta = statg[i, 0:1, :], statg[i, 1:2, :]
        if masked:
            token = first_q + lax.broadcasted_iota(jnp.int32, (1, HALF), 1)
            begin = begin_of(token, starts_ref)
        dq_part = None
        for n in range(2):
            rows = pl.ds(n * 256, 256)
            keys, values = k_in[slot, rows], v_in[slot, rows]
            scores = lax.dot_general(keys, queries, NT, preferred_element_type=FULL)
            prob_grad = lax.dot_general(values, out_grads, NT, preferred_element_type=FULL)
            soft = jnp.exp(scores - lse)
            if masked:
                key_index = first_k + n * 256 + lax.broadcasted_iota(jnp.int32, (256, 1), 0)
                soft = jnp.where((key_index <= token) & (key_index >= begin), soft, 0.0)
            score_grad = (soft * (prob_grad - delta)).astype(LOW)
            dvacc[rows, :] += jnp.dot(soft.astype(LOW), out_grads, preferred_element_type=FULL)
            dkacc[rows, :] += jnp.dot(score_grad, queries, preferred_element_type=FULL)
            part = jnp.dot(ktbuf[:, n * 256 : (n + 1) * 256], score_grad, preferred_element_type=FULL)
            dq_part = part if dq_part is None else dq_part + part
        dqacc[i] = dqacc[i] + dq_part

    place_of = {2: 0, 1: 1, 3: 2}
    kvs = RingReduce(
        lambda rel, half: kvsrc.at[place_of[rel], half],
        lambda half: kvpass.at[half],
        lambda side, half: kvgot.at[side, half],
        xp, xm, sems, 7,
    )
    between = {
        (0, 0): windows_relayed,
        (0, 1): windows_summed,
        (1, 0): windows_forwarded,
        (1, 1): pieces_sent,
        (2, 1): pieces_forwarded,
        (3, 0): pieces_near,
    }
    for step, rel in enumerate((2, 1, 3, 0)):
        pair = (x + rel) % 4
        for turn in range(2):
            if (step, turn) in between:
                between[step, turn]()
            cc = 1 - c if turn == 0 else c
            slot = pair * 2 + cc
            first_k = 4096 * pair + 1024 * y + BLK * cc
            dkacc[...] = jnp.zeros_like(dkacc)
            dvacc[...] = jnp.zeros_like(dvacc)
            ktbuf[...] = jnp.transpose(k_in[slot])

            def visit(i, carry):
                first_q = tile_first(i, x, c)
                some = first_k <= first_q + (HALF - 1)
                full = (first_k + BLK - 1 <= first_q) & (first_k > 0) & (first_q < 31 * BLK)

                @pl.when(full)
                def _():
                    tile(i, first_q, slot, first_k, False)

                @pl.when(some & jnp.logical_not(full))
                def _():
                    tile(i, first_q, slot, first_k, True)

                return carry

            lax.fori_loop(0, 8, visit, 0)
            to_sibling = remote(sibsend.at[step], sibrecv.at[step], sib_s.at[step], sib_r.at[step], sibling)
            if turn == 0:
                sibsend[step, 0] = dkacc[...].astype(LOW)
                sibsend[step, 1] = dvacc[...].astype(LOW)
                go(to_sibling)
            else:
                to_sibling.wait_recv()
                for half, ref in enumerate((dkacc, dvacc)):
                    both = ref[...] + sibrecv[step, half].astype(FULL)
                    if rel == 0:
                        ref[...] = both
                    else:
                        kvsrc[place_of[rel], half] = both.astype(LOW)
                if rel == 2:
                    kvs.start(0, 1)
                elif rel == 1:
                    kvs.start(3)
                elif rel == 3:
                    kvs.start(2)
                    kvs.relay()

    def cast(i, carry):
        dqsend[i] = jnp.transpose(dqacc[i]).astype(LOW)
        return carry

    lax.fori_loop(0, 8, cast, 0)
    dqs = RingReduce(
        lambda rel, half: dqsend.at[2 * ((y + rel) % 4) + half],
        lambda half: dqpass.at[half],
        lambda side, half: dqgot.at[side, half],
        yp, ym, sems, 8,
    )
    dqs.start()
    kvs.finish()
    zrows = BLK // 4
    for n in range(4):
        for half, ref in enumerate((dkacc, dvacc)):
            rows = pl.ds(n * zrows, zrows)
            whole = ref[rows, :] + kvgot[0, half, rows, :].astype(FULL) + kvgot[1, half, rows, :].astype(FULL)
            zpart[n, half] = whole.astype(LOW)
    zs = RingReduce(
        lambda rel, half: zpart.at[(z + rel) % 4, half],
        lambda half: zpass.at[half],
        lambda side, half: zgot.at[side, half],
        zp, zm, sems, 9,
    )
    zg = RingGather(lambda index, half: dkv_ref.at[index, half], z, zp, zm, sems, 10)
    zs.start()
    dqs.relay()
    zs.relay()
    dqs.finish()
    back = remote(dqback, dqhigh, sw_s.at[2], sw_r.at[2], partner)
    dqback[...] = (dqsend[2 * y + 1].astype(FULL) + dqs.arrived(1)).astype(LOW)
    go(back)

    draws = RingGather(
        lambda index, half: draw_ref.at[pl.ds(half * HALF, HALF), pl.ds(pl.multiple_of(index * HD, HD), HD)],
        z, zp, zm, sems, 11,
    )
    gain = gain_ref[...]
    gain_grad = None
    for half in range(2):
        if half == 0:
            grad = dqsend[2 * y].astype(FULL) + dqs.arrived(0)
        else:
            back.wait_recv()
            grad = dqhigh[...].astype(FULL)
        grad = grad * (HD**-0.5)
        rows = pl.ds(half * HALF, HALF)
        cosine, sine = cos_ref[rows, :], sin_ref[rows, :]
        first, second = grad[:, : HD // 2], grad[:, HD // 2 :]
        turned = jnp.concatenate([first * cosine + second * sine, second * cosine - first * sine], axis=1)
        raw = raw_ref[rows, :]
        inverse = lax.rsqrt(jnp.mean(raw * raw, axis=1, keepdims=True) + EPS)
        unit = raw * inverse
        scaled = gain * turned
        raw_grad = inverse * (scaled - unit * jnp.mean(unit * scaled, axis=1, keepdims=True))
        draw_ref[rows, pl.ds(pl.multiple_of(z * HD, HD), HD)] = raw_grad.astype(LOW)
        draws.own(half)
        part = jnp.sum(unit * turned, axis=0, keepdims=True)
        gain_grad = part if gain_grad is None else gain_grad + part
    gaing[z] = jnp.broadcast_to(gain_grad, (8, HD))
    for n, peer in enumerate((zp, zm, z2)):
        go(remote(gaing.at[z], gaing.at[z], gn_s.at[n], gn_r.at[z], peer))

    zs.finish()
    for half in range(2):
        dkv_ref[z, half] = (zpart[z, half].astype(FULL) + zs.arrived(half)).astype(LOW)
        zg.own(half)
    pieces_far()
    draws.forward()
    zg.forward()
    draws.near()
    zg.near()
    draws.far()
    zg.far()
    for rel in (1, 3, 2):
        other = (z + rel) % 4
        remote(gaing.at[z], gaing.at[other], gn_s.at[0], gn_r.at[other], sibling).wait_recv()
    dgain_ref[...] = sum(gaing[n] for n in range(4))
    for h in range(2):
        for half in range(2):
            keep(h, half).wait()
            for n in range(4):
                piece_to_sibling(h, n, half).wait_recv()
    for ring in [dos, kvs, dqs, zs, zg, draws] + reduces + gathers + pieces:
        ring.drain()
    for copy in copies:
        copy.wait_send()


def backward_attention(
    doc_starts, out_grad, stats, q_all, k_all, v_all, piece_a, piece_b, query_raw, cosine, sine, query_gain
):
    width = piece_a.shape[1]
    return pl.pallas_call(
        attn_backward,
        name="attn_backward",
        out_shape=[
            shape(LOW, BLK, 4 * HD),
            shape(FULL, 8, HD),
            shape(LOW, 4, 2, BLK // 4, HD),
            shape(LOW, 2 * ROWS + 64, width),
        ],
        in_specs=[SMEM] + [VMEM] * 11,
        out_specs=[VMEM] * 3 + [ANY],
        scratch_shapes=[
            vmem(LOW, 8, HALF, HD),
            vmem(FULL, 8, 8, HALF),
            vmem(FULL, 8, HD, HALF),
            vmem(FULL, BLK, HD),
            vmem(FULL, BLK, HD),
            vmem(LOW, HD, BLK),
            vmem(LOW, 4, 2, BLK, HD),
            vmem(LOW, 4, 2, BLK, HD),
            vmem(LOW, 3, 2, BLK, HD),
            vmem(LOW, 2, BLK, HD),
            vmem(LOW, 2, 2, BLK, HD),
            vmem(LOW, 8, HALF, HD),
            vmem(LOW, 2, HALF, HD),
            vmem(LOW, 2, 2, HALF, HD),
            vmem(LOW, HALF, HD),
            vmem(LOW, HALF, HD),
            vmem(LOW, 4, 2, BLK // 4, HD),
            vmem(LOW, 2, BLK // 4, HD),
            vmem(LOW, 2, 2, BLK // 4, HD),
            vmem(FULL, 4, 8, HD),
            vmem(LOW, 2, WINDOW, width),
            vmem(LOW, 2, 2, WINDOW, width),
            vmem(LOW, PIECE, width),
            vmem(LOW, PIECE, width),
            dma(12, 6), dma(12, 6), dma(2, 3), dma(8), dma(3), dma(3), dma(4), dma(4), dma(3), dma(4),
            dma(2, 4, 2), dma(2, 4, 2), dma(2, 2),
        ],
        compiler_params=params(2, 48),
        cost_estimate=cost(15),
    )(doc_starts, out_grad, stats, q_all, k_all, v_all, piece_a, piece_b, query_raw, cosine, sine, query_gain)


def head_sum_kernel(part_ref, out_ref, passing, got, rs, rr):
    x, y, c, z = place()
    zp, zm = at(x, y, c, z + 1), at(x, y, c, z + 3)
    greet([zp, zm])
    rows = part_ref.shape[0] // 4
    zs = RingReduce(
        lambda rel, half: rows_at(part_ref, ((z + rel) % 4) * rows + half * (rows // 2), rows // 2),
        lambda half: passing.at[half],
        lambda side, half: got.at[side, half],
        zp, zm, (rs, rr), 0,
    )
    zg = RingGather(
        lambda index, half: rows_at(out_ref, index * rows + half * (rows // 2), rows // 2),
        z, zp, zm, (rs, rr), 1,
    )
    zs.start()
    zs.relay()
    zs.finish()
    for half in range(2):
        own = pl.ds(pl.multiple_of(z * rows + half * (rows // 2), 16), rows // 2)
        out_ref[own, :] = (part_ref[own, :].astype(FULL) + zs.arrived(half)).astype(LOW)
        zg.own(half)
    zg.forward()
    zg.near()
    zg.far()
    zs.drain()
    zg.drain()


def head_sum(part):
    rows, columns = part.shape
    return pl.pallas_call(
        head_sum_kernel,
        name="head_sum",
        out_shape=shape(LOW, rows, columns),
        in_specs=[VMEM],
        out_specs=VMEM,
        scratch_shapes=[vmem(LOW, 2, rows // 8, columns), vmem(LOW, 2, 2, rows // 8, columns), dma(2, 6), dma(2, 6)],
        compiler_params=params(3, 32),
        cost_estimate=cost(1),
    )(part)


def late_sum_kernel(part_ref, out_ref, core_recv, half, plane_recv, c_ssem, c_rsem, p_ssem, p_rsem, g_ssem, g_rsem, f_ssem, f_rsem):
    x, y, c, z = place()
    sibling = at(x, y, 1 - c, z)
    shifts = [(a, b) for a in range(4) for b in range(4) if (a, b) != (0, 0)]
    peers = [at(x + a, y + b, c, z) for a, b in shifts]
    greet(peers + [sibling])
    first = pl.multiple_of(2 * c, 2)
    copies = []

    def core_copy(m):
        return remote(part_ref.at[2 * (1 - c) + m], core_recv.at[m], c_ssem.at[m], c_rsem.at[m], sibling)

    for m in range(2):
        copies.append(core_copy(m))
        copies[-1].start()
    for m in range(2):
        core_copy(m).wait_recv()

        def add(r, carry):
            both = part_ref[first + m, r].astype(jnp.float32) + core_recv[m, r].astype(jnp.float32)
            half[m * 8 + r] = both.astype(jnp.bfloat16)
            return carry

        lax.fori_loop(0, 8, add, 0)
    me = x * 4 + y
    for n, (a, b) in enumerate(shifts):
        target = ((x + a) % 4) * 4 + (y + b) % 4
        copies.append(remote(half.at[target], plane_recv.at[me], p_ssem.at[n], p_rsem.at[me], peers[n]))
        copies[-1].start()
    total = half[me].astype(jnp.float32)
    for n, (a, b) in enumerate(shifts):
        source = ((x + a) % 4) * 4 + (y + b) % 4
        remote(half.at[0], plane_recv.at[source], p_ssem.at[0], p_rsem.at[source], sibling).wait_recv()
        total = total + plane_recv[source].astype(jnp.float32)

    def piece(owner):
        return out_ref.at[first + owner // 8, owner % 8]

    out_ref[first + me // 8, me % 8] = total.astype(jnp.bfloat16)
    for n in range(15):
        copies.append(remote(piece(me), piece(me), g_ssem.at[n], g_rsem.at[me], peers[n]))
        copies[-1].start()
    copies.append(remote(piece(me), piece(me), f_ssem.at[me], f_rsem.at[me], sibling))
    copies[-1].start()
    for a, b in shifts:
        source = ((x + a) % 4) * 4 + (y + b) % 4
        remote(half.at[0], piece(source), g_ssem.at[0], g_rsem.at[source], sibling).wait_recv()
        copies.append(remote(piece(source), piece(source), f_ssem.at[source], f_rsem.at[source], sibling))
        copies[-1].start()
    for n in range(16):
        theirs = out_ref.at[2 * (1 - c) + n // 8, n % 8]
        remote(half.at[0], theirs, f_ssem.at[0], f_rsem.at[n], sibling).wait_recv()
    for copy in copies:
        copy.wait_send()


def late_sum(part):
    _, _, rows, columns = part.shape
    return pl.pallas_call(
        late_sum_kernel,
        name="late_sum",
        out_shape=shape(LOW, *part.shape),
        in_specs=[VMEM],
        out_specs=VMEM,
        scratch_shapes=[
            vmem(LOW, 2, 8, rows, columns),
            vmem(LOW, 16, rows, columns),
            vmem(LOW, 16, rows, columns),
            dma(2), dma(2), dma(15), dma(16), dma(15), dma(16), dma(16), dma(16),
        ],
        compiler_params=pltpu.CompilerParams(
            collective_id=9, has_side_effects=True, vmem_limit_bytes=40 << 20
        ),
        cost_estimate=pl.CostEstimate(flops=10**8, bytes_accessed=10 * 2**20, transcendentals=0),
    )(part)


def per_device(
    tokens,
    cotangent,
    doc_starts,
    query_weight,
    key_weight,
    value_weight,
    out_weight,
    gate_weight,
    up_weight,
    down_weight,
    input_gain,
    attn_gain,
    prenorm_gain,
    post_gain,
    query_gain,
    key_gain,
):
    row_count = tokens.shape[0]
    first_row = lax.axis_index("seq") * row_count
    own_index = first_row + jnp.arange(row_count, dtype=jnp.int32)
    own_position = doc_layout(doc_starts, own_index)[1]
    cos_table, sine_table = rope_tables(own_position, HD)
    query_scale = HD ** (-0.5)
    inputs = tokens.astype(jnp.float32)
    query_weight_all = lax.all_gather(query_weight, "head", axis=1, tiled=True)
    out_weight_all = lax.all_gather(out_weight, "head", axis=0, tiled=True)
    normed, input_back = jax.vjp(rms_norm, inputs, input_gain)
    normed_low = normed.astype(jnp.bfloat16)
    query_raw = jnp.dot(normed_low, query_weight, preferred_element_type=jnp.float32)
    key_raw = jnp.dot(normed_low, key_weight, preferred_element_type=jnp.float32)
    value_low = jnp.dot(normed_low, value_weight, preferred_element_type=jnp.float32).astype(
        jnp.bfloat16
    )

    def query_piece(source, scaling):
        return rotate(rms_norm(source, scaling), cos_table, sine_table) * query_scale

    def key_piece(source, scaling):
        return rotate(rms_norm(source, scaling), cos_table, sine_table)

    query_rows = query_piece(query_raw, query_gain)
    query_low = query_rows.astype(jnp.bfloat16)
    key_rows, key_back = jax.vjp(key_piece, key_raw, key_gain)
    key_low = key_rows.astype(jnp.bfloat16)
    mix_all, lse_rows, q_all, k_all, v_all = forward_attention(
        doc_starts, query_low, key_low, value_low
    )
    lse_row = lse_rows[:, 0].reshape(-1)
    attn_mix = lax.dynamic_slice_in_dim(mix_all, lax.axis_index("head") * HD, HD, 1)
    attn_out = jnp.dot(mix_all, out_weight_all, preferred_element_type=jnp.float32)
    hidden_state, attn_back = jax.vjp(residual_norm, inputs, attn_out, attn_gain)
    ffn_in, prenorm_back = jax.vjp(rms_norm, hidden_state, prenorm_gain)
    ffn_low = ffn_in.astype(jnp.bfloat16)
    gate_rows = jnp.dot(ffn_low, gate_weight, preferred_element_type=jnp.float32)
    up_rows = jnp.dot(ffn_low, up_weight, preferred_element_type=jnp.float32)
    act_rows, act_back = jax.vjp(gated_act, gate_rows, up_rows)
    act_low = act_rows.astype(jnp.bfloat16)
    ffn_out = head_sum(
        jnp.dot(act_low, down_weight, preferred_element_type=jnp.float32).astype(jnp.bfloat16)
    ).astype(jnp.float32)
    mixed, post_back = jax.vjp(residual_norm, hidden_state, ffn_out, post_gain)
    upstream = cotangent.astype(jnp.float32)
    hidden_grad, ffn_out_grad, post_gain_grad = post_back(upstream)
    ffn_out_low = ffn_out_grad.astype(jnp.bfloat16)
    act_grad = dot_last(ffn_out_low, down_weight)
    gate_grad, up_grad = act_back(act_grad)
    gate_low = gate_grad.astype(jnp.bfloat16)
    up_low = up_grad.astype(jnp.bfloat16)
    ffn_in_sum, piece_a, piece_b, rest = ffn_grads(
        (dot_last(gate_low, gate_weight) + dot_last(up_low, up_weight)).astype(jnp.bfloat16),
        ffn_low,
        ffn_out_low,
        jnp.transpose(gate_low),
        jnp.transpose(up_low),
        jnp.transpose(act_low),
    )
    ffn_in_grad = ffn_in_sum.astype(jnp.float32)
    hidden_more, prenorm_gain_grad = prenorm_back(ffn_in_grad)
    hidden_grad = hidden_grad + hidden_more
    input_grad, attn_out_grad, attn_gain_grad = attn_back(hidden_grad)
    attn_out_low = attn_out_grad.astype(jnp.bfloat16)
    out_weight_grad_t = dot_first(attn_out_low, attn_mix)
    mix_grad = dot_last(attn_out_low, out_weight).astype(jnp.bfloat16)
    delta = jnp.sum(mix_grad.astype(jnp.float32) * attn_mix.astype(jnp.float32), axis=1)
    stats = jnp.stack([lse_row, delta] + [jnp.zeros_like(delta)] * 6)
    stats = jnp.transpose(stats.reshape(8, 2, HALF), (1, 0, 2))
    query_raw_all, query_gain_rows, key_value_grad, big = backward_attention(
        doc_starts,
        mix_grad,
        stats,
        q_all,
        k_all,
        v_all,
        piece_a,
        piece_b,
        query_raw,
        cos_table[:, : HD // 2],
        sine_table[:, : HD // 2],
        query_gain.reshape(1, HD),
    )
    query_gain_part = query_gain_rows[0]
    key_grad = key_value_grad[:, 0].reshape(row_count, HD).astype(jnp.float32)
    value_grad_low = key_value_grad[:, 1].reshape(row_count, HD)
    query_raw_low = lax.dynamic_slice_in_dim(query_raw_all, lax.axis_index("head") * HD, HD, 1)
    query_weight_grad = dot_first(normed_low, query_raw_low)
    key_raw_grad, key_gain_grad = key_back(key_grad)
    key_raw_low = key_raw_grad.astype(jnp.bfloat16)
    key_weight_grad = dot_first(normed_low, key_raw_low)
    value_weight_grad = dot_first(normed_low, value_grad_low)
    normed_grad = (
        dot_last(query_raw_all, query_weight_all)
        + dot_last(key_raw_low, key_weight)
        + dot_last(value_grad_low, value_weight)
    )
    input_more, input_gain_grad = input_back(normed_grad)
    tokens_grad = input_grad + input_more
    width = tokens.shape[1]
    rest_rows = rest.size // HD
    gains = jnp.concatenate(
        [
            input_gain_grad,
            attn_gain_grad,
            prenorm_gain_grad,
            post_gain_grad,
            query_gain_part,
            key_gain_grad,
        ]
    ).astype(jnp.bfloat16)
    gain_rows = gains.size // HD
    extra = jnp.concatenate(
        [
            gains.reshape(gain_rows, HD),
            rest.reshape(rest_rows, HD),
            jnp.zeros((4 * 128 - gain_rows - rest_rows, HD), jnp.bfloat16),
        ]
    ).reshape(4, 128, HD)
    late = jnp.stack(
        [query_weight_grad, key_weight_grad, value_weight_grad, out_weight_grad_t]
    ).astype(jnp.bfloat16)
    late = jnp.concatenate([late, extra], axis=1).reshape(4, 8, (width + 128) // 8, HD)
    late = late_sum(late).reshape(4, width + 128, HD)
    query_weight_grad = late[0, :width].astype(jnp.float32)
    key_weight_grad = late[1, :width].astype(jnp.float32)
    value_weight_grad = late[2, :width].astype(jnp.float32)
    out_weight_grad = jnp.transpose(late[3, :width].astype(jnp.float32))
    extra = late[:, width:].reshape(4 * 128, HD)
    gains = extra[:gain_rows].reshape(-1).astype(jnp.float32)
    rest = extra[gain_rows : gain_rows + rest_rows].reshape(rest.shape)
    input_gain_grad = gains[:width]
    attn_gain_grad = gains[width : 2 * width]
    prenorm_gain_grad = gains[2 * width : 3 * width]
    post_gain_grad = gains[3 * width : 4 * width]
    query_gain_grad = gains[4 * width : 4 * width + HD]
    key_gain_grad = gains[4 * width + HD : 4 * width + 2 * HD]
    hidden = gate_weight.shape[1]
    gate_weight_grad = jnp.transpose(big[:hidden].astype(jnp.float32))
    up_weight_grad = jnp.transpose(big[hidden : 2 * hidden].astype(jnp.float32))
    down_weight_grad = big[2 * hidden :].astype(jnp.float32)
    down_weight_grad = lax.dynamic_update_slice(
        down_weight_grad, rest.astype(jnp.float32), (hidden - rest.shape[0], 0)
    )
    return (
        mixed.astype(jnp.bfloat16),
        tokens_grad,
        query_weight_grad,
        key_weight_grad,
        value_weight_grad,
        out_weight_grad,
        gate_weight_grad,
        up_weight_grad,
        down_weight_grad,
        input_gain_grad,
        attn_gain_grad,
        prenorm_gain_grad,
        post_gain_grad,
        query_gain_grad,
        key_gain_grad,
    )


def solution(mesh):
    placed = (
        P("seq", None),
        P("seq", None),
        P(),
        P(None, "head"),
        P(),
        P(),
        P("head", None),
        P(None, "head"),
        P(None, "head"),
        P("head", None),
        P(),
        P(),
        P(),
        P(),
        P(),
        P(),
    )
    return jax.shard_map(
        per_device,
        mesh=mesh,
        in_specs=placed,
        out_specs=(
            P("seq", None),
            P("seq", None),
            P(None, "head"),
            P(),
            P(),
            P("head", None),
            P(None, "head"),
            P(None, "head"),
            P("head", None),
            P(),
            P(),
            P(),
            P(),
            P(),
            P(),
        ),
        check_vma=False,
    )
```

time: 1370 us -> 426 us (0.31)
  waiting for transfers between devices: 989 us -> 1.38 us
  Pallas kernels: 0 us -> 298 us
  blocking collectives: 132 us -> 0 us
  matrix products: 86.6 us -> 43.6 us
  other arithmetic: 83.9 us -> 43.1 us
  local copies, waits for them, and re-layouts: 45.5 us -> 17.5 us
    reduce_scatter x2 -> x0, waiting for transfers between devices: 619 us -> none  [the longest x1 523 us: per_device(): lax.psum_scatter(key_all_grad.astype(jnp.bfloat16), 'seq', scatter_dimens...]
    pallas_call x0 -> x5, Pallas kernels: none -> 298 us  [the longest x1 107 us: backward_attention(): pl.pallas_call(attn_backward, name='attn_backward', out_shape=[shape(LOW,...]
    psum x5 -> x0, waiting for transfers between devices: 269 us -> none  [the longest x1 137 us: per_device(): lax.psum(jnp.dot(attn_mix, out_weight, preferred_element_type=jnp.float32...]
    psum x2 -> x0, blocking collectives: 132 us -> none  [the longest x1 125 us: per_device(): lax.psum(input_gain_grad.astype(jnp.bfloat16), 'seq').astype(jnp.float32)]
    all_gather x2, waiting for transfers between devices: 100 us -> 0.01 us  [the longest x1 0.01 us: per_device(): out_weight_all = lax.all_gather(out_weight, 'head', axis=0, tiled=True)]
    convert_element_type x17 -> x4, other arithmetic: 44.2 us -> 12.5 us  [the longest x1 11.2 us: per_device(): down_weight_grad = big[2 * hidden:].astype(jnp.float32)]
    dot_general x19 -> x1, matrix products: 29 us -> 3.42 us  [per_device(): jnp.dot(mix_all, out_weight_all, preferred_element_type=jnp.float32)]
    dot_general x7 -> x4, matrix products: 20.6 us -> 5.76 us  [dot_first(): lax.dot_general(left_side, right_side, (((0,), (0,)), ((), ())), preferre...]
  transfers between devices with their start and end apart: 9 -> 2, of which waited for: 8 -> 0; matrix products, arithmetic and copies ran while one was open for 5% -> 14% of each run, Pallas kernels for 0% -> 59%
where the time goes in v2:
time: 426 us; the launch traced here: 419 us
  Pallas kernels  298 us (70%)
  matrix products  43.6 us (10%)
  other arithmetic  43.1 us (10%)
  local copies, waits for them, and re-layouts  17.5 us (4%)
  between operations  15.1 us (4%)
    pallas_call x1, Pallas kernels, backward_attention(): pl.pallas_call(attn_backward, name='attn_backward', out_shape=[shape(LOW,...  107 us
    pallas_call x1, Pallas kernels, forward_attention(): pl.pallas_call(attn_forward, name='attn_forward', out_shape=[shape(LOW, B...  72.3 us
    pallas_call x1, Pallas kernels, late_sum(): pl.pallas_call(late_sum_kernel, name='late_sum', out_shape=shape(LOW, *pa...  49.9 us
    pallas_call x1, Pallas kernels, ffn_grads(): pl.pallas_call(ffn_grads_kernel, name='ffn_grads', out_shape=[shape(LOW,...  45.6 us
    pallas_call x1, Pallas kernels, head_sum(): pl.pallas_call(head_sum_kernel, name='head_sum', out_shape=shape(LOW, row...  23.7 us
    dot_general x7, matrix products, dot_last(): lax.dot_general(left_side, right_side, (((1,), (1,)), ((), ())), preferre...  22.7 us
    unnamed x92, local copies, waits for them, and re-layouts  12.8 us
    convert_element_type x1, other arithmetic, per_device(): down_weight_grad = big[2 * hidden:].astype(jnp.float32)  11.2 us
  transfers between devices with their start and end apart: 2, of which 0 were waited for; matrix products, arithmetic and copies ran while one was open for 14% of the time, Pallas kernels for 59%

profile of v2, /device:TPU:1, one launch (start us, length us, event | category | flops | bytes accessed | tf_op | source)
XLA Modules:
  0.0 418.9 jit_solution(18079847767637333118)
XLA Ops:
  7.3 0.7 all-gather.3.cloned.1.call-update
  8.0 0.7 all-gather.5.cloned.1.call-update
  8.7 1.6 fusion.41
  10.4 1.5 multiply_reduce_fusion.8
  11.9 1.8 multiply_reduce_fusion.7
  14.4 0.8 copy-done.23
  15.2 0.7 slice_negate_fusion.1
  15.9 0.8 slice_negate_fusion.2
  17.6 3.7 fusion.51
  21.3 72.3 %attn_forward.1 = (bf16[512,1024]{1,0:T(8,128)(2,1)S(1)}, f32[2,8,256]{2,1,0:T(8,128)S(1)}, bf16[8,256,256]{2,1,0:T(8,128)(2,1)S(1)}, bf16[8,512,256]{2,1,0:T(8,128)(2,1)S(1)}, bf16[8,512,256]{2,1,0:T(8,128)(2,1)S(1)}) custom-call(s32[7]{0:T(128)S(1)} %copy-done.2, bf16[512,256]{1,0:T(8,128)(2,1)S(1)} %get-tuple-element.74.q_ref, ...), custom_call_target="tpu_custom_call" | custom-call | flops 6000000000 | bytes 20971520 | tf_op jit(solution)/shard_map/attn_forward/pallas_call | solution.py:391
  93.6 1.3 copy-done.5
  94.9 1.3 copy-done.6
  96.2 1.0 copy-done.9
  98.0 3.4 multiply_reduce_fusion.3
  102.1 0.7 copy-done.11
  103.1 1.3 copy-done.41
  104.4 2.5 fusion.95
  107.0 2.5 fusion.96
  109.5 2.8 convolution_convert_fusion.part_ref
  112.3 23.7 %head_sum.1 = bf16[512,1152]{1,0:T(8,128)(2,1)S(1)} custom-call(bf16[512,1152]{1,0:T(8,128)(2,1)S(1)} %convolution_convert_fusion.part_ref), custom_call_target="tpu_custom_call" | custom-call | flops 1000000000 | bytes 20971520 | tf_op jit(solution)/shard_map/head_sum/pallas_call | solution.py:950
  136.3 1.0 fusion.35
  137.9 7.9 %fusion.16 = (bf16[1728,512]{1,0:T(8,128)(2,1)}, bf16[1728,512]{1,0:T(8,128)(2,1)}, bf16[1728,512]{1,0:T(8,128)(2,1)}, f32[512,1728]{0,1:T(8,128)S(1)}) fusion(f32[512,1728]{0,1:T(8,128)S(1)} %fusion.96, f32[512,1728]{0,1:T(8,128)S(1)} %fusion.95, bf16[512,1152]{1,0:T(8,128)(2,1)S(1)} %fusion.36.out_grad_ref, bf16[1728,1152]{1,0:T(8,128)(2,1)S(1)} %copy-done.40), kind=kOutput, calls=%fused_computation.36 | convolution fusion | flops 2061434880 | bytes 21086208 | tf_op jit(solution)/shard_map/dot_general | solution.py:47
  145.8 4.1 fusion.43
  150.0 3.8 fusion.18.part_ref
  153.8 45.6 %ffn_grads.1 = (bf16[512,1152]{1,0:T(8,128)(2,1)}, bf16[320,1152]{1,0:T(8,128)(2,1)}, bf16[320,1152]{1,0:T(8,128)(2,1)}, bf16[64,1152]{1,0:T(8,128)(2,1)}) custom-call(bf16[512,1152]{1,0:T(8,128)(2,1)} %fusion.18.part_ref, bf16[512,1152]{1,0:T(8,128)(2,1)} %copy-done.24, bf16[512,1152]{1,0:T(8,128)(2,1)} %copy-done.25, ...), custom_call_target="tpu_custom_call" | custom-call | flops 6000000000 | bytes 20971520 | tf_op jit(solution)/shard_map/ffn_grads/pallas_call | solution.py:525
  199.4 2.2 fusion.34
  201.7 3.8 multiply_reduce_fusion
  206.0 0.9 copy-done.13
  208.7 106.8 %attn_backward.1 = (bf16[512,1024]{1,0:T(8,128)(2,1)S(1)}, f32[8,256]{1,0:T(8,128)S(1)}, bf16[4,2,128,256]{3,2,1,0:T(8,128)(2,1)S(1)}, bf16[5184,1152]{1,0:T(8,128)(2,1)}) custom-call(s32[7]{0:T(128)S(1)} %copy-done.2, bf16[512,256]{1,0:T(8,128)(2,1)S(1)} %get-tuple-element.91.do_ref, f32[2,8,256]{2,1,0:T(8,128)S(1)} %maximum_bitcast_fusion.stat_ref, ...), custom_call_target="tpu_custom_call" | custom-call | flops 15000000512 | bytes 20971520 | tf_op jit(solution)/shard_map/attn_backward/pallas_call | solution.py:875
  315.6 1.8 convert_multiply_fusion.12
  317.5 1.4 multiply_reduce_fusion.4
  318.9 1.3 fusion.28
  320.3 1.5 fusion.25
  321.8 1.5 fusion.50
  323.3 1.5 fusion.26
  324.8 3.3 fusion.97
  329.4 1.5 fusion.27
  330.9 2.4 fusion.30
  335.1 1.5 pad_maximum_fusion
  336.6 49.9 %late_sum.1 = bf16[4,8,160,256]{3,2,1,0:T(8,128)(2,1)S(1)} custom-call(bf16[4,8,160,256]{3,2,1,0:T(8,128)(2,1)S(1)} %bitcast.115), custom_call_target="tpu_custom_call" | custom-call | flops 100000000 | bytes 10485760 | tf_op jit(solution)/shard_map/late_sum/pallas_call | solution.py:1020
  386.5 2.1 fusion.90
  388.5 0.8 slice_convert_fusion.1
  389.9 11.2 %slice_convert_fusion = (f32[1728,1152]{1,0:T(8,128)}, f32[1152,1728]{0,1:T(8,128)}, f32[1152,1728]{0,1:T(8,128)}) fusion(bf16[5184,1152]{1,0:T(8,128)(2,1)} %get-tuple-element.40), kind=kLoop, calls=%fused_computation.15 | loop fusion | flops 5971968 | bytes 35831808 | tf_op jit(solution)/shard_map/convert_element_type | solution.py:1197
  401.0 1.2 reshape.207
  402.2 2.1 copy.46
  404.4 2.2 convert_bitcast_fusion.2
  407.2 0.7 constant_dynamic-update-slice_fusion
  408.0 3.7 fusion.38
  (138 shorter events, 11.2 us)
Async XLA Ops:
  7.2 9.7 %copy-start = (bf16[1152,256]{1,0:T(8,128)(2,1)S(1)}, bf16[1152,256]{1,0:T(8,128)(2,1)}, u32[]{:S(2)}) copy-start(bf16[1152,256]{1,0:T(8,128)(2,1)} %param.21) | copy-start | bytes 1769476
  7.2 3.1 copy-start.30
  7.2 3.1 copy-start.15
  7.2 3.1 copy-start.37
  7.2 90.7 %all-gather.3.cloned.1.call-start = ((), (), s32[]{:S(2)}) async-start(), calls=%async_computation | async-start | bytes 2949120 | tf_op jit(solution)/shard_map/all_gather | solution.py:1065
  8.0 316.8 %all-gather.5.cloned.1.call-start = ((), (), s32[]{:S(2)}) async-start(), calls=%async_computation.1 | async-start | bytes 2949120 | tf_op jit(solution)/shard_map/all_gather | solution.py:1064
  11.8 2.1 copy-start.32
  11.8 2.3 copy-start.1
  11.9 2.3 copy-start.38
  14.1 2.6 copy-start.2
  14.4 0.8 copy-start.23
  14.4 1.5 copy-start.22
  93.6 1.3 copy-start.5
  94.9 1.3 copy-start.6
  96.2 1.0 copy-start.9
  98.0 3.5 copy-start.16
  98.0 3.5 copy-start.36
  101.4 1.4 copy-start.11
  101.4 1.4 copy-start.34
  101.5 3.0 copy-start.41
  104.4 2.5 copy-start.24
  104.4 2.6 copy-start.42
  107.0 2.5 copy-start.40
  112.3 24.0 %copy-start.20 = (bf16[512,1152]{1,0:T(8,128)(2,1)S(1)}, bf16[512,1152]{1,0:T(8,128)(2,1)}, u32[]{:S(2)}) copy-start(bf16[512,1152]{1,0:T(8,128)(2,1)} %param.17) | copy-start | bytes 3538948
  112.3 24.0 %copy-start.35 = (f32[1152]{0:T(1024)S(1)}, f32[1152]{0:T(1024)}, u32[]{:S(2)}) copy-start(f32[1152]{0:T(1024)} %param.29) | copy-start | bytes 13828
  137.9 7.9 %copy-start.25 = (bf16[512,1152]{1,0:T(8,128)(2,1)}, bf16[512,1152]{1,0:T(8,128)(2,1)S(1)}, u32[]{:S(2)}) copy-start(bf16[512,1152]{1,0:T(8,128)(2,1)S(1)} %fusion.36.out_grad_ref) | copy-start | bytes 3538948
  199.4 2.2 copy-start.12
  199.4 2.3 copy-start.21
  205.5 1.4 copy-start.13
  205.5 1.5 copy-start.29
  207.1 0.7 copy-start.39
  207.1 1.1 copy-start.7
  207.1 1.3 copy-start.8
  207.1 1.7 copy-start.10
  315.6 4.7 %copy-start.3 = (bf16[512,1024]{1,0:T(8,128)(2,1)}, bf16[512,1024]{1,0:T(8,128)(2,1)S(1)}, u32[]{:S(2)}) copy-start(bf16[512,1024]{1,0:T(8,128)(2,1)S(1)} %get-tuple-element.36) | copy-start | bytes 3145732
  317.5 2.8 copy-start.17
  321.8 3.0 copy-start.4
  324.8 3.3 copy-start.31
  328.1 1.3 copy-start.18
  330.8 3.9 copy-start.33
  330.8 4.2 %copy-start.26 = (bf16[1,1152,256]{2,1,0:T(8,128)(2,1)S(1)}, bf16[1,1152,256]{2,1,0:T(8,128)(2,1)}, u32[]{:S(2)}) copy-start(bf16[1,1152,256]{2,1,0:T(8,128)(2,1)} %fusion.28) | copy-start | bytes 1769476
  330.8 4.2 %copy-start.27 = (bf16[1,1152,256]{2,1,0:T(8,128)(2,1)S(1)}, bf16[1,1152,256]{2,1,0:T(8,128)(2,1)}, u32[]{:S(2)}) copy-start(bf16[1,1152,256]{2,1,0:T(8,128)(2,1)} %fusion.25) | copy-start | bytes 1769476
  330.9 4.2 %copy-start.28 = (bf16[1,1152,256]{2,1,0:T(8,128)(2,1)S(1)}, bf16[1,1152,256]{2,1,0:T(8,128)(2,1)}, u32[]{:S(2)}) copy-start(bf16[1,1152,256]{2,1,0:T(8,128)(2,1)} %fusion.26) | copy-start | bytes 1769476
  401.0 6.9 %copy-start.14 = (f32[512,1152]{1,0:T(8,128)S(1)}, f32[512,1152]{1,0:T(8,128)}, u32[]{:S(2)}) copy-start(f32[512,1152]{1,0:T(8,128)} %copy-done.13) | copy-start | bytes 7077892
  404.4 3.6 copy-start.19
Sparse Core Ops, SparseCore 0:
  9.7 36.4 all-gather.2
  47.9 37.8 all-gather.4

commit v3 on v2

--- a/solution.py
+++ b/solution.py
@@ -41,26 +41,6 @@
     half_width = values.shape[-1] // 2
     turned = jnp.concatenate([-values[..., half_width:], values[..., :half_width]], axis=-1)
     return values * cos_table + turned * sine_table
-
-
-def dot_last(left_side, right_side):
-    return lax.dot_general(
-        left_side, right_side, (((1,), (1,)), ((), ())), preferred_element_type=jnp.float32
-    )
-
-
-def dot_first(left_side, right_side):
-    return lax.dot_general(
-        left_side, right_side, (((0,), (0,)), ((), ())), preferred_element_type=jnp.float32
-    )
-
-
-def residual_norm(residual, branch, scaling):
-    return residual + rms_norm(branch, scaling)
-
-
-def gated_act(gate_vals, up_vals):
-    return jax.nn.gelu(gate_vals, approximate=True) * up_vals
 
 
 MESH_ID = pl.DeviceIdType.MESH
@@ -424,144 +404,341 @@
 CUTS = (0, 448, 896, 1280, 1728, 2144, 2560)
 
 
-def ffn_grads_kernel(
-    part_ref, ffn_ref, out_grad_ref, gate_ref, up_ref, act_ref,
-    sum_ref, piece_a_ref, piece_b_ref, rest_ref,
-    left, right, sib_send, sib_recv, mine, pass_ab, got_ab, z_pass, z_got,
+BLOCKS = ((0, 384), (384, 384), (768, 384), (1152, 384), (1536, 192))
+THIRD = 384
+CORNER = 0.7978845608028654
+
+
+def unit_of(values):
+    inverse = lax.rsqrt(jnp.mean(values * values, axis=1, keepdims=True) + EPS)
+    return inverse, values * inverse
+
+
+def norm_back(inverse, unit, scaled):
+    return inverse * (scaled - unit * jnp.mean(unit * scaled, axis=1, keepdims=True))
+
+
+def middle_kernel(
+    again_ref, pgain_ref, fgain_ref, lse_ref,
+    mix_hbm, wout_hbm, tokens_hbm, cot_hbm, gate_hbm, up_hbm, down_hbm,
+    mixed_ref, mgrad_ref, stat_ref, resid_ref, early_ref, piece_a_ref, piece_b_ref,
+    weights, wout, mix, tokens, cot, attn_out, left, right, turned, turned_up, aol,
+    part_f, part_b, sum_f, sum_b, z_pass, z_got, sib_recv, pass_ab, got_ab, grows,
     in_sem, sib_s, sib_r, rs, rr,
 ):
     x, y, c, z = place()
     xp, xm, yp, ym = at(x + 1, y, c, z), at(x + 3, y, c, z), at(x, y + 1, c, z), at(x, y + 3, c, z)
     zp, zm, sibling = at(x, y, c, z + 1), at(x, y, c, z + 3), at(x, y, 1 - c, z)
-    hidden = gate_ref.shape[0]
-    loads = [pltpu.make_async_copy(out_grad_ref, right.at[1], in_sem.at[0])]
-    loads.append(pltpu.make_async_copy(ffn_ref, right.at[0], in_sem.at[1]))
-    for n, ref in enumerate((gate_ref, up_ref, act_ref)):
-        loads.append(pltpu.make_async_copy(ref, left.at[pl.ds(n * hidden, hidden)], in_sem.at[2 + n]))
+    hidden = gate_hbm.shape[0]
+    width = weights.shape[1]
+    loads = [
+        pltpu.make_async_copy(src, dst, in_sem.at[n])
+        for n, (src, dst) in enumerate(
+            (
+                (mix_hbm, mix),
+                (wout_hbm, wout),
+                (tokens_hbm, tokens),
+                (gate_hbm, weights.at[pl.ds(0, hidden)]),
+                (up_hbm, weights.at[pl.ds(hidden, hidden)]),
+                (down_hbm, weights.at[pl.ds(2 * hidden, hidden)]),
+                (cot_hbm, cot),
+            )
+        )
+    ]
     for load in loads:
         load.start()
     greet([xp, xm, yp, ym, zp, zm, sibling])
-    rows = part_ref.shape[0] // 4
-
-    zs = RingReduce(
-        lambda rel, half: rows_at(part_ref, ((z + rel) % 4) * rows + half * (rows // 2), rows // 2),
-        lambda half: z_pass.at[half],
-        lambda side, half: z_got.at[side, half],
-        zp, zm, (rs, rr), 0,
-    )
-    zg = RingGather(
-        lambda index, half: rows_at(sum_ref, index * rows + half * (rows // 2), rows // 2),
-        z, zp, zm, (rs, rr), 1,
-    )
-    zs.start()
-    for load in loads:
-        load.wait()
+    sems = (rs, rr)
+    thirds = [pl.ds(k * THIRD, THIRD) for k in range(width // THIRD)]
+
+    def rows_of(r):
+        return pl.ds(r * HALF, HALF)
+
+    def head_sum(r, number, part, whole):
+        quarter = HALF // 4
+        first = r * HALF
+
+        def span(ref, index, half):
+            return rows_at(ref, first + quarter * index + half * (quarter // 2), quarter // 2)
+
+        reduce = RingReduce(
+            lambda rel, half: span(part, (z + rel) % 4, half),
+            lambda half: z_pass.at[number, half],
+            lambda side, half: z_got.at[number, side, half],
+            zp, zm, sems, 2 * number,
+        )
+        gather = RingGather(lambda index, half: span(whole, index, half), z, zp, zm, sems, 2 * number + 1)
+
+        def summed():
+            reduce.finish()
+            for half in range(2):
+                own = span(part, z, half)[...].astype(FULL) + reduce.arrived(half)
+                span(whole, z, half)[...] = own.astype(LOW)
+                gather.own(half)
+
+        def gathered():
+            gather.near()
+            gather.far()
+
+        return reduce, gather, summed, gathered
+
+    sums = [head_sum(0, 0, part_f, sum_f), head_sum(1, 1, part_f, sum_f)]
+    sums += [head_sum(0, 2, part_b, sum_b), head_sum(1, 3, part_b, sum_b)]
+
+    def forward(r, hooks):
+        rows, columns = rows_of(r), pl.ds(r * HALF, HALF)
+        if r == 0:
+            for load in loads[:3]:
+                load.wait()
+        for third in thirds:
+            attn_out[rows, third] = jnp.dot(mix[rows, :], wout[:, third], preferred_element_type=FULL)
+        _, unit = unit_of(attn_out[rows, :])
+        state = tokens[rows, :].astype(FULL) + unit * again_ref[...]
+        resid_ref[rows, :] = state
+        _, unit = unit_of(state)
+        right[0, rows, :] = (unit * pgain_ref[...]).astype(LOW)
+        if r == 0:
+            for load in loads[3:5]:
+                load.wait()
+        for n, (start, size) in enumerate(BLOCKS):
+            low = right[0, rows, :]
+            gate = lax.dot_general(weights[pl.ds(start, size), :], low, NT, preferred_element_type=FULL)
+            up = lax.dot_general(weights[pl.ds(hidden + start, size), :], low, NT, preferred_element_type=FULL)
+            square = gate * gate
+            bend = jnp.tanh(CORNER * gate * (1.0 + 0.044715 * square))
+            share = 0.5 * (1.0 + bend)
+            gelu = gate * share
+            slope = share + 0.5 * gate * (1.0 - bend * bend) * (CORNER * (1.0 + 3.0 * 0.044715 * square))
+            act = (gelu * up).astype(LOW)
+            left[pl.ds(start, size), columns] = (up * slope).astype(LOW)
+            left[pl.ds(hidden + start, size), columns] = gelu.astype(LOW)
+            left[pl.ds(2 * hidden + start, size), columns] = act
+            turned[:, start : start + size] = jnp.transpose(act)
+            if n in hooks:
+                hooks[n]()
+        if r == 0:
+            loads[5].wait()
+        for third in thirds:
+            part = jnp.dot(
+                turned[:, :hidden], weights[pl.ds(2 * hidden, hidden), third], preferred_element_type=FULL
+            )
+            part_f[rows, third] = part.astype(LOW)
+
+    def backward(r, hooks):
+        rows, columns = rows_of(r), pl.ds(r * HALF, HALF)
+        if r == 0:
+            loads[6].wait()
+        inverse, unit = unit_of(sum_f[rows, :].astype(FULL))
+        mixed_ref[rows, :] = (resid_ref[rows, :] + unit * fgain_ref[...]).astype(LOW)
+        grad = cot[rows, :].astype(FULL)
+        grows[2, r : r + 1, :] = jnp.sum(unit * grad, axis=0, keepdims=True)
+        right[1, rows, :] = norm_back(inverse, unit, fgain_ref[...] * grad).astype(LOW)
+        for n, (start, size) in enumerate(BLOCKS):
+            act_grad = lax.dot_general(
+                weights[pl.ds(2 * hidden + start, size), :], right[1, rows, :], NT, preferred_element_type=FULL
+            )
+            for first, turn in ((start, turned), (hidden + start, turned_up)):
+                span = pl.ds(first, size)
+                grads = (act_grad * left[span, columns].astype(FULL)).astype(LOW)
+                left[span, columns] = grads
+                turn[:, start : start + size] = jnp.transpose(grads)
+            if n in hooks:
+                hooks[n]()
+        for third in thirds:
+            part = jnp.dot(turned[:, :hidden], weights[pl.ds(0, hidden), third], preferred_element_type=FULL)
+            part = part + jnp.dot(
+                turned_up[:, :hidden], weights[pl.ds(hidden, hidden), third], preferred_element_type=FULL
+            )
+            part_b[rows, third] = part.astype(LOW)
+
+    own_head = pl.ds(pl.multiple_of(z * HD, HD), HD)
+
+    def finish(r):
+        rows = rows_of(r)
+        grad = sum_b[rows, :].astype(FULL)
+        inverse, unit = unit_of(resid_ref[rows, :])
+        grows[1, r : r + 1, :] = jnp.sum(unit * grad, axis=0, keepdims=True)
+        grad = cot[rows, :].astype(FULL) + norm_back(inverse, unit, pgain_ref[...] * grad)
+        resid_ref[rows, :] = grad
+        inverse, unit = unit_of(attn_out[rows, :])
+        grows[0, r : r + 1, :] = jnp.sum(unit * grad, axis=0, keepdims=True)
+        aol[rows, :] = norm_back(inverse, unit, again_ref[...] * grad).astype(LOW)
+        grads = lax.dot_general(aol[rows, :], wout[own_head, :], NT, preferred_element_type=FULL).astype(LOW)
+        mgrad_ref[rows, :] = grads
+        products = grads.astype(FULL) * mix[rows, own_head].astype(FULL)
+        delta = jnp.sum(jnp.transpose(products), axis=0, keepdims=True)
+        number = lax.broadcasted_iota(jnp.int32, (8, HALF), 0)
+        stat_ref[r] = jnp.where(number == 1, delta, lse_ref[r])
+
+    sib_send, mine = weights.at[pl.ds(0, ROWS)], weights.at[pl.ds(ROWS, ROWS)]
 
     def product(core, n, target, added):
         first, size = CUTS[n], CUTS[n + 1] - CUTS[n]
         lhs = left[pl.ds(pl.multiple_of(ROWS * core + first, 16), size), :]
         which = jnp.where(n >= 2, core, 0)
-        width = right.shape[2] // 3
-        for k in range(3):
-            columns = pl.ds(k * width, width)
-            tile = jnp.dot(lhs, right[which, :, columns], preferred_element_type=FULL)
+        for third in thirds:
+            tile = jnp.dot(lhs, right[which, :, third], preferred_element_type=FULL)
             if added is not None:
-                tile = tile + added[pl.ds(first, size), columns].astype(FULL)
-            target[pl.ds(first, size), columns] = tile.astype(LOW)
+                tile = tile + added[pl.ds(first, size), third].astype(FULL)
+            target[pl.ds(first, size), third] = tile.astype(LOW)
 
     def to_sibling(n):
         span = pl.ds(CUTS[n], CUTS[n + 1] - CUTS[n])
         return remote(sib_send.at[span], sib_recv.at[span], sib_s.at[n], sib_r.at[n], sibling)
 
+    def side_ring(h, me, plus, minus):
+        return RingReduce(
+            lambda rel, half: rows_at(
+                weights, ROWS + SIDE * h + PIECE * ((me + rel) % 4) + half * (PIECE // 2), PIECE // 2
+            ),
+            lambda half: pass_ab.at[h, half],
+            lambda side, half: got_ab.at[h, side, half],
+            plus, minus, sems, 8 + h,
+        )
+
+    rings = (side_ring(0, x, xp, xm), side_ring(1, y, yp, ym))
+    forward(0, {})
+    sums[0][0].start()
+    forward(1, {3: sums[0][0].relay})
+    sums[0][2]()
+    sums[1][0].start()
+    sums[0][1].forward()
+    sums[1][0].relay()
+    sums[0][3]()
+    backward(0, {1: sums[1][2], 4: sums[1][1].forward})
+    sums[2][0].start()
+    sums[1][3]()
+    backward(1, {2: sums[2][0].relay, 4: sums[2][2]})
+    sums[3][0].start()
+    rest = jnp.dot(left[2 * ROWS :, :], right[1], preferred_element_type=FULL)
+    early_ref[pl.ds(HD, 64), :] = rest.astype(LOW)
     count = len(CUTS) - 1
     for n in range(count):
         product(1 - c, n, sib_send, None)
         to_sibling(n).start()
-        if n == count // 2 - 1:
-            zs.relay()
-    zs.finish()
-    for half in range(2):
-        own = pl.ds(pl.multiple_of(z * rows + half * (rows // 2), 16), rows // 2)
-        sum_ref[own, :] = (part_ref[own, :].astype(FULL) + zs.arrived(half)).astype(LOW)
-        zg.own(half)
-
-    def side_ring(h, me, plus, minus):
-        return RingReduce(
-            lambda rel, half: rows_at(mine, SIDE * h + PIECE * ((me + rel) % 4) + half * (PIECE // 2), PIECE // 2),
-            lambda half: pass_ab.at[h, half],
-            lambda side, half: got_ab.at[h, side, half],
-            plus, minus, (rs, rr), 2 + h,
-        )
-
-    rings = (side_ring(0, x, xp, xm), side_ring(1, y, yp, ym))
+        if n == 0:
+            sums[2][1].forward()
+            sums[3][0].relay()
+        if n == 2:
+            sums[3][2]()
+    sums[2][3]()
     for n in range(count):
         to_sibling(n).wait_recv()
         product(c, n, mine, sib_recv)
+        if n == 0:
+            sums[3][1].forward()
         if n == count // 2 - 1:
             rings[0].start()
-            zg.forward()
     rings[1].start()
-    rest = jnp.dot(left[2 * ROWS :, :], right[1], preferred_element_type=FULL)
-    rest_ref[...] = rest.astype(LOW)
-    for ring in rings:
-        ring.relay()
-    zg.near()
-    zg.far()
+    finish(0)
+    sums[3][3]()
+    rings[0].relay()
+    finish(1)
+    rings[1].relay()
+    lhs = jnp.transpose(mix[:, own_head])
+    for third in thirds:
+        early_ref[0:HD, third] = jnp.dot(lhs, aol[:, third], preferred_element_type=FULL).astype(LOW)
+    number = lax.broadcasted_iota(jnp.int32, (32, width), 0)
+    gains = jnp.zeros((32, width), FULL)
+    for n in range(3):
+        gains = jnp.where(number == n, grows[n, 0:1, :] + grows[n, 1:2, :], gains)
+    early_ref[pl.ds(HD + 64, 32), :] = gains.astype(LOW)
     for h, (ring, me, out) in enumerate(((rings[0], x, piece_a_ref), (rings[1], y, piece_b_ref))):
         ring.finish()
         for half in range(2):
             size = PIECE // 2
-            own = mine[pl.ds(pl.multiple_of(SIDE * h + PIECE * me + half * size, 16), size), :]
+            own = rows_at(weights, ROWS + SIDE * h + PIECE * me + half * size, size)[...]
             out[pl.ds(half * size, size), :] = (own.astype(FULL) + ring.arrived(half)).astype(LOW)
-    for ring in (zs, zg) + rings:
+    for reduce, gather, _, _ in sums:
+        reduce.drain()
+        gather.drain()
+    for ring in rings:
         ring.drain()
     for n in range(count):
         to_sibling(n).wait_send()
 
 
-def ffn_grads(part, ffn_low, ffn_out_low, gate_t, up_t, act_t):
-    rows, width = part.shape
+def middle(again, pgain, fgain, lse, mix, wout, tokens, cot, gate_t, up_t, down):
+    rows, width = tokens.shape
     hidden = gate_t.shape[0]
+    stacked = 3 * hidden
     return pl.pallas_call(
-        ffn_grads_kernel,
-        name="ffn_grads",
+        middle_kernel,
+        name="middle",
         out_shape=[
             shape(LOW, rows, width),
+            shape(LOW, rows, HD),
+            shape(FULL, 2, 8, HALF),
+            shape(FULL, rows, width),
+            shape(LOW, HD + 96, width),
             shape(LOW, PIECE, width),
             shape(LOW, PIECE, width),
-            shape(LOW, 3 * hidden - 2 * ROWS, width),
         ],
-        in_specs=[VMEM] + [ANY] * 5,
-        out_specs=[VMEM] * 4,
+        in_specs=[VMEM] * 4 + [ANY] * 7,
+        out_specs=[VMEM] * 7,
         scratch_shapes=[
-            vmem(LOW, 3 * hidden, rows),
+            vmem(LOW, stacked, width),
+            vmem(LOW, 4 * HD, width),
+            vmem(LOW, rows, 4 * HD),
+            vmem(LOW, rows, width),
+            vmem(LOW, rows, width),
+            vmem(FULL, rows, width),
+            vmem(LOW, stacked, rows),
             vmem(LOW, 2, rows, width),
-            vmem(LOW, ROWS, width),
-            vmem(LOW, ROWS, width),
+            vmem(LOW, HALF, 1792),
+            vmem(LOW, HALF, 1792),
+            vmem(LOW, rows, width),
+            *[vmem(LOW, rows, width)] * 4,
+            vmem(LOW, 4, 2, HALF // 8, width),
+            vmem(LOW, 4, 2, 2, HALF // 8, width),
             vmem(LOW, ROWS, width),
             vmem(LOW, 2, 2, PIECE // 2, width),
             vmem(LOW, 2, 2, 2, PIECE // 2, width),
-            vmem(LOW, 2, rows // 8, width),
-            vmem(LOW, 2, 2, rows // 8, width),
-            dma(5), dma(6), dma(6), dma(4, 6), dma(4, 6),
+            vmem(FULL, 3, 8, width),
+            dma(7), dma(6), dma(6), dma(10, 6), dma(10, 6),
         ],
-        compiler_params=params(4, 56),
-        cost_estimate=cost(6),
-    )(part, ffn_low, ffn_out_low, gate_t, up_t, act_t)
+        compiler_params=params(4, 60),
+        cost_estimate=cost(20),
+    )(again, pgain, fgain, lse, mix, wout, tokens, cot, gate_t, up_t, down)
+
+
+LATE = 112
+EARLY = 176
+KEEPERS = 11
 
 
 def attn_backward(
-    starts_ref, do_ref, stat_ref, q_in, k_in, v_in, piece_a_ref, piece_b_ref, raw_ref, cos_ref, sin_ref, gain_ref,
-    draw_ref, dgain_ref, dkv_ref, big_ref,
+    starts_ref, do_ref, stat_ref, piece_a_ref, piece_b_ref, qgain_ref, kgain_ref, igain_ref, early_ref,
+    q_hbm, k_hbm, v_hbm, raw_hbm, kraw_hbm, cos_hbm, sin_hbm, wk_hbm, wv_hbm, normed_hbm, wq_hbm, tokens_hbm, resid_hbm,
+    late_ref, esum_ref, tgrad_ref, dgain_ref, big_ref,
     dog, statg, dqacc, dkacc, dvacc, ktbuf, sibsend, sibrecv, kvsrc, kvpass, kvgot,
     dqsend, dqpass, dqgot, dqback, dqhigh, zpart, zpass, zgot, gaing, winpass, wingot, full_a, full_b,
+    draw_ref, dkv_ref, dkraw, dvrow, part, core_recv, half_sum, plane_recv, grow, grecv,
+    e_core, e_half, e_plane,
+    q_in, k_in, v_in, raw_ref, kraw_ref, cos_ref, sin_ref, wk_ref, wv_ref, normed_t, wq_ref, tok_ref, resid_ref,
     rs, rr, st_s, st_r, sw_s, sw_r, sib_s, sib_r, gn_s, gn_r, sf_s, sf_r, own_sem,
+    load_sem, c_s, c_r, p_s, p_r, g_s, g_r, f_s, f_r, i_s, i_r,
+    ep_s, ep_r, eg_s, eg_r, ef_s, ef_r,
 ):
     x, y, c, z = place()
     xp, xm, yp, ym = at(x + 1, y, c, z), at(x + 3, y, c, z), at(x, y + 1, c, z), at(x, y + 3, c, z)
     zp, zm, y2, z2 = at(x, y, c, z + 1), at(x, y, c, z + 3), at(x, y + 2, c, z), at(x, y, c, z + 2)
     sibling, partner = at(x, y, 1 - c, z), at(3 - x, y, c, z)
-    greet([partner, sibling, xp, xm, yp, ym, y2, zp, zm, z2])
+    shifts = [(a, b) for a in range(4) for b in range(4) if (a, b) != (0, 0)]
+    plane = [at(x + a, y + b, c, z) for a, b in shifts]
+    loads = [
+        pltpu.make_async_copy(src, dst, load_sem.at[n])
+        for n, (src, dst) in enumerate(
+            (
+                (q_hbm, q_in), (k_hbm, k_in), (v_hbm, v_in), (raw_hbm, raw_ref), (kraw_hbm, kraw_ref),
+                (cos_hbm, cos_ref), (sin_hbm, sin_ref), (wk_hbm, wk_ref), (wv_hbm, wv_ref),
+                (normed_hbm, normed_t), (wq_hbm, wq_ref), (tokens_hbm, tok_ref), (resid_hbm, resid_ref),
+            )
+        )
+    ]
+    for load in loads:
+        load.start()
+    greet(plane + [sibling, zp, zm, z2])
     copies = []
 
     def go(copy):
@@ -581,6 +758,67 @@
         lambda half: do_low if half == 0 else dog.at[2 * y + 1],
     )
     dos.own(0)
+    chip = x * 4 + y
+    e_cross = remote(rows_at(early_ref, EARLY * (1 - c), EARLY), e_core, c_s.at[1], c_r.at[1], sibling)
+    go(e_cross)
+
+    def early_part(owner):
+        return remote(
+            rows_at(e_half, 16 * owner, 16), e_plane.at[chip], ep_s.at[owner], ep_r.at[chip],
+            at(owner // 4, owner % 4, c, z),
+        )
+
+    def early_spread():
+        e_cross.wait_recv()
+        own = early_ref[pl.ds(pl.multiple_of(EARLY * c, 16), EARLY), :]
+        e_half[...] = (own.astype(FULL) + e_core[...].astype(FULL)).astype(LOW)
+        for owner in range(KEEPERS):
+            pl.when(chip != owner)(early_part(owner).start)
+
+    def early_piece(core, owner):
+        return rows_at(esum_ref, EARLY * core + 16 * owner, 16)
+
+    def early_out(n):
+        return remote(early_piece(c, chip), early_piece(c, chip), eg_s.at[n], eg_r.at[chip], plane[n])
+
+    def early_across(owner):
+        block = early_piece(c, owner)
+        return remote(block, block, ef_s.at[owner], ef_r.at[owner], sibling)
+
+    def early_summed():
+        @pl.when(chip < KEEPERS)
+        def _():
+            total = rows_at(e_half, 16 * chip, 16)[...].astype(FULL)
+            for a, b in shifts:
+                source = ((x + a) % 4) * 4 + (y + b) % 4
+                block = rows_at(e_half, 0, 16)
+                remote(block, e_plane.at[source], ep_s.at[0], ep_r.at[source], sibling).wait_recv()
+                total = total + e_plane[source].astype(FULL)
+            early_piece(c, chip)[...] = total.astype(LOW)
+            for n in range(15):
+                early_out(n).start()
+            early_across(chip).start()
+
+    def early_passed():
+        for owner in range(KEEPERS):
+
+            @pl.when(chip != owner)
+            def _():
+                block = early_piece(c, owner)
+                remote(rows_at(e_half, 0, 16), block, eg_s.at[0], eg_r.at[owner], sibling).wait_recv()
+                early_across(owner).start()
+
+    def early_done():
+        for owner in range(KEEPERS):
+            block = early_piece(1 - c, owner)
+            remote(rows_at(e_half, 0, 16), block, ef_s.at[0], ef_r.at[owner], sibling).wait_recv()
+            early_across(owner).wait_send()
+            pl.when(chip != owner)(early_part(owner).wait_send)
+
+        @pl.when(chip < KEEPERS)
+        def _():
+            for n in range(15):
+                early_out(n).wait_send()
 
     def stats_to(upper, rel, peer):
         slot = 2 * y + upper
@@ -649,6 +887,9 @@
             remote(stat_ref.at[0], statg.at[slot], st_s.at[0, 0], st_r.at[slot], sibling).wait_recv()
 
     def windows_relayed():
+        for load in loads[:3]:
+            load.wait()
+        early_spread()
         for ring in reduces:
             ring.relay()
 
@@ -661,35 +902,33 @@
                 gather.own(half)
 
     def windows_forwarded():
+        early_summed()
         for gather in gathers:
             gather.forward()
 
-    def pieces_sent():
-        for h, gather in enumerate(gathers):
+    def pieces_sent(h):
+        for half in range(2):
+            pieces[h].own(half)
+            source = sides[h][1].at[pl.ds(half * (PIECE // 2), PIECE // 2)]
+            go(piece_to_sibling(h, owners[h][0], half, source))
+            keep(h, half).start()
+
+    def windows_gathered():
+        for gather in gathers:
             gather.near()
             gather.far()
+        pieces_sent(1)
+
+    def pieces_near(h):
+        pieces[h].near()
+        for rel in (1, 3):
             for half in range(2):
-                pieces[h].own(half)
-                source = sides[h][1].at[pl.ds(half * (PIECE // 2), PIECE // 2)]
-                go(piece_to_sibling(h, owners[h][0], half, source))
-                keep(h, half).start()
-
-    def pieces_forwarded():
-        for ring in pieces:
-            ring.forward()
-
-    def pieces_near():
-        for h, ring in enumerate(pieces):
-            ring.near()
-            for rel in (1, 3):
-                for half in range(2):
-                    go(piece_to_sibling(h, (owners[h][0] + rel) % 4, half))
-
-    def pieces_far():
-        for h, ring in enumerate(pieces):
-            ring.far()
-            for half in range(2):
-                go(piece_to_sibling(h, (owners[h][0] + 2) % 4, half))
+                go(piece_to_sibling(h, (owners[h][0] + rel) % 4, half))
+
+    def pieces_far(h):
+        pieces[h].far()
+        for half in range(2):
+            go(piece_to_sibling(h, (owners[h][0] + 2) % 4, half))
 
     def tile(i, first_q, slot, first_k, masked):
         queries, out_grads = q_in[i], dog[i]
@@ -725,9 +964,11 @@
         (0, 0): windows_relayed,
         (0, 1): windows_summed,
         (1, 0): windows_forwarded,
-        (1, 1): pieces_sent,
-        (2, 1): pieces_forwarded,
-        (3, 0): pieces_near,
+        (1, 1): windows_gathered,
+        (2, 1): pieces[1].forward,
+        (2, 0): early_passed,
+        (3, 0): lambda: pieces_sent(0),
+        (3, 1): lambda: pieces_near(1),
     }
     for step, rel in enumerate((2, 1, 3, 0)):
         pair = (x + rel) % 4
@@ -778,18 +1019,6 @@
                     kvs.start(2)
                     kvs.relay()
 
-    def cast(i, carry):
-        dqsend[i] = jnp.transpose(dqacc[i]).astype(LOW)
-        return carry
-
-    lax.fori_loop(0, 8, cast, 0)
-    dqs = RingReduce(
-        lambda rel, half: dqsend.at[2 * ((y + rel) % 4) + half],
-        lambda half: dqpass.at[half],
-        lambda side, half: dqgot.at[side, half],
-        yp, ym, sems, 8,
-    )
-    dqs.start()
     kvs.finish()
     zrows = BLK // 4
     for n in range(4):
@@ -805,8 +1034,27 @@
     )
     zg = RingGather(lambda index, half: dkv_ref.at[index, half], z, zp, zm, sems, 10)
     zs.start()
+
+    def cast(i, carry):
+        dqsend[i] = jnp.transpose(dqacc[i]).astype(LOW)
+        return carry
+
+    lax.fori_loop(0, 8, cast, 0)
+    dqs = RingReduce(
+        lambda rel, half: dqsend.at[2 * ((y + rel) % 4) + half],
+        lambda half: dqpass.at[half],
+        lambda side, half: dqgot.at[side, half],
+        yp, ym, sems, 8,
+    )
+    dqs.start()
+    zs.relay()
     dqs.relay()
-    zs.relay()
+    zs.finish()
+    for half in range(2):
+        dkv_ref[z, half] = (zpart[z, half].astype(FULL) + zs.arrived(half)).astype(LOW)
+        zg.own(half)
+    for load in loads[3:]:
+        load.wait()
     dqs.finish()
     back = remote(dqback, dqhigh, sw_s.at[2], sw_r.at[2], partner)
     dqback[...] = (dqsend[2 * y + 1].astype(FULL) + dqs.arrived(1)).astype(LOW)
@@ -816,7 +1064,17 @@
         lambda index, half: draw_ref.at[pl.ds(half * HALF, HALF), pl.ds(pl.multiple_of(index * HD, HD), HD)],
         z, zp, zm, sems, 11,
     )
-    gain = gain_ref[...]
+
+    def unrotated(grad, raw, gain, rows):
+        cosine, sine = cos_ref[rows, :], sin_ref[rows, :]
+        first, second = grad[:, : HD // 2], grad[:, HD // 2 :]
+        turned = jnp.concatenate([first * cosine + second * sine, second * cosine - first * sine], axis=1)
+        inverse = lax.rsqrt(jnp.mean(raw * raw, axis=1, keepdims=True) + EPS)
+        unit = raw * inverse
+        scaled = gain * turned
+        raw_grad = inverse * (scaled - unit * jnp.mean(unit * scaled, axis=1, keepdims=True))
+        return raw_grad.astype(LOW), jnp.sum(unit * turned, axis=0, keepdims=True)
+
     gain_grad = None
     for half in range(2):
         if half == 0:
@@ -824,39 +1082,122 @@
         else:
             back.wait_recv()
             grad = dqhigh[...].astype(FULL)
-        grad = grad * (HD**-0.5)
         rows = pl.ds(half * HALF, HALF)
-        cosine, sine = cos_ref[rows, :], sin_ref[rows, :]
-        first, second = grad[:, : HD // 2], grad[:, HD // 2 :]
-        turned = jnp.concatenate([first * cosine + second * sine, second * cosine - first * sine], axis=1)
-        raw = raw_ref[rows, :]
-        inverse = lax.rsqrt(jnp.mean(raw * raw, axis=1, keepdims=True) + EPS)
-        unit = raw * inverse
-        scaled = gain * turned
-        raw_grad = inverse * (scaled - unit * jnp.mean(unit * scaled, axis=1, keepdims=True))
-        draw_ref[rows, pl.ds(pl.multiple_of(z * HD, HD), HD)] = raw_grad.astype(LOW)
+        raw_grad, piece = unrotated(grad * (HD**-0.5), raw_ref[rows, :], qgain_ref[...], rows)
+        draw_ref[rows, pl.ds(pl.multiple_of(z * HD, HD), HD)] = raw_grad
         draws.own(half)
-        part = jnp.sum(unit * turned, axis=0, keepdims=True)
-        gain_grad = part if gain_grad is None else gain_grad + part
+        gain_grad = piece if gain_grad is None else gain_grad + piece
     gaing[z] = jnp.broadcast_to(gain_grad, (8, HD))
     for n, peer in enumerate((zp, zm, z2)):
         go(remote(gaing.at[z], gaing.at[z], gn_s.at[n], gn_r.at[z], peer))
 
-    zs.finish()
-    for half in range(2):
-        dkv_ref[z, half] = (zpart[z, half].astype(FULL) + zs.arrived(half)).astype(LOW)
-        zg.own(half)
-    pieces_far()
+    chunk_rows = normed_t.shape[0] // 8
+
+    def weight_grad(m, rhs):
+        def block(r, carry):
+            lhs = normed_t[pl.ds(pl.multiple_of(r * chunk_rows, 16), chunk_rows), :]
+            tile = jnp.dot(lhs, rhs[...], preferred_element_type=FULL).astype(LOW)
+            part[pl.ds(pl.multiple_of((8 * m + r) * chunk_rows, 16), chunk_rows), :] = tile
+            return carry
+
+        lax.fori_loop(0, 8, block, 0)
+
+    zg.forward()
+    weight_grad(0, draw_ref.at[:, pl.ds(pl.multiple_of(z * HD, HD), HD)])
     draws.forward()
-    zg.forward()
-    draws.near()
     zg.near()
-    draws.far()
     zg.far()
+    key_gain_grad = None
+    for n in range(4):
+        rows = pl.ds(n * zrows, zrows)
+        raw_grad, piece = unrotated(dkv_ref[n, 0].astype(FULL), kraw_ref[rows, :], kgain_ref[...], rows)
+        dkraw[rows, :] = raw_grad
+        dvrow[rows, :] = dkv_ref[n, 1]
+        key_gain_grad = piece if key_gain_grad is None else key_gain_grad + piece
     for rel in (1, 3, 2):
         other = (z + rel) % 4
         remote(gaing.at[z], gaing.at[other], gn_s.at[0], gn_r.at[other], sibling).wait_recv()
-    dgain_ref[...] = sum(gaing[n] for n in range(4))
+    query_gain_grad = sum(gaing[n, 0:1, :] for n in range(4))
+    number = lax.broadcasted_iota(jnp.int32, (16, HD), 0)
+    both = jnp.where(number == 0, query_gain_grad, jnp.where(number == 1, key_gain_grad, 0.0))
+    part[pl.ds(24 * chunk_rows, 16), :] = both.astype(LOW)
+    part[pl.ds(24 * chunk_rows + 16, LATE), :] = jnp.zeros((LATE, HD), LOW)
+    weight_grad(1, dkraw)
+    weight_grad(2, dvrow)
+
+    side = 16 * LATE
+
+    def late_piece(ref, core, owner):
+        return rows_at(ref, side * core + LATE * owner, LATE)
+
+    cross = remote(rows_at(part, side * (1 - c), side), core_recv, c_s.at[0], c_r.at[0], sibling)
+    go(cross)
+    cross.wait_recv()
+
+    def add(r, carry):
+        both = part[pl.ds(pl.multiple_of(side * c + 2 * LATE * r, 16), 2 * LATE), :].astype(FULL)
+        rows = pl.ds(pl.multiple_of(2 * LATE * r, 16), 2 * LATE)
+        half_sum[rows, :] = (both + core_recv[rows, :].astype(FULL)).astype(LOW)
+        return carry
+
+    lax.fori_loop(0, 8, add, 0)
+    for n, (a, b) in enumerate(shifts):
+        target = ((x + a) % 4) * 4 + (y + b) % 4
+        go(remote(late_piece(half_sum, 0, target), plane_recv.at[chip], p_s.at[n], p_r.at[chip], plane[n]))
+
+    pieces[0].forward()
+    pieces_far(1)
+    draws.near()
+    draws.far()
+    gain_row = None
+    for half in range(2):
+        rows = pl.ds(half * HALF, HALF)
+        grad = lax.dot_general(draw_ref[rows, :], wq_ref[...], NT, preferred_element_type=FULL)
+        grad = grad + lax.dot_general(dkraw[rows, :], wk_ref[...], NT, preferred_element_type=FULL)
+        grad = grad + lax.dot_general(dvrow[rows, :], wv_ref[...], NT, preferred_element_type=FULL)
+        value = tok_ref[rows, :].astype(FULL)
+        inverse = lax.rsqrt(jnp.mean(value * value, axis=1, keepdims=True) + EPS)
+        unit = value * inverse
+        scaled = igain_ref[...] * grad
+        back_grad = inverse * (scaled - unit * jnp.mean(unit * scaled, axis=1, keepdims=True))
+        tgrad_ref[rows, :] = resid_ref[rows, :] + back_grad
+        piece = jnp.sum(unit * grad, axis=0, keepdims=True)
+        gain_row = piece if gain_row is None else gain_row + piece
+    grow[0] = jnp.broadcast_to(gain_row, grow.shape[1:])
+    to_core = remote(grow.at[0], grow.at[1], i_s.at[15], i_r.at[16], sibling)
+    go(to_core)
+
+    total = late_piece(half_sum, 0, chip)[...].astype(FULL)
+    for a, b in shifts:
+        source = ((x + a) % 4) * 4 + (y + b) % 4
+        remote(late_piece(half_sum, 0, 0), plane_recv.at[source], p_s.at[0], p_r.at[source], sibling).wait_recv()
+        total = total + plane_recv[source].astype(FULL)
+
+    def piece_of(owner):
+        return late_piece(late_ref, c, owner)
+
+    piece_of(chip)[...] = total.astype(LOW)
+    for n in range(15):
+        go(remote(piece_of(chip), piece_of(chip), g_s.at[n], g_r.at[chip], plane[n]))
+    go(remote(piece_of(chip), piece_of(chip), f_s.at[chip], f_r.at[chip], sibling))
+    to_core.wait_recv()
+    grecv[chip] = grow[0] + grow[1]
+    for n in range(15):
+        go(remote(grecv.at[chip], grecv.at[chip], i_s.at[n], i_r.at[chip], plane[n]))
+    pieces_near(0)
+    pieces_far(0)
+    for a, b in shifts:
+        source = ((x + a) % 4) * 4 + (y + b) % 4
+        remote(late_piece(half_sum, 0, 0), piece_of(source), g_s.at[0], g_r.at[source], sibling).wait_recv()
+        go(remote(piece_of(source), piece_of(source), f_s.at[source], f_r.at[source], sibling))
+    for a, b in shifts:
+        source = ((x + a) % 4) * 4 + (y + b) % 4
+        remote(grecv.at[chip], grecv.at[source], i_s.at[0], i_r.at[source], sibling).wait_recv()
+    dgain_ref[...] = sum(grecv[n] for n in range(16))
+    for n in range(16):
+        theirs = late_piece(late_ref, 1 - c, n)
+        remote(late_piece(half_sum, 0, 0), theirs, f_s.at[0], f_r.at[n], sibling).wait_recv()
+    early_done()
     for h in range(2):
         for half in range(2):
             keep(h, half).wait()
@@ -868,21 +1209,21 @@
         copy.wait_send()
 
 
-def backward_attention(
-    doc_starts, out_grad, stats, q_all, k_all, v_all, piece_a, piece_b, query_raw, cosine, sine, query_gain
-):
-    width = piece_a.shape[1]
+def backward_attention(doc_starts, *operands):
+    width = operands[2].shape[1]
+    streamed = operands[8:]
     return pl.pallas_call(
         attn_backward,
         name="attn_backward",
         out_shape=[
-            shape(LOW, BLK, 4 * HD),
-            shape(FULL, 8, HD),
-            shape(LOW, 4, 2, BLK // 4, HD),
+            shape(LOW, 32 * LATE, HD),
+            shape(LOW, 2 * EARLY, width),
+            shape(FULL, BLK, width),
+            shape(FULL, 8, width),
             shape(LOW, 2 * ROWS + 64, width),
         ],
-        in_specs=[SMEM] + [VMEM] * 11,
-        out_specs=[VMEM] * 3 + [ANY],
+        in_specs=[SMEM] + [VMEM] * 8 + [ANY] * 13,
+        out_specs=[VMEM] * 4 + [ANY],
         scratch_shapes=[
             vmem(LOW, 8, HALF, HD),
             vmem(FULL, 8, 8, HALF),
@@ -908,132 +1249,28 @@
             vmem(LOW, 2, 2, WINDOW, width),
             vmem(LOW, PIECE, width),
             vmem(LOW, PIECE, width),
+            vmem(LOW, BLK, 4 * HD),
+            vmem(LOW, 4, 2, BLK // 4, HD),
+            vmem(LOW, BLK, HD),
+            vmem(LOW, BLK, HD),
+            vmem(LOW, 32 * LATE, HD),
+            vmem(LOW, 16 * LATE, HD),
+            vmem(LOW, 16 * LATE, HD),
+            vmem(LOW, 16, LATE, HD),
+            vmem(FULL, 2, 8, width),
+            vmem(FULL, 16, 8, width),
+            vmem(LOW, EARLY, width),
+            vmem(LOW, EARLY, width),
+            vmem(LOW, 16, 16, width),
+            *[vmem(operand.dtype, *operand.shape) for operand in streamed],
             dma(12, 6), dma(12, 6), dma(2, 3), dma(8), dma(3), dma(3), dma(4), dma(4), dma(3), dma(4),
             dma(2, 4, 2), dma(2, 4, 2), dma(2, 2),
+            dma(13), dma(2), dma(2), dma(15), dma(16), dma(15), dma(16), dma(16), dma(16), dma(16), dma(17),
+            dma(KEEPERS), dma(16), dma(15), dma(16), dma(KEEPERS), dma(KEEPERS),
         ],
-        compiler_params=params(2, 48),
+        compiler_params=params(2, 58),
         cost_estimate=cost(15),
-    )(doc_starts, out_grad, stats, q_all, k_all, v_all, piece_a, piece_b, query_raw, cosine, sine, query_gain)
-
-
-def head_sum_kernel(part_ref, out_ref, passing, got, rs, rr):
-    x, y, c, z = place()
-    zp, zm = at(x, y, c, z + 1), at(x, y, c, z + 3)
-    greet([zp, zm])
-    rows = part_ref.shape[0] // 4
-    zs = RingReduce(
-        lambda rel, half: rows_at(part_ref, ((z + rel) % 4) * rows + half * (rows // 2), rows // 2),
-        lambda half: passing.at[half],
-        lambda side, half: got.at[side, half],
-        zp, zm, (rs, rr), 0,
-    )
-    zg = RingGather(
-        lambda index, half: rows_at(out_ref, index * rows + half * (rows // 2), rows // 2),
-        z, zp, zm, (rs, rr), 1,
-    )
-    zs.start()
-    zs.relay()
-    zs.finish()
-    for half in range(2):
-        own = pl.ds(pl.multiple_of(z * rows + half * (rows // 2), 16), rows // 2)
-        out_ref[own, :] = (part_ref[own, :].astype(FULL) + zs.arrived(half)).astype(LOW)
-        zg.own(half)
-    zg.forward()
-    zg.near()
-    zg.far()
-    zs.drain()
-    zg.drain()
-
-
-def head_sum(part):
-    rows, columns = part.shape
-    return pl.pallas_call(
-        head_sum_kernel,
-        name="head_sum",
-        out_shape=shape(LOW, rows, columns),
-        in_specs=[VMEM],
-        out_specs=VMEM,
-        scratch_shapes=[vmem(LOW, 2, rows // 8, columns), vmem(LOW, 2, 2, rows // 8, columns), dma(2, 6), dma(2, 6)],
-        compiler_params=params(3, 32),
-        cost_estimate=cost(1),
-    )(part)
-
-
-def late_sum_kernel(part_ref, out_ref, core_recv, half, plane_recv, c_ssem, c_rsem, p_ssem, p_rsem, g_ssem, g_rsem, f_ssem, f_rsem):
-    x, y, c, z = place()
-    sibling = at(x, y, 1 - c, z)
-    shifts = [(a, b) for a in range(4) for b in range(4) if (a, b) != (0, 0)]
-    peers = [at(x + a, y + b, c, z) for a, b in shifts]
-    greet(peers + [sibling])
-    first = pl.multiple_of(2 * c, 2)
-    copies = []
-
-    def core_copy(m):
-        return remote(part_ref.at[2 * (1 - c) + m], core_recv.at[m], c_ssem.at[m], c_rsem.at[m], sibling)
-
-    for m in range(2):
-        copies.append(core_copy(m))
-        copies[-1].start()
-    for m in range(2):
-        core_copy(m).wait_recv()
-
-        def add(r, carry):
-            both = part_ref[first + m, r].astype(jnp.float32) + core_recv[m, r].astype(jnp.float32)
-            half[m * 8 + r] = both.astype(jnp.bfloat16)
-            return carry
-
-        lax.fori_loop(0, 8, add, 0)
-    me = x * 4 + y
-    for n, (a, b) in enumerate(shifts):
-        target = ((x + a) % 4) * 4 + (y + b) % 4
-        copies.append(remote(half.at[target], plane_recv.at[me], p_ssem.at[n], p_rsem.at[me], peers[n]))
-        copies[-1].start()
-    total = half[me].astype(jnp.float32)
-    for n, (a, b) in enumerate(shifts):
-        source = ((x + a) % 4) * 4 + (y + b) % 4
-        remote(half.at[0], plane_recv.at[source], p_ssem.at[0], p_rsem.at[source], sibling).wait_recv()
-        total = total + plane_recv[source].astype(jnp.float32)
-
-    def piece(owner):
-        return out_ref.at[first + owner // 8, owner % 8]
-
-    out_ref[first + me // 8, me % 8] = total.astype(jnp.bfloat16)
-    for n in range(15):
-        copies.append(remote(piece(me), piece(me), g_ssem.at[n], g_rsem.at[me], peers[n]))
-        copies[-1].start()
-    copies.append(remote(piece(me), piece(me), f_ssem.at[me], f_rsem.at[me], sibling))
-    copies[-1].start()
-    for a, b in shifts:
-        source = ((x + a) % 4) * 4 + (y + b) % 4
-        remote(half.at[0], piece(source), g_ssem.at[0], g_rsem.at[source], sibling).wait_recv()
-        copies.append(remote(piece(source), piece(source), f_ssem.at[source], f_rsem.at[source], sibling))
-        copies[-1].start()
-    for n in range(16):
-        theirs = out_ref.at[2 * (1 - c) + n // 8, n % 8]
-        remote(half.at[0], theirs, f_ssem.at[0], f_rsem.at[n], sibling).wait_recv()
-    for copy in copies:
-        copy.wait_send()
-
-
-def late_sum(part):
-    _, _, rows, columns = part.shape
-    return pl.pallas_call(
-        late_sum_kernel,
-        name="late_sum",
-        out_shape=shape(LOW, *part.shape),
-        in_specs=[VMEM],
-        out_specs=VMEM,
-        scratch_shapes=[
-            vmem(LOW, 2, 8, rows, columns),
-            vmem(LOW, 16, rows, columns),
-            vmem(LOW, 16, rows, columns),
-            dma(2), dma(2), dma(15), dma(16), dma(15), dma(16), dma(16), dma(16),
-        ],
-        compiler_params=pltpu.CompilerParams(
-            collective_id=9, has_side_effects=True, vmem_limit_bytes=40 << 20
-        ),
-        cost_estimate=pl.CostEstimate(flops=10**8, bytes_accessed=10 * 2**20, transcendentals=0),
-    )(part)
+    )(doc_starts, *operands)
 
 
 def per_device(
@@ -1063,7 +1300,7 @@
     inputs = tokens.astype(jnp.float32)
     query_weight_all = lax.all_gather(query_weight, "head", axis=1, tiled=True)
     out_weight_all = lax.all_gather(out_weight, "head", axis=0, tiled=True)
-    normed, input_back = jax.vjp(rms_norm, inputs, input_gain)
+    normed = rms_norm(inputs, input_gain)
     normed_low = normed.astype(jnp.bfloat16)
     query_raw = jnp.dot(normed_low, query_weight, preferred_element_type=jnp.float32)
     key_raw = jnp.dot(normed_low, key_weight, preferred_element_type=jnp.float32)
@@ -1079,118 +1316,59 @@
 
     query_rows = query_piece(query_raw, query_gain)
     query_low = query_rows.astype(jnp.bfloat16)
-    key_rows, key_back = jax.vjp(key_piece, key_raw, key_gain)
+    key_rows = key_piece(key_raw, key_gain)
     key_low = key_rows.astype(jnp.bfloat16)
     mix_all, lse_rows, q_all, k_all, v_all = forward_attention(
         doc_starts, query_low, key_low, value_low
     )
-    lse_row = lse_rows[:, 0].reshape(-1)
-    attn_mix = lax.dynamic_slice_in_dim(mix_all, lax.axis_index("head") * HD, HD, 1)
-    attn_out = jnp.dot(mix_all, out_weight_all, preferred_element_type=jnp.float32)
-    hidden_state, attn_back = jax.vjp(residual_norm, inputs, attn_out, attn_gain)
-    ffn_in, prenorm_back = jax.vjp(rms_norm, hidden_state, prenorm_gain)
-    ffn_low = ffn_in.astype(jnp.bfloat16)
-    gate_rows = jnp.dot(ffn_low, gate_weight, preferred_element_type=jnp.float32)
-    up_rows = jnp.dot(ffn_low, up_weight, preferred_element_type=jnp.float32)
-    act_rows, act_back = jax.vjp(gated_act, gate_rows, up_rows)
-    act_low = act_rows.astype(jnp.bfloat16)
-    ffn_out = head_sum(
-        jnp.dot(act_low, down_weight, preferred_element_type=jnp.float32).astype(jnp.bfloat16)
-    ).astype(jnp.float32)
-    mixed, post_back = jax.vjp(residual_norm, hidden_state, ffn_out, post_gain)
-    upstream = cotangent.astype(jnp.float32)
-    hidden_grad, ffn_out_grad, post_gain_grad = post_back(upstream)
-    ffn_out_low = ffn_out_grad.astype(jnp.bfloat16)
-    act_grad = dot_last(ffn_out_low, down_weight)
-    gate_grad, up_grad = act_back(act_grad)
-    gate_low = gate_grad.astype(jnp.bfloat16)
-    up_low = up_grad.astype(jnp.bfloat16)
-    ffn_in_sum, piece_a, piece_b, rest = ffn_grads(
-        (dot_last(gate_low, gate_weight) + dot_last(up_low, up_weight)).astype(jnp.bfloat16),
-        ffn_low,
-        ffn_out_low,
-        jnp.transpose(gate_low),
-        jnp.transpose(up_low),
-        jnp.transpose(act_low),
-    )
-    ffn_in_grad = ffn_in_sum.astype(jnp.float32)
-    hidden_more, prenorm_gain_grad = prenorm_back(ffn_in_grad)
-    hidden_grad = hidden_grad + hidden_more
-    input_grad, attn_out_grad, attn_gain_grad = attn_back(hidden_grad)
-    attn_out_low = attn_out_grad.astype(jnp.bfloat16)
-    out_weight_grad_t = dot_first(attn_out_low, attn_mix)
-    mix_grad = dot_last(attn_out_low, out_weight).astype(jnp.bfloat16)
-    delta = jnp.sum(mix_grad.astype(jnp.float32) * attn_mix.astype(jnp.float32), axis=1)
-    stats = jnp.stack([lse_row, delta] + [jnp.zeros_like(delta)] * 6)
-    stats = jnp.transpose(stats.reshape(8, 2, HALF), (1, 0, 2))
-    query_raw_all, query_gain_rows, key_value_grad, big = backward_attention(
+    width = tokens.shape[1]
+    mixed, mix_grad, stats, resid, early, piece_a, piece_b = middle(
+        attn_gain.reshape(1, width),
+        prenorm_gain.reshape(1, width),
+        post_gain.reshape(1, width),
+        lse_rows,
+        mix_all,
+        out_weight_all,
+        tokens,
+        cotangent,
+        jnp.transpose(gate_weight),
+        jnp.transpose(up_weight),
+        down_weight,
+    )
+    late, early, tokens_grad, input_gain_rows, big = backward_attention(
         doc_starts,
         mix_grad,
         stats,
+        piece_a,
+        piece_b,
+        query_gain.reshape(1, HD),
+        key_gain.reshape(1, HD),
+        input_gain.reshape(1, width),
+        early,
         q_all,
         k_all,
         v_all,
-        piece_a,
-        piece_b,
         query_raw,
+        key_raw,
         cos_table[:, : HD // 2],
         sine_table[:, : HD // 2],
-        query_gain.reshape(1, HD),
-    )
-    query_gain_part = query_gain_rows[0]
-    key_grad = key_value_grad[:, 0].reshape(row_count, HD).astype(jnp.float32)
-    value_grad_low = key_value_grad[:, 1].reshape(row_count, HD)
-    query_raw_low = lax.dynamic_slice_in_dim(query_raw_all, lax.axis_index("head") * HD, HD, 1)
-    query_weight_grad = dot_first(normed_low, query_raw_low)
-    key_raw_grad, key_gain_grad = key_back(key_grad)
-    key_raw_low = key_raw_grad.astype(jnp.bfloat16)
-    key_weight_grad = dot_first(normed_low, key_raw_low)
-    value_weight_grad = dot_first(normed_low, value_grad_low)
-    normed_grad = (
-        dot_last(query_raw_all, query_weight_all)
-        + dot_last(key_raw_low, key_weight)
-        + dot_last(value_grad_low, value_weight)
-    )
-    input_more, input_gain_grad = input_back(normed_grad)
-    tokens_grad = input_grad + input_more
-    width = tokens.shape[1]
-    rest_rows = rest.size // HD
-    gains = jnp.concatenate(
-        [
-            input_gain_grad,
-            attn_gain_grad,
-            prenorm_gain_grad,
-            post_gain_grad,
-            query_gain_part,
-            key_gain_grad,
-        ]
-    ).astype(jnp.bfloat16)
-    gain_rows = gains.size // HD
-    extra = jnp.concatenate(
-        [
-            gains.reshape(gain_rows, HD),
-            rest.reshape(rest_rows, HD),
-            jnp.zeros((4 * 128 - gain_rows - rest_rows, HD), jnp.bfloat16),
-        ]
-    ).reshape(4, 128, HD)
-    late = jnp.stack(
-        [query_weight_grad, key_weight_grad, value_weight_grad, out_weight_grad_t]
-    ).astype(jnp.bfloat16)
-    late = jnp.concatenate([late, extra], axis=1).reshape(4, 8, (width + 128) // 8, HD)
-    late = late_sum(late).reshape(4, width + 128, HD)
-    query_weight_grad = late[0, :width].astype(jnp.float32)
-    key_weight_grad = late[1, :width].astype(jnp.float32)
-    value_weight_grad = late[2, :width].astype(jnp.float32)
-    out_weight_grad = jnp.transpose(late[3, :width].astype(jnp.float32))
-    extra = late[:, width:].reshape(4 * 128, HD)
-    gains = extra[:gain_rows].reshape(-1).astype(jnp.float32)
-    rest = extra[gain_rows : gain_rows + rest_rows].reshape(rest.shape)
-    input_gain_grad = gains[:width]
-    attn_gain_grad = gains[width : 2 * width]
-    prenorm_gain_grad = gains[2 * width : 3 * width]
-    post_gain_grad = gains[3 * width : 4 * width]
-    query_gain_grad = gains[4 * width : 4 * width + HD]
-    key_gain_grad = gains[4 * width + HD : 4 * width + 2 * HD]
+        key_weight,
+        value_weight,
+        jnp.transpose(normed_low),
+        query_weight_all,
+        tokens,
+        resid,
+    )
+    input_gain_grad = input_gain_rows[0]
+    query_weight_grad = late[:width].astype(jnp.float32)
+    key_weight_grad = late[width : 2 * width].astype(jnp.float32)
+    value_weight_grad = late[2 * width : 3 * width].astype(jnp.float32)
+    query_gain_grad = late[3 * width].astype(jnp.float32)
+    key_gain_grad = late[3 * width + 1].astype(jnp.float32)
+    out_weight_grad = early[:HD].astype(jnp.float32)
+    rest = early[HD : HD + 64]
+    gains = early[HD + 64 : HD + 67].astype(jnp.float32)
+    attn_gain_grad, prenorm_gain_grad, post_gain_grad = gains[0], gains[1], gains[2]
     hidden = gate_weight.shape[1]
     gate_weight_grad = jnp.transpose(big[:hidden].astype(jnp.float32))
     up_weight_grad = jnp.transpose(big[hidden : 2 * hidden].astype(jnp.float32))
@@ -1199,7 +1377,7 @@
         down_weight_grad, rest.astype(jnp.float32), (hidden - rest.shape[0], 0)
     )
     return (
-        mixed.astype(jnp.bfloat16),
+        mixed,
         tokens_grad,
         query_weight_grad,
         key_weight_grad,

time: 426 us -> 396 us (0.930)
  matrix products: 43.6 us -> 3.6 us
  Pallas kernels: 298 us -> 325 us
  other arithmetic: 43.1 us -> 25.3 us
    pallas_call x1, Pallas kernels: 107 us -> 156 us  [backward_attention(): pl.pallas_call(attn_backward, name='attn_backward', out_shape=[shape(LOW,...]
    dot_general x15 -> x0, matrix products: 39.7 us -> none  [the longest x7 22.7 us: dot_last(): lax.dot_general(left_side, right_side, (((1,), (1,)), ((), ())), preferre...]
    pallas_call x3 -> x1, Pallas kernels: 119 us -> 97.9 us  [middle(): pl.pallas_call(middle_kernel, name='middle', out_shape=[shape(LOW, rows,...]
    reduce_sum x4 -> x0, other arithmetic: 8.38 us -> none  [rms_norm(): values * lax.rsqrt(jnp.mean(values * values, axis=-1, keepdims=True) + EPS)]
    unnamed x92 -> x35, local copies, waits for them, and re-layouts: 12.8 us -> 9.21 us
  transfers between devices with their start and end apart: 2 -> 2, of which waited for: 0 -> 0; matrix products, arithmetic and copies ran while one was open for 14% -> 5% of each run, Pallas kernels for 59% -> 44%
where the time goes in v3:
time: 396 us; the launch traced here: 388 us
  Pallas kernels  325 us (82%)
  other arithmetic  25.3 us (6%)
  local copies, waits for them, and re-layouts  18.2 us (5%)
  between operations  14.7 us (4%)
    pallas_call x1, Pallas kernels, backward_attention(): pl.pallas_call(attn_backward, name='attn_backward', out_shape=[shape(LOW,...  156 us
    pallas_call x1, Pallas kernels, middle(): pl.pallas_call(middle_kernel, name='middle', out_shape=[shape(LOW, rows,...  97.9 us
    pallas_call x1, Pallas kernels, forward_attention(): pl.pallas_call(attn_forward, name='attn_forward', out_shape=[shape(LOW, B...  71 us
    convert_element_type x1, other arithmetic, per_device(): down_weight_grad = big[2 * hidden:].astype(jnp.float32)  9.38 us
    unnamed x35, local copies, waits for them, and re-layouts  9.21 us
  transfers between devices with their start and end apart: 2, of which 0 were waited for; matrix products, arithmetic and copies ran while one was open for 5% of the time, Pallas kernels for 44%

profile of v3, /device:TPU:1, one launch (start us, length us, event | category | flops | bytes accessed | tf_op | source)
XLA Modules:
  0.0 388.2 jit_solution(560669123796538421)
XLA Ops:
  7.2 0.0 all-gather.3.cloned.1.call-start
  7.2 0.7 all-gather.3.cloned.1.call-update
  7.9 0.0 all-gather.5.cloned.1.call-start
  8.0 0.7 all-gather.5.cloned.1.call-update
  8.7 0.5 multiply_exponential_fusion
  9.2 1.6 copy.36
  10.8 0.3 fusion
  11.1 0.6 broadcast_in_dim.30.igain_ref
  11.7 0.8 multiply_reduce_fusion.1
  12.5 0.2 copy.37.raw_hbm
  12.7 0.0 copy-start.8
  12.7 0.0 copy-start.13
  12.7 2.0 multiply_reduce_fusion
  14.7 0.2 copy.38.kraw_hbm
  14.9 0.0 copy-start.9
  15.0 0.2 multiply_multiply_fusion
  15.3 0.7 slice_negate_fusion.1
  16.0 0.1 select_reduce_fusion
  16.1 1.3 reshape.89.again_ref
  17.4 1.3 reshape.90.pgain_ref
  18.7 1.3 reshape.91.fgain_ref
  20.0 0.8 broadcast_multiply_fusion
  20.8 3.3 fusion.3
  24.1 0.7 slice.88.cos_hbm
  24.8 0.7 slice.89.sin_hbm
  25.5 0.8 convolution_convert_fusion.v_ref
  26.4 1.4 fusion.10.normed_hbm
  27.7 71.0 %attn_forward.1 = (bf16[512,1024]{1,0:T(8,128)(2,1)S(1)}, f32[2,8,256]{2,1,0:T(8,128)S(1)}, bf16[8,256,256]{2,1,0:T(8,128)(2,1)S(1)}, bf16[8,512,256]{2,1,0:T(8,128)(2,1)S(1)}, bf16[8,512,256]{2,1,0:T(8,128)(2,1)S(1)}) custom-call(s32[7]{0:T(128)S(1)} %copy-done, bf16[512,256]{1,0:T(8,128)(2,1)S(1)} %get-tuple-element.65.q_ref, ...), custom_call_target="tpu_custom_call" | custom-call | flops 6000000000 | bytes 20971520 | tf_op jit(solution)/shard_map/attn_forward/pallas_call | solution.py:371
  98.7 0.0 copy-start.1
  98.7 1.3 copy-done.1
  100.0 1.3 copy-done.2
  101.4 1.0 copy-done.3
  102.3 1.0 copy-done.4
  103.3 0.6 copy-done.5
  103.9 97.9 %middle.1 = (bf16[512,1152]{1,0:T(8,128)(2,1)}, bf16[512,256]{1,0:T(8,128)(2,1)}, f32[2,8,256]{2,1,0:T(8,128)}, f32[512,1152]{1,0:T(8,128)}, bf16[352,1152]{1,0:...) custom-call(f32[1,1152]{1,0:T(1,128)} %reshape.89.again_ref, f32[1,1152]{1,0:T(1,128)} %reshape.90.pgain_ref, ...), custom_call_target="tpu_custom_call" | custom-call | flops 20000000000 | bytes 20971520 | tf_op jit(solution)/shard_map/middle/pallas_call | solution.py:665
  201.8 0.0 all-gather.5.cloned.1.call-done.wq_hbm
  201.8 156.0 %attn_backward.1 = (bf16[3584,256]{1,0:T(8,128)(2,1)}, bf16[352,1152]{1,0:T(8,128)(2,1)}, f32[512,1152]{1,0:T(8,128)}, f32[8,1152]{1,0:T(8,128)}, bf16[5184,1152]{1,0:T(8,128)(2,1)}) custom-call(s32[7]{0:T(128)} %starts_ref.3, bf16[512,256]{1,0:T(8,128)(2,1)} %get-tuple-element.35.do_ref, f32[2,8,256]{2,1,0:T(8,128)} %get-tuple-element.36.stat_ref, ...), custom_call_target="tpu_custom_call" | custom-call | flops 15000000512 | bytes 20971520 | tf_op jit(solution)/shard_map/attn_backward/pallas_call | solution.py:1215
  357.9 2.2 slice_convert_fusion.1
  360.0 0.7 slice_convert_fusion.5
  360.8 3.3 slice_convert_fusion.2
  364.1 1.3 slice_convert_fusion.6
  365.4 9.4 %slice_convert_fusion = (f32[1728,1152]{1,0:T(8,128)S(1)}, f32[1152,1728]{0,1:T(8,128)}, f32[1152,1728]{0,1:T(8,128)}) fusion(bf16[5184,1152]{1,0:T(8,128)(2,1)} %get-tuple-element.47), kind=kLoop, calls=%fused_computation.2 | loop fusion | flops 5971968 | bytes 35831808 | tf_op jit(solution)/shard_map/convert_element_type | solution.py:1375
  374.8 1.1 convert_dynamic-update-slice_fusion
  375.8 0.0 copy-start.6
  375.9 0.7 slice_reduce_fusion
  376.6 1.9 slice_reduce_fusion.3
  378.5 1.0 copy.44
  379.5 1.4 copy.45
  (29 shorter events, 0.1 us)
Async XLA Ops:
  7.2 4.5 %copy-start.11 = (bf16[1152,256]{1,0:T(8,128)(2,1)S(1)}, bf16[1152,256]{1,0:T(8,128)(2,1)}, u32[]{:S(2)}) copy-start(bf16[1152,256]{1,0:T(8,128)(2,1)} %param.19) | copy-start | bytes 1769476
  7.2 3.9 %copy-start.12 = (f32[1152]{0:T(1024)S(1)}, f32[1152]{0:T(1024)}, u32[]{:S(2)}) copy-start(f32[1152]{0:T(1024)} %param.26) | copy-start | bytes 13828
  7.2 96.7 %all-gather.3.cloned.1.call-start = ((), (), s32[]{:S(2)}) async-start(), calls=%async_computation | async-start | bytes 2949120 | tf_op jit(solution)/shard_map/all_gather | solution.py:1302
  7.9 193.9 %all-gather.5.cloned.1.call-start = ((), (), s32[]{:S(2)}) async-start(), calls=%async_computation.1 | async-start | bytes 2949120 | tf_op jit(solution)/shard_map/all_gather | solution.py:1301
  12.7 2.5 copy-start.8
  12.7 2.3 copy-start.13
  12.7 2.3 copy-start.14
  14.9 9.2 %copy-start.9 = (f32[512,256]{1,0:T(8,128)}, f32[512,256]{1,0:T(8,128)S(1)}, u32[]{:S(2)}) copy-start(f32[512,256]{1,0:T(8,128)S(1)} %copy.38.kraw_hbm) | copy-start | bytes 1572868
  14.9 1.1 copy-start
  20.8 4.8 %copy-start.15 = (bf16[1152,256]{1,0:T(8,128)(2,1)S(1)}, bf16[1152,256]{1,0:T(8,128)(2,1)}, u32[]{:S(2)}) copy-start(bf16[1152,256]{1,0:T(8,128)(2,1)} %wv_hbm.1) | copy-start | bytes 1769476
  98.7 1.3 copy-start.1
  100.0 1.3 copy-start.2
  101.4 1.0 copy-start.3
  102.3 1.0 copy-start.4
  103.3 0.6 copy-start.5
  365.4 13.1 %copy-start.10 = (bf16[512,1152]{1,0:T(8,128)(2,1)S(1)}, bf16[512,1152]{1,0:T(8,128)(2,1)}, u32[]{:S(2)}) copy-start(bf16[512,1152]{1,0:T(8,128)(2,1)} %get-tuple-element.89) | copy-start | bytes 3538948
  374.8 4.8 %copy-start.7 = (f32[512,1152]{1,0:T(8,128)S(1)}, f32[512,1152]{1,0:T(8,128)}, u32[]{:S(2)}) copy-start(f32[512,1152]{1,0:T(8,128)} %get-tuple-element.90) | copy-start | bytes 7077892
  375.8 5.1 %copy-start.6 = (f32[1728,1152]{1,0:T(8,128)}, f32[1728,1152]{1,0:T(8,128)S(1)}, u32[]{:S(2)}) copy-start(f32[1728,1152]{1,0:T(8,128)S(1)} %convert_dynamic-update-slice_fusion) | copy-start | bytes 23887876
Sparse Core Ops, SparseCore 0:
  9.7 36.4 all-gather.2
  47.8 38.4 all-gather.4
